TPU v7x, 256 devices: a whole 4x4x8 slice. The times are simulated.
256 devices in a mesh: tm: 8 (over z_hi, core), gz: 32 (over z_lo, x, y).
Axes of the slice: x: 4, y: 4, z: 8 (z_hi: 4, z_lo: 2; z = z_hi * 2 + z_lo), core: 2. Of those that a mesh axis runs over, the one named last changes fastest.
Arguments:
- start_states: float32 [8, 256, 64, 256], P('tm', 'gz'), may hold values from -1.2 to 1.2
Outputs:
- new_states: float32 [8, 256, 64, 256], P('tm', 'gz')
All inputs are finite; a program needn't handle non-finite values.
Results may differ from a plain program's by a relative error of at most 0.000086.
Values sent between devices are 32-bit elements; how exact they have to be, the bound alone decides.
No kernel may reach another device: no remote copies, remote signals or barrier semaphores. Data moves between devices by JAX's collectives and lax.ppermute only.
A program may use at most 64 MiB of HBM per device.

v0:
```python
import jax
import jax.numpy as jnp
from jax import lax
from jax.sharding import PartitionSpec as P

COARSE_STEPS = 2
FINE_STEPS = 8


fine_dt = 0.025
coarse_dt = 0.1
fine_coef = 4.8
coarse_coef = 1.2


def with_halo(cells, sides, width):
    for axis, dim in sides:
        count = lax.axis_size(axis)
        ends = count - 1
        head = lax.slice_in_dim(cells, 0, width, axis=dim)
        tail = lax.slice_in_dim(cells, cells.shape[dim] - width, cells.shape[dim], axis=dim)
        cells = jnp.concatenate(
            [
                lax.ppermute(tail, axis, [(i, (i + 1) % count) for i in range(ends)]),
                cells,
                lax.ppermute(head, axis, [((i + 1) % count, i) for i in range(ends)]),
            ],
            axis=dim,
        )
    return cells


def passed_along(array, axis, by):
    length = lax.axis_size(axis)
    pairs = [(i, i + by) for i in range(length) if 0 <= i + by < length]
    return lax.ppermute(array, axis, pairs)


def rate(padded, coef):
    center = padded[1:-1]
    lap = padded[2:] + padded[:-2]
    lap = lap + jnp.roll(center, 1, 1) + jnp.roll(center, -1, 1)
    lap = lap + jnp.roll(center, 1, 2) + jnp.roll(center, -1, 2)
    lap = lap - 6.0 * center
    return coef * lap + center - center * center * center


def fine_pad(field):
    return with_halo(field, (("gz", 0),), 1)


def coarse_pad(field):
    return with_halo(field, (("gz", 0),), 1)


def coarse_heun(field):
    first = rate(coarse_pad(field), coarse_coef)
    middle = field + coarse_dt * first
    second = rate(coarse_pad(middle), coarse_coef)
    return field + 0.5 * coarse_dt * (first + second)


def coarse_propagate(field):
    for step in range(COARSE_STEPS):
        field = coarse_heun(field)
    return field


def fine_heun(field):
    first = rate(fine_pad(field), fine_coef)
    middle = field + fine_dt * first
    second = rate(fine_pad(middle), fine_coef)
    return field + 0.5 * fine_dt * (first + second)


def restrict(field):
    field = field[0::2] + field[1::2]
    field = field[:, 0::2] + field[:, 1::2]
    field = field[:, :, 0::2] + field[:, :, 1::2]
    return field * 0.125


def prolong(field):
    return jnp.repeat(jnp.repeat(jnp.repeat(field, 2, 0), 2, 1), 2, 2)


def per_device(start_states):
    start = start_states[0]
    fine_end = start
    for step in range(FINE_STEPS):
        fine_end = fine_heun(fine_end)
    coarse_start = restrict(start)
    coarse_old = coarse_propagate(coarse_start)
    jump = restrict(fine_end) - coarse_old
    slab = lax.axis_index("tm")
    slabs = lax.axis_size("tm")
    current = coarse_start
    picked = coarse_start
    for turn in range(slabs):
        picked = coarse_propagate(current)
        if turn + 1 < slabs:
            arrived = passed_along(picked + jump, "tm", 1)
            current = jnp.where(slab == 0, coarse_start, arrived)
    result = prolong(picked) + (fine_end - prolong(coarse_old))
    return result[None]


def solution(mesh):
    placed = (P("tm", "gz", None, None),)
    return jax.shard_map(
        per_device, mesh=mesh, in_specs=placed, out_specs=P("tm", "gz", None, None), check_vma=False
    )
```

profile of v0, /device:TPU:158, one launch (start us, length us, event | category | flops | bytes accessed | tf_op | source)
XLA Modules:
  0.0 662.8 jit_solution(1036220254485639728)
XLA Ops:
  12.4 6.7 %collective-permute-start.1 = (f32[1,32,128]{2,1,0:T(8,128)S(1)}, f32[1,32,128]{2,1,0:T(8,128)S(1)}, u32[]{:S(2)}, u32[]{:S(2)}) collective-permute-start(f32[1,32,128]{2,1,0:T(8,128)S(1)} %get-tuple-element.527), channel_id=1, source_target_pairs={{0,1},{1,2},{2,3},{3,4},{4,5},{5,6},{6,7},{7,8},{8,9},{9,10},{10,1... | collective-permute-start | bytes 49160 | tf_op jit(solution)/shard_map/ppermute | solution.py:24
  21.8 7.2 %collective-permute-done = f32[1,32,128]{2,1,0:T(8,128)S(1)} collective-permute-done((f32[1,32,128]{2,1,0:T(8,128)S(1)}, f32[1,32,128]{2,1,0:T(8,128)S(1)}, u32[]{:S(2)}, u32[]{:S(2)}) %collective-permute-start) | collective-permute-done | bytes 16416 | tf_op jit(solution)/shard_map/ppermute | solution.py:26
  35.2 5.9 collective-permute-done.2
  47.3 5.9 collective-permute-done.4
  60.4 6.1 collective-permute-start.11
  68.5 8.4 %collective-permute-done.10 = f32[1,64,256]{2,1,0:T(8,128)S(1)} collective-permute-done((f32[1,64,256]{2,1,0:T(8,128)S(1)}, f32[1,64,256]{2,1,0:T(8,128)S(1)}, u32[]{:S(2)}, u32[]{:S(2)}) %collective-permute-start.10) | collective-permute-done | bytes 65568 | tf_op jit(solution)/shard_map/ppermute | solution.py:26
  84.0 6.1 collective-permute-done.12
  97.3 6.1 collective-permute-done.14
  110.5 6.1 collective-permute-done.16
  123.7 6.1 collective-permute-done.18
  137.4 6.0 collective-permute-done.20
  150.5 6.3 collective-permute-done.22
  163.9 6.1 collective-permute-done.24
  177.1 6.1 collective-permute-done.26
  190.4 6.1 collective-permute-done.28
  203.6 6.1 collective-permute-done.30
  216.9 6.1 collective-permute-done.32
  230.1 6.1 collective-permute-done.34
  243.4 6.1 collective-permute-done.36
  256.6 6.1 collective-permute-done.38
  281.8 5.9 collective-permute-done.41
  293.9 5.9 collective-permute-done.43
  306.0 5.9 collective-permute-done.45
  318.1 5.9 collective-permute-done.47
  337.9 5.9 collective-permute-done.50
  350.0 5.9 collective-permute-done.52
  362.1 5.9 collective-permute-done.54
  394.0 5.9 collective-permute-done.59
  406.1 5.9 collective-permute-done.61
  438.3 5.9 collective-permute-done.67
  598.8 5.9 collective-permute-done.92
  618.7 5.9 collective-permute-done.95
  (497 shorter events, 462.8 us)
Async XLA Ops:
  0.9 58.5 %collective-permute-start.9 = (f32[1,64,256]{2,1,0:T(8,128)S(1)}, f32[1,64,256]{2,1,0:T(8,128)S(1)}, u32[]{:S(2)}, u32[]{:S(2)}) collective-permute-start(f32[1,64,256]{2,1,0:T(8,128)S(1)} %get-tuple-element.207), channel_id=1, source_target_pairs={{0,1},{1,2},{2,3},{3,4},{4,5},{5,6},{6,7},{7,8},{8,9},{9,10},{10,1... | collective-permute-start | bytes 196616 | tf_op jit(solution)/shard_map/ppermute | solution.py:24
  3.4 56.0 %collective-permute-start.8 = (f32[1,64,256]{2,1,0:T(8,128)S(1)}, f32[1,64,256]{2,1,0:T(8,128)S(1)}, u32[]{:S(2)}, u32[]{:S(2)}) collective-permute-start(f32[1,64,256]{2,1,0:T(8,128)S(1)} %get-tuple-element.206), channel_id=1, source_target_pairs={{1,0},{2,1},{3,2},{4,3},{5,4},{6,5},{7,6},{8,7},{9,8},{10,9},{11,1... | collective-permute-start | bytes 196616 | tf_op jit(solution)/shard_map/ppermute | solution.py:26
  19.2 9.9 %collective-permute-start = (f32[1,32,128]{2,1,0:T(8,128)S(1)}, f32[1,32,128]{2,1,0:T(8,128)S(1)}, u32[]{:S(2)}, u32[]{:S(2)}) collective-permute-start(f32[1,32,128]{2,1,0:T(8,128)S(1)} %get-tuple-element.526), channel_id=1, source_target_pairs={{1,0},{2,1},{3,2},{4,3},{5,4},{6,5},{7,6},{8,7},{9,8},{10,9},{11,1... | collective-permute-start | bytes 49160 | tf_op jit(solution)/shard_map/ppermute | solution.py:26
  31.2 9.9 %collective-permute-start.2 = (f32[1,32,128]{2,1,0:T(8,128)S(1)}, f32[1,32,128]{2,1,0:T(8,128)S(1)}, u32[]{:S(2)}, u32[]{:S(2)}) collective-permute-start(f32[1,32,128]{2,1,0:T(8,128)S(1)} %get-tuple-element.524), channel_id=1, source_target_pairs={{1,0},{2,1},{3,2},{4,3},{5,4},{6,5},{7,6},{8,7},{9,8},{10,9},{11,1... | collective-permute-start | bytes 49160 | tf_op jit(solution)/shard_map/ppermute | solution.py:26
  43.4 9.9 %collective-permute-start.4 = (f32[1,32,128]{2,1,0:T(8,128)S(1)}, f32[1,32,128]{2,1,0:T(8,128)S(1)}, u32[]{:S(2)}, u32[]{:S(2)}) collective-permute-start(f32[1,32,128]{2,1,0:T(8,128)S(1)} %get-tuple-element.506), channel_id=1, source_target_pairs={{1,0},{2,1},{3,2},{4,3},{5,4},{6,5},{7,6},{8,7},{9,8},{10,9},{11,1... | collective-permute-start | bytes 49160 | tf_op jit(solution)/shard_map/ppermute | solution.py:26
  53.5 214.3 %collective-permute-start.7 = (f32[1,32,128]{2,1,0:T(8,128)S(1)}, f32[1,32,128]{2,1,0:T(8,128)S(1)}, u32[]{:S(2)}, u32[]{:S(2)}) collective-permute-start(f32[1,32,128]{2,1,0:T(8,128)S(1)} %get-tuple-element.497), channel_id=1, source_target_pairs={{0,1},{1,2},{2,3},{3,4},{4,5},{5,6},{6,7},{7,8},{8,9},{9,10},{10,1... | collective-permute-start | bytes 49160 | tf_op jit(solution)/shard_map/ppermute | solution.py:24
  55.5 212.4 %collective-permute-start.6 = (f32[1,32,128]{2,1,0:T(8,128)S(1)}, f32[1,32,128]{2,1,0:T(8,128)S(1)}, u32[]{:S(2)}, u32[]{:S(2)}) collective-permute-start(f32[1,32,128]{2,1,0:T(8,128)S(1)} %get-tuple-element.496), channel_id=1, source_target_pairs={{1,0},{2,1},{3,2},{4,3},{5,4},{6,5},{7,6},{8,7},{9,8},{10,9},{11,1... | collective-permute-start | bytes 49160 | tf_op jit(solution)/shard_map/ppermute | solution.py:26
  66.5 10.4 %collective-permute-start.10 = (f32[1,64,256]{2,1,0:T(8,128)S(1)}, f32[1,64,256]{2,1,0:T(8,128)S(1)}, u32[]{:S(2)}, u32[]{:S(2)}) collective-permute-start(f32[1,64,256]{2,1,0:T(8,128)S(1)} %get-tuple-element.204), channel_id=1, source_target_pairs={{1,0},{2,1},{3,2},{4,3},{5,4},{6,5},{7,6},{8,7},{9,8},{10,9},{11,1... | collective-permute-start | bytes 196616 | tf_op jit(solution)/shard_map/ppermute | solution.py:26
  79.8 10.4 %collective-permute-start.12 = (f32[1,64,256]{2,1,0:T(8,128)S(1)}, f32[1,64,256]{2,1,0:T(8,128)S(1)}, u32[]{:S(2)}, u32[]{:S(2)}) collective-permute-start(f32[1,64,256]{2,1,0:T(8,128)S(1)} %get-tuple-element.186), channel_id=1, source_target_pairs={{1,0},{2,1},{3,2},{4,3},{5,4},{6,5},{7,6},{8,7},{9,8},{10,9},{11,1... | collective-permute-start | bytes 196616 | tf_op jit(solution)/shard_map/ppermute | solution.py:26
  93.0 10.4 %collective-permute-start.14 = (f32[1,64,256]{2,1,0:T(8,128)S(1)}, f32[1,64,256]{2,1,0:T(8,128)S(1)}, u32[]{:S(2)}, u32[]{:S(2)}) collective-permute-start(f32[1,64,256]{2,1,0:T(8,128)S(1)} %get-tuple-element.184), channel_id=1, source_target_pairs={{1,0},{2,1},{3,2},{4,3},{5,4},{6,5},{7,6},{8,7},{9,8},{10,9},{11,1... | collective-permute-start | bytes 196616 | tf_op jit(solution)/shard_map/ppermute | solution.py:26
  106.3 10.4 %collective-permute-start.16 = (f32[1,64,256]{2,1,0:T(8,128)S(1)}, f32[1,64,256]{2,1,0:T(8,128)S(1)}, u32[]{:S(2)}, u32[]{:S(2)}) collective-permute-start(f32[1,64,256]{2,1,0:T(8,128)S(1)} %get-tuple-element.166), channel_id=1, source_target_pairs={{1,0},{2,1},{3,2},{4,3},{5,4},{6,5},{7,6},{8,7},{9,8},{10,9},{11,1... | collective-permute-start | bytes 196616 | tf_op jit(solution)/shard_map/ppermute | solution.py:26
  119.5 10.4 %collective-permute-start.18 = (f32[1,64,256]{2,1,0:T(8,128)S(1)}, f32[1,64,256]{2,1,0:T(8,128)S(1)}, u32[]{:S(2)}, u32[]{:S(2)}) collective-permute-start(f32[1,64,256]{2,1,0:T(8,128)S(1)} %get-tuple-element.164), channel_id=1, source_target_pairs={{1,0},{2,1},{3,2},{4,3},{5,4},{6,5},{7,6},{8,7},{9,8},{10,9},{11,1... | collective-permute-start | bytes 196616 | tf_op jit(solution)/shard_map/ppermute | solution.py:26
  132.8 10.6 %collective-permute-start.20 = (f32[1,64,256]{2,1,0:T(8,128)S(1)}, f32[1,64,256]{2,1,0:T(8,128)S(1)}, u32[]{:S(2)}, u32[]{:S(2)}) collective-permute-start(f32[1,64,256]{2,1,0:T(8,128)S(1)} %get-tuple-element.146), channel_id=1, source_target_pairs={{1,0},{2,1},{3,2},{4,3},{5,4},{6,5},{7,6},{8,7},{9,8},{10,9},{11,1... | collective-permute-start | bytes 196616 | tf_op jit(solution)/shard_map/ppermute | solution.py:26
  146.2 10.6 %collective-permute-start.22 = (f32[1,64,256]{2,1,0:T(8,128)S(1)}, f32[1,64,256]{2,1,0:T(8,128)S(1)}, u32[]{:S(2)}, u32[]{:S(2)}) collective-permute-start(f32[1,64,256]{2,1,0:T(8,128)S(1)} %get-tuple-element.144), channel_id=1, source_target_pairs={{1,0},{2,1},{3,2},{4,3},{5,4},{6,5},{7,6},{8,7},{9,8},{10,9},{11,1... | collective-permute-start | bytes 196616 | tf_op jit(solution)/shard_map/ppermute | solution.py:26
  159.7 10.4 %collective-permute-start.24 = (f32[1,64,256]{2,1,0:T(8,128)S(1)}, f32[1,64,256]{2,1,0:T(8,128)S(1)}, u32[]{:S(2)}, u32[]{:S(2)}) collective-permute-start(f32[1,64,256]{2,1,0:T(8,128)S(1)} %get-tuple-element.126), channel_id=1, source_target_pairs={{1,0},{2,1},{3,2},{4,3},{5,4},{6,5},{7,6},{8,7},{9,8},{10,9},{11,1... | collective-permute-start | bytes 196616 | tf_op jit(solution)/shard_map/ppermute | solution.py:26
  172.9 10.4 %collective-permute-start.26 = (f32[1,64,256]{2,1,0:T(8,128)S(1)}, f32[1,64,256]{2,1,0:T(8,128)S(1)}, u32[]{:S(2)}, u32[]{:S(2)}) collective-permute-start(f32[1,64,256]{2,1,0:T(8,128)S(1)} %get-tuple-element.124), channel_id=1, source_target_pairs={{1,0},{2,1},{3,2},{4,3},{5,4},{6,5},{7,6},{8,7},{9,8},{10,9},{11,1... | collective-permute-start | bytes 196616 | tf_op jit(solution)/shard_map/ppermute | solution.py:26
  186.2 10.4 %collective-permute-start.28 = (f32[1,64,256]{2,1,0:T(8,128)S(1)}, f32[1,64,256]{2,1,0:T(8,128)S(1)}, u32[]{:S(2)}, u32[]{:S(2)}) collective-permute-start(f32[1,64,256]{2,1,0:T(8,128)S(1)} %get-tuple-element.106), channel_id=1, source_target_pairs={{1,0},{2,1},{3,2},{4,3},{5,4},{6,5},{7,6},{8,7},{9,8},{10,9},{11,1... | collective-permute-start | bytes 196616 | tf_op jit(solution)/shard_map/ppermute | solution.py:26
  199.4 10.4 %collective-permute-start.30 = (f32[1,64,256]{2,1,0:T(8,128)S(1)}, f32[1,64,256]{2,1,0:T(8,128)S(1)}, u32[]{:S(2)}, u32[]{:S(2)}) collective-permute-start(f32[1,64,256]{2,1,0:T(8,128)S(1)} %get-tuple-element.104), channel_id=1, source_target_pairs={{1,0},{2,1},{3,2},{4,3},{5,4},{6,5},{7,6},{8,7},{9,8},{10,9},{11,1... | collective-permute-start | bytes 196616 | tf_op jit(solution)/shard_map/ppermute | solution.py:26
  212.7 10.4 %collective-permute-start.32 = (f32[1,64,256]{2,1,0:T(8,128)S(1)}, f32[1,64,256]{2,1,0:T(8,128)S(1)}, u32[]{:S(2)}, u32[]{:S(2)}) collective-permute-start(f32[1,64,256]{2,1,0:T(8,128)S(1)} %get-tuple-element.86), channel_id=1, source_target_pairs={{1,0},{2,1},{3,2},{4,3},{5,4},{6,5},{7,6},{8,7},{9,8},{10,9},{11,1... | collective-permute-start | bytes 196616 | tf_op jit(solution)/shard_map/ppermute | solution.py:26
  225.9 10.4 %collective-permute-start.34 = (f32[1,64,256]{2,1,0:T(8,128)S(1)}, f32[1,64,256]{2,1,0:T(8,128)S(1)}, u32[]{:S(2)}, u32[]{:S(2)}) collective-permute-start(f32[1,64,256]{2,1,0:T(8,128)S(1)} %get-tuple-element.84), channel_id=1, source_target_pairs={{1,0},{2,1},{3,2},{4,3},{5,4},{6,5},{7,6},{8,7},{9,8},{10,9},{11,1... | collective-permute-start | bytes 196616 | tf_op jit(solution)/shard_map/ppermute | solution.py:26
  239.1 10.4 %collective-permute-start.36 = (f32[1,64,256]{2,1,0:T(8,128)S(1)}, f32[1,64,256]{2,1,0:T(8,128)S(1)}, u32[]{:S(2)}, u32[]{:S(2)}) collective-permute-start(f32[1,64,256]{2,1,0:T(8,128)S(1)} %get-tuple-element.66), channel_id=1, source_target_pairs={{1,0},{2,1},{3,2},{4,3},{5,4},{6,5},{7,6},{8,7},{9,8},{10,9},{11,1... | collective-permute-start | bytes 196616 | tf_op jit(solution)/shard_map/ppermute | solution.py:26
  252.4 10.4 %collective-permute-start.38 = (f32[1,64,256]{2,1,0:T(8,128)S(1)}, f32[1,64,256]{2,1,0:T(8,128)S(1)}, u32[]{:S(2)}, u32[]{:S(2)}) collective-permute-start(f32[1,64,256]{2,1,0:T(8,128)S(1)} %get-tuple-element.64), channel_id=1, source_target_pairs={{1,0},{2,1},{3,2},{4,3},{5,4},{6,5},{7,6},{8,7},{9,8},{10,9},{11,1... | collective-permute-start | bytes 196616 | tf_op jit(solution)/shard_map/ppermute | solution.py:26
  277.8 9.9 %collective-permute-start.41 = (f32[1,32,128]{2,1,0:T(8,128)S(1)}, f32[1,32,128]{2,1,0:T(8,128)S(1)}, u32[]{:S(2)}, u32[]{:S(2)}) collective-permute-start(f32[1,32,128]{2,1,0:T(8,128)S(1)} %get-tuple-element.486), channel_id=1, source_target_pairs={{1,0},{2,1},{3,2},{4,3},{5,4},{6,5},{7,6},{8,7},{9,8},{10,9},{11,1... | collective-permute-start | bytes 49160 | tf_op jit(solution)/shard_map/ppermute | solution.py:26
  289.9 9.9 %collective-permute-start.43 = (f32[1,32,128]{2,1,0:T(8,128)S(1)}, f32[1,32,128]{2,1,0:T(8,128)S(1)}, u32[]{:S(2)}, u32[]{:S(2)}) collective-permute-start(f32[1,32,128]{2,1,0:T(8,128)S(1)} %get-tuple-element.484), channel_id=1, source_target_pairs={{1,0},{2,1},{3,2},{4,3},{5,4},{6,5},{7,6},{8,7},{9,8},{10,9},{11,1... | collective-permute-start | bytes 49160 | tf_op jit(solution)/shard_map/ppermute | solution.py:26
  302.0 9.9 %collective-permute-start.45 = (f32[1,32,128]{2,1,0:T(8,128)S(1)}, f32[1,32,128]{2,1,0:T(8,128)S(1)}, u32[]{:S(2)}, u32[]{:S(2)}) collective-permute-start(f32[1,32,128]{2,1,0:T(8,128)S(1)} %get-tuple-element.466), channel_id=1, source_target_pairs={{1,0},{2,1},{3,2},{4,3},{5,4},{6,5},{7,6},{8,7},{9,8},{10,9},{11,1... | collective-permute-start | bytes 49160 | tf_op jit(solution)/shard_map/ppermute | solution.py:26
  314.1 9.9 %collective-permute-start.47 = (f32[1,32,128]{2,1,0:T(8,128)S(1)}, f32[1,32,128]{2,1,0:T(8,128)S(1)}, u32[]{:S(2)}, u32[]{:S(2)}) collective-permute-start(f32[1,32,128]{2,1,0:T(8,128)S(1)} %get-tuple-element.464), channel_id=1, source_target_pairs={{1,0},{2,1},{3,2},{4,3},{5,4},{6,5},{7,6},{8,7},{9,8},{10,9},{11,1... | collective-permute-start | bytes 49160 | tf_op jit(solution)/shard_map/ppermute | solution.py:26
  333.9 9.9 %collective-permute-start.50 = (f32[1,32,128]{2,1,0:T(8,128)S(1)}, f32[1,32,128]{2,1,0:T(8,128)S(1)}, u32[]{:S(2)}, u32[]{:S(2)}) collective-permute-start(f32[1,32,128]{2,1,0:T(8,128)S(1)} %get-tuple-element.446), channel_id=1, source_target_pairs={{1,0},{2,1},{3,2},{4,3},{5,4},{6,5},{7,6},{8,7},{9,8},{10,9},{11,1... | collective-permute-start | bytes 49160 | tf_op jit(solution)/shard_map/ppermute | solution.py:26
  346.0 9.9 %collective-permute-start.52 = (f32[1,32,128]{2,1,0:T(8,128)S(1)}, f32[1,32,128]{2,1,0:T(8,128)S(1)}, u32[]{:S(2)}, u32[]{:S(2)}) collective-permute-start(f32[1,32,128]{2,1,0:T(8,128)S(1)} %get-tuple-element.444), channel_id=1, source_target_pairs={{1,0},{2,1},{3,2},{4,3},{5,4},{6,5},{7,6},{8,7},{9,8},{10,9},{11,1... | collective-permute-start | bytes 49160 | tf_op jit(solution)/shard_map/ppermute | solution.py:26
  358.1 9.9 %collective-permute-start.54 = (f32[1,32,128]{2,1,0:T(8,128)S(1)}, f32[1,32,128]{2,1,0:T(8,128)S(1)}, u32[]{:S(2)}, u32[]{:S(2)}) collective-permute-start(f32[1,32,128]{2,1,0:T(8,128)S(1)} %get-tuple-element.426), channel_id=1, source_target_pairs={{1,0},{2,1},{3,2},{4,3},{5,4},{6,5},{7,6},{8,7},{9,8},{10,9},{11,1... | collective-permute-start | bytes 49160 | tf_op jit(solution)/shard_map/ppermute | solution.py:26
  390.1 9.9 %collective-permute-start.59 = (f32[1,32,128]{2,1,0:T(8,128)S(1)}, f32[1,32,128]{2,1,0:T(8,128)S(1)}, u32[]{:S(2)}, u32[]{:S(2)}) collective-permute-start(f32[1,32,128]{2,1,0:T(8,128)S(1)} %get-tuple-element.406), channel_id=1, source_target_pairs={{1,0},{2,1},{3,2},{4,3},{5,4},{6,5},{7,6},{8,7},{9,8},{10,9},{11,1... | collective-permute-start | bytes 49160 | tf_op jit(solution)/shard_map/ppermute | solution.py:26
  402.2 9.9 %collective-permute-start.61 = (f32[1,32,128]{2,1,0:T(8,128)S(1)}, f32[1,32,128]{2,1,0:T(8,128)S(1)}, u32[]{:S(2)}, u32[]{:S(2)}) collective-permute-start(f32[1,32,128]{2,1,0:T(8,128)S(1)} %get-tuple-element.404), channel_id=1, source_target_pairs={{1,0},{2,1},{3,2},{4,3},{5,4},{6,5},{7,6},{8,7},{9,8},{10,9},{11,1... | collective-permute-start | bytes 49160 | tf_op jit(solution)/shard_map/ppermute | solution.py:26
  414.3 9.9 %collective-permute-start.63 = (f32[1,32,128]{2,1,0:T(8,128)S(1)}, f32[1,32,128]{2,1,0:T(8,128)S(1)}, u32[]{:S(2)}, u32[]{:S(2)}) collective-permute-start(f32[1,32,128]{2,1,0:T(8,128)S(1)} %get-tuple-element.386), channel_id=1, source_target_pairs={{1,0},{2,1},{3,2},{4,3},{5,4},{6,5},{7,6},{8,7},{9,8},{10,9},{11,1... | collective-permute-start | bytes 49160 | tf_op jit(solution)/shard_map/ppermute | solution.py:26
  (72 other events, 524.9 us)
where the time goes:
time: 666 us; the launch traced here: 663 us
  waiting for transfers between devices  322 us (48%)
  starting transfers between devices  299 us (45%)
  local copies, waits for them, and re-layouts  24.8 us (4%)
  other arithmetic  13.6 us (2%)
    ppermute x48, waiting for transfers between devices, with_halo(): lax.ppermute(head, axis, [((i + 1) % count, i) for i in range(ends)])  279 us
    ppermute x48, starting transfers between devices, with_halo(): lax.ppermute(head, axis, [((i + 1) % count, i) for i in range(ends)])  184 us
    ppermute x48, starting transfers between devices, with_halo(): lax.ppermute(tail, axis, [(i, (i + 1) % count) for i in range(ends)])  102 us
    ppermute x7, waiting for transfers between devices, passed_along(): return lax.ppermute(array, axis, pairs)  39.5 us
    ppermute x7, starting transfers between devices, passed_along(): return lax.ppermute(array, axis, pairs)  13.7 us
  transfers between devices with their start and end apart: 103, of which 67 were waited for; matrix products, arithmetic and copies ran while one was open for 4% of the time, Pallas kernels for 0%

commit v1 on v0

v1 whole, which is shorter than its diff:
```python
import functools
import math

import jax
import jax.numpy as jnp
from jax import lax
from jax.experimental import pallas as pl
from jax.experimental.pallas import tpu as pltpu
from jax.sharding import PartitionSpec as P

COARSE_STEPS = 2
FINE_STEPS = 8

fine_dt = 0.025
coarse_dt = 0.1
fine_coef = 4.8
coarse_coef = 1.2

KAPPA = math.sqrt(fine_dt)
FINE_A = 1.0 + fine_dt * (1.0 - 6.0 * fine_coef)
FINE_C = fine_dt * fine_coef
COARSE_A = 1.0 + coarse_dt * (1.0 - 6.0 * coarse_coef)
COARSE_B = coarse_dt / fine_dt
COARSE_C = coarse_dt * coarse_coef

CZ, NX, NY = 8, 64, 256
WIDE = 2 * FINE_STEPS
CC, CX, CY = CZ // 2, NX // 2, NY // 2
REACH = 2 * COARSE_STEPS
VMEM_LIMIT = 40 * 1024 * 1024


def x_sum(a):
    n = a.shape[0]
    after = jnp.concatenate([a[8:], pltpu.roll(a[:8], 7, 0)], axis=0)
    before = jnp.concatenate([pltpu.roll(a[n - 8 :], 1, 0), a[: n - 8]], axis=0)
    return after + before


def split_dot(a, m):
    hi = a.astype(jnp.bfloat16)
    rest = a - hi.astype(jnp.float32)
    mid = rest.astype(jnp.bfloat16)
    low = (rest - mid.astype(jnp.float32)).astype(jnp.bfloat16)
    dot = functools.partial(jnp.dot, preferred_element_type=jnp.float32)
    return dot(hi, m) + (dot(mid, m) + dot(low, m))


def fine_euler(src, p, c):
    out = []
    for j, by in ((0, 1), (1, CY - 1)):
        a = src[p, j]
        b = src[p, 1 - j]
        total = (src[p - 1, j] + src[p + 1, j]) + (x_sum(a) + (b + pltpu.roll(b, by, 1)))
        out.append(c * total + a * (FINE_A - a * a))
    return out


def coarse_euler(src, p, c):
    a = src[p]
    total = (src[p - 1] + src[p + 1]) + (x_sum(a) + (pltpu.roll(a, 1, 1) + pltpu.roll(a, CY - 1, 1)))
    return c * total + a * (COARSE_A - COARSE_B * (a * a))


def inside(first, p, count, coef):
    g = first + p
    return jnp.where((g >= 0) & (g < count), coef, 0.0).astype(jnp.float32)


def coarse_propagate(v, v1, first, count):
    n = CC + 2 * REACH
    for step in range(COARSE_STEPS):
        lo = 2 * step + 1
        for p in range(lo, n - lo):
            v1[p] = coarse_euler(v, p, inside(first, p, count, COARSE_C))
        for p in range(lo + 1, n - lo - 1):
            v[p] = 0.5 * (v[p] + coarse_euler(v1, p, inside(first, p, count, COARSE_C)))


def restricted(v, p):
    s = (v[p, 0] + v[p + 1, 0]) + (v[p, 1] + v[p + 1, 1])
    rows = [s[16 * i : 16 * i + 8] + s[16 * i + 8 : 16 * i + 16] for i in range(4)]
    return 0.125 * jnp.concatenate(rows, axis=0)


def prep_kernel(x_ref, out_ref, x, sems):
    copies = []
    for h in range(2):
        copies.append(pltpu.make_async_copy(x_ref.at[0, :, :, pl.ds(h * CY, CY)], x.at[h], sems.at[h]))
        copies[-1].start()
    y = lax.broadcasted_iota(jnp.int32, (NY, NY), 0)
    k = lax.broadcasted_iota(jnp.int32, (NY, NY), 1)
    m = (y == 2 * (k % CY) + k // CY).astype(jnp.float32).astype(jnp.bfloat16)

    for copy in copies:
        copy.wait()

    def body(p, carry):
        halves = []
        for h in range(2):
            rows = [x[h, p, pl.ds(i, 8, stride=8), :] for i in range(8)]
            halves.append(jnp.concatenate(rows, axis=0))
        r = split_dot(jnp.concatenate(halves, axis=1), m) * KAPPA
        out_ref[p, 0] = r[:, :CY]
        out_ref[p, 1] = r[:, CY:]
        return carry

    lax.fori_loop(0, CZ, body, 0)


def fine_kernel(
    blocks, place_ref, l2, l1, own, r1, r2, fe_ref, co_ref, jump_ref, send_ref, v, v1, cv, cv1, sems
):
    place = place_ref[0]
    copies = []
    for n, ref in enumerate((l2, l1, own, r1, r2)):
        copies.append(pltpu.make_async_copy(ref, v.at[pl.ds(n * CZ, CZ)], sems.at[n]))
        copies[-1].start()
    for copy in copies:
        copy.wait()
    for q in range(CC + 2 * REACH):
        cv[q] = restricted(v, WIDE - 2 * REACH + 2 * q)
    coarse_propagate(cv, cv1, place * CC - REACH, blocks * CC)
    first = place * CZ - WIDE
    n = CZ + 2 * WIDE
    for step in range(FINE_STEPS):
        lo = 2 * step + 1

        def predict(p, carry):
            a, b = fine_euler(v, p, inside(first, p, blocks * CZ, FINE_C))
            v1[p, 0] = a
            v1[p, 1] = b
            return carry

        def correct(p, carry):
            a, b = fine_euler(v1, p, inside(first, p, blocks * CZ, FINE_C))
            v[p, 0] = 0.5 * (v[p, 0] + a)
            v[p, 1] = 0.5 * (v[p, 1] + b)
            return carry

        lax.fori_loop(lo, n - lo, predict, 0)
        lax.fori_loop(lo + 1, n - lo - 1, correct, 0)
    fe_ref[...] = v[pl.ds(WIDE, CZ)]
    for q in range(CC):
        old = cv[REACH + q]
        jump = restricted(v, WIDE + 2 * q) - old
        co_ref[q] = old
        jump_ref[q] = jump
        send_ref[q] = old + jump


def sweep_kernel(blocks, turn, place_ref, left, mid, right, jump_ref, picked_ref, out_ref, send_ref, cv, cv1):
    place = place_ref[0]
    slab = place_ref[1]

    @pl.when(slab == turn)
    def _():
        for n, ref in enumerate((left, mid, right)):
            cv[pl.ds(n * CC, CC)] = ref[...]
        coarse_propagate(cv, cv1, place * CC - REACH, blocks * CC)
        for q in range(CC):
            new = cv[REACH + q]
            out_ref[q] = new
            send_ref[q] = new + jump_ref[q]

    @pl.when(slab != turn)
    def _():
        out_ref[...] = picked_ref[...]
        send_ref[...] = jump_ref[...]


def final_kernel(fe_ref, co_ref, picked_ref, out_ref, x, sems):
    k = lax.broadcasted_iota(jnp.int32, (NY, NY), 0)
    y = lax.broadcasted_iota(jnp.int32, (NY, NY), 1)
    m = (y == 2 * (k % CY) + k // CY).astype(jnp.float32).astype(jnp.bfloat16)

    def body(p, carry):
        new = picked_ref[p // 2]
        old = co_ref[p // 2]

        def spread(a):
            rows = []
            for i in range(8):
                rows.append(a[8 * (i // 2) : 8 * (i // 2) + 8])
            return jnp.concatenate(rows, axis=0)

        new = spread(new)
        old = spread(old)
        r = jnp.concatenate([new + (fe_ref[p, j] - old) for j in range(2)], axis=1)
        r = split_dot(r, m) * (1.0 / KAPPA)
        for h in range(2):
            for i in range(8):
                x[h, p, pl.ds(i, 8, stride=8), :] = r[8 * i : 8 * i + 8, h * CY : (h + 1) * CY]
        return carry

    lax.fori_loop(0, CZ, body, 0)
    copies = []
    for h in range(2):
        copies.append(pltpu.make_async_copy(x.at[h], out_ref.at[0, :, :, pl.ds(h * CY, CY)], sems.at[h]))
        copies[-1].start()
    for copy in copies:
        copy.wait()


VM = pl.BlockSpec(memory_space=pltpu.VMEM)
SM = pl.BlockSpec(memory_space=pltpu.SMEM)
HB = pl.BlockSpec(memory_space=pl.ANY)
PARAMS = pltpu.CompilerParams(vmem_limit_bytes=VMEM_LIMIT)
fine_shape = jax.ShapeDtypeStruct((CZ, 2, NX, CY), jnp.float32)
coarse_shape = jax.ShapeDtypeStruct((CC, CX, CY), jnp.float32)
HALVES = [pltpu.VMEM((2, CZ, NX, CY), jnp.float32), pltpu.SemaphoreType.DMA((2,))]


def shifted(array, by):
    count = lax.axis_size("gz")
    return lax.ppermute(array, "gz", [(i, i + by) for i in range(count) if 0 <= i + by < count])


def handed(array, turn, by):
    count = lax.axis_size("gz")
    pairs = [((turn - 1) * count + i, turn * count + i + by) for i in range(count) if 0 <= i + by < count]
    return lax.ppermute(array, ("tm", "gz"), pairs)


def per_device(start_states):
    blocks = lax.axis_size("gz")
    slabs = lax.axis_size("tm")
    place = jnp.stack([lax.axis_index("gz"), lax.axis_index("tm")]).astype(jnp.int32)
    own = pl.pallas_call(
        prep_kernel,
        out_shape=fine_shape,
        in_specs=[HB],
        out_specs=VM,
        scratch_shapes=HALVES,
        compiler_params=PARAMS,
    )(start_states)
    l1, r1, l2, r2 = shifted(own, 1), shifted(own, -1), shifted(own, 2), shifted(own, -2)
    wide = (CZ + 2 * WIDE, 2, NX, CY)
    coarse_wide = (CC + 2 * REACH, CX, CY)
    fine_end, coarse_old, jump, send = pl.pallas_call(
        functools.partial(fine_kernel, blocks),
        out_shape=(fine_shape, coarse_shape, coarse_shape, coarse_shape),
        in_specs=[SM] + [HB] * 5,
        out_specs=(VM,) * 4,
        scratch_shapes=[
            pltpu.VMEM(wide, jnp.float32),
            pltpu.VMEM(wide, jnp.float32),
            pltpu.VMEM(coarse_wide, jnp.float32),
            pltpu.VMEM(coarse_wide, jnp.float32),
            pltpu.SemaphoreType.DMA((5,)),
        ],
        compiler_params=PARAMS,
    )(place, l2, l1, own, r1, r2)
    picked = coarse_old
    for turn in range(1, slabs):
        left, mid, right = handed(send, turn, 1), handed(send, turn, 0), handed(send, turn, -1)
        picked, send = pl.pallas_call(
            functools.partial(sweep_kernel, blocks, turn),
            out_shape=(coarse_shape, coarse_shape),
            in_specs=[SM] + [VM] * 5,
            out_specs=(VM,) * 2,
            scratch_shapes=[pltpu.VMEM(coarse_wide, jnp.float32)] * 2,
            compiler_params=PARAMS,
        )(place, left, mid, right, jump, picked)
    return pl.pallas_call(
        final_kernel,
        out_shape=jax.ShapeDtypeStruct((1, CZ, NX, NY), jnp.float32),
        in_specs=[VM] * 3,
        out_specs=HB,
        scratch_shapes=HALVES,
        compiler_params=PARAMS,
    )(fine_end, coarse_old, picked)


def solution(mesh):
    placed = (P("tm", "gz", None, None),)
    return jax.shard_map(
        per_device, mesh=mesh, in_specs=placed, out_specs=P("tm", "gz", None, None), check_vma=False
    )
```

time: 666 us -> 150 us (0.23)
  the two profiles are of different devices: /device:TPU:158 before, /device:TPU:225 now
where the time goes in v1:
time: 150 us; the launch traced here: 148 us
  waiting for transfers between devices  71.8 us (48%)
  Pallas kernels  43.5 us (29%)
  starting transfers between devices  31.2 us (21%)
    ppermute x21, waiting for transfers between devices, handed(): return lax.ppermute(array, ('tm', 'gz'), pairs)  47.5 us
    pallas_call x1, Pallas kernels, per_device(): pl.pallas_call(functools.partial(fine_kernel, blocks), out_shape=(fine_sh...  34.3 us
    ppermute x4, waiting for transfers between devices, shifted(): lax.ppermute(array, 'gz', [(i, i + by) for i in range(count) if 0 <= i +...  24.3 us
    ppermute x21, starting transfers between devices, handed(): return lax.ppermute(array, ('tm', 'gz'), pairs)  15.8 us
    ppermute x4, starting transfers between devices, shifted(): lax.ppermute(array, 'gz', [(i, i + by) for i in range(count) if 0 <= i +...  15.4 us
    pallas_call x7, Pallas kernels, per_device(): pl.pallas_call(functools.partial(sweep_kernel, blocks, turn), out_shape=(...  4.91 us
  transfers between devices with their start and end apart: 25, of which 7 were waited for; matrix products, arithmetic and copies ran while one was open for 0% of the time, Pallas kernels for 0%

profile of v1, /device:TPU:225, one launch (start us, length us, event | category | flops | bytes accessed | tf_op | source)
XLA Modules:
  0.0 148.0 jit_solution(444193174573400514)
XLA Ops:
  0.0 1.0 copy-done
  1.0 1.7 %shard_map.17.own = f32[8,2,64,128]{3,2,1,0:T(8,128)S(1)} custom-call(f32[1,8,64,256]{3,2,1,0:T(8,128)S(1)} %copy-done), custom_call_target="tpu_custom_call" | custom-call | tf_op jit(solution)/shard_map/pallas_call | solution.py:229
  2.8 7.5 %collective-permute-start.3 = (f32[8,2,64,128]{3,2,1,0:T(8,128)S(1)}, f32[8,2,64,128]{3,2,1,0:T(8,128)S(1)}, u32[]{:S(2)}, u32[]{:S(2)}) collective-permute-start(f32[8,2,64,128]{3,2,1,0:T(8,128)S(1)} %shard_map.17.own), channel_id=1, source_target_pairs={{2,0},{3,1},{4,2},{5,3},{6,4},{7,5},{8,6},{9,7},{10,8},{11,9},{12,... | collective-permute-start | bytes 1572872 | tf_op jit(solution)/shard_map/ppermute | solution.py:216
  10.2 2.7 %collective-permute-start.2 = (f32[8,2,64,128]{3,2,1,0:T(8,128)S(1)}, f32[8,2,64,128]{3,2,1,0:T(8,128)S(1)}, u32[]{:S(2)}, u32[]{:S(2)}) collective-permute-start(f32[8,2,64,128]{3,2,1,0:T(8,128)S(1)} %shard_map.17.own), channel_id=1, source_target_pairs={{1,0},{2,1},{3,2},{4,3},{5,4},{6,5},{7,6},{8,7},{9,8},{10,9},{11,1... | collective-permute-start | bytes 1572872 | tf_op jit(solution)/shard_map/ppermute | solution.py:216
  12.9 2.6 %collective-permute-start.1 = (f32[8,2,64,128]{3,2,1,0:T(8,128)S(1)}, f32[8,2,64,128]{3,2,1,0:T(8,128)S(1)}, u32[]{:S(2)}, u32[]{:S(2)}) collective-permute-start(f32[8,2,64,128]{3,2,1,0:T(8,128)S(1)} %shard_map.17.own), channel_id=1, source_target_pairs={{0,1},{1,2},{2,3},{3,4},{4,5},{5,6},{6,7},{7,8},{8,9},{9,10},{10,1... | collective-permute-start | bytes 1572872 | tf_op jit(solution)/shard_map/ppermute | solution.py:216
  15.5 2.6 %collective-permute-start = (f32[8,2,64,128]{3,2,1,0:T(8,128)S(1)}, f32[8,2,64,128]{3,2,1,0:T(8,128)S(1)}, u32[]{:S(2)}, u32[]{:S(2)}) collective-permute-start(f32[8,2,64,128]{3,2,1,0:T(8,128)S(1)} %shard_map.17.own), channel_id=1, source_target_pairs={{0,2},{1,3},{2,4},{3,5},{4,6},{5,7},{6,8},{7,9},{8,10},{9,11},{10,... | collective-permute-start | bytes 1572872 | tf_op jit(solution)/shard_map/ppermute | solution.py:216
  18.3 2.5 %collective-permute-done.3.r2 = f32[8,2,64,128]{3,2,1,0:T(8,128)S(1)} collective-permute-done((f32[8,2,64,128]{3,2,1,0:T(8,128)S(1)}, f32[8,2,64,128]{3,2,1,0:T(8,128)S(1)}, u32[]{:S(2)}, u32[]{:S(2)}) %collective-permute-start.3) | collective-permute-done | bytes 524320 | tf_op jit(solution)/shard_map/ppermute | solution.py:216
  20.8 11.7 %collective-permute-done.2.r1 = f32[8,2,64,128]{3,2,1,0:T(8,128)S(1)} collective-permute-done((f32[8,2,64,128]{3,2,1,0:T(8,128)S(1)}, f32[8,2,64,128]{3,2,1,0:T(8,128)S(1)}, u32[]{:S(2)}, u32[]{:S(2)}) %collective-permute-start.2) | collective-permute-done | bytes 524320 | tf_op jit(solution)/shard_map/ppermute | solution.py:216
  32.5 4.5 %collective-permute-done.1.l1 = f32[8,2,64,128]{3,2,1,0:T(8,128)S(1)} collective-permute-done((f32[8,2,64,128]{3,2,1,0:T(8,128)S(1)}, f32[8,2,64,128]{3,2,1,0:T(8,128)S(1)}, u32[]{:S(2)}, u32[]{:S(2)}) %collective-permute-start.1) | collective-permute-done | bytes 524320 | tf_op jit(solution)/shard_map/ppermute | solution.py:216
  37.0 5.6 %collective-permute-done.l2 = f32[8,2,64,128]{3,2,1,0:T(8,128)S(1)} collective-permute-done((f32[8,2,64,128]{3,2,1,0:T(8,128)S(1)}, f32[8,2,64,128]{3,2,1,0:T(8,128)S(1)}, u32[]{:S(2)}, u32[]{:S(2)}) %collective-permute-start) | collective-permute-done | bytes 524320 | tf_op jit(solution)/shard_map/ppermute | solution.py:216
  42.6 34.3 %shard_map.18 = (f32[8,2,64,128]{3,2,1,0:T(8,128)S(1)}, f32[4,32,128]{2,1,0:T(8,128)S(1)}, f32[4,32,128]{2,1,0:T(8,128)S(1)}, f32[4,32,128]{2,1,0:T(8,128)S(1)}) custom-call(s32[2]{0:T(128)S(1)} %pad_add_fusion.place_ref, f32[8,2,64,128]{3,2,1,0:T(8,128)S(1)} %collective-permute-done.l2, f32[8,2,64,128]{3,2,1,0:T(8,128)S(1)} %collective-permute-done.1.l1, ...), custom_call_target="tpu_custom_call" | custom-call | tf_op jit(solution)/shard_map/pallas_call | solution.py:240
  76.9 0.7 collective-permute-start.6
  77.6 0.7 collective-permute-start.5
  78.2 0.7 collective-permute-start.4
  80.2 0.7 collective-permute-start.8
  80.9 0.7 collective-permute-start.7
  82.1 0.7 collective-permute-start.12
  83.5 0.7 collective-permute-start.10
  84.7 0.7 collective-permute-start.15
  85.4 0.7 collective-permute-start.14
  87.4 0.7 collective-permute-start.18
  88.0 0.7 collective-permute-start.17
  88.7 0.7 collective-permute-start.16
  90.0 0.7 collective-permute-start.21
  92.6 1.3 collective-permute-start.24
  93.9 1.3 collective-permute-start.23
  95.2 1.3 collective-permute-start.22
  96.5 43.2 %collective-permute-done.24.right = f32[4,32,128]{2,1,0:T(8,128)S(1)} collective-permute-done((f32[4,32,128]{2,1,0:T(8,128)S(1)}, f32[4,32,128]{2,1,0:T(8,128)S(1)}, u32[]{:S(2)}, u32[]{:S(2)}) %collective-permute-start.24) | collective-permute-done | bytes 65568 | tf_op jit(solution)/shard_map/ppermute | solution.py:222
  139.7 2.8 %collective-permute-done.23.mid = f32[4,32,128]{2,1,0:T(8,128)S(1)} collective-permute-done((f32[4,32,128]{2,1,0:T(8,128)S(1)}, f32[4,32,128]{2,1,0:T(8,128)S(1)}, u32[]{:S(2)}, u32[]{:S(2)}) %collective-permute-start.23) | collective-permute-done | bytes 65568 | tf_op jit(solution)/shard_map/ppermute | solution.py:222
  142.6 1.4 collective-permute-done.22.left
  144.0 1.6 %shard_map.25 = (f32[4,32,128]{2,1,0:T(8,128)S(1)}, f32[4,32,128]{2,1,0:T(8,128)}) custom-call(s32[2]{0:T(128)S(1)} %pad_add_fusion.place_ref, f32[4,32,128]{2,1,0:T(8,128)S(1)} %collective-permute-done.22.left, f32[4,32,128]{2,1,0:T(8,128)S(1)} %collective-permute-done.23.mid, f32[4,32,128]{2,1,0:T(8,128)S(1)} %collective-permute-done.24.right, ...), custom_call_target="tpu_custom_call" | custom-call | tf_op jit(solution)/shard_map/pallas_call | solution.py:257
  145.5 2.5 %shard_map.26 = f32[1,8,64,256]{3,2,1,0:T(8,128)} custom-call(f32[8,2,64,128]{3,2,1,0:T(8,128)S(1)} %get-tuple-element.22.fe_ref, f32[4,32,128]{2,1,0:T(8,128)S(1)} %get-tuple-element.23.picked_ref.co_ref, f32[4,32,128]{2,1,0:T(8,128)S(1)} %get-tuple-element.38.picked_ref), custom_call_target="tpu_custom_call" | custom-call | tf_op jit(solution)/shard_map/pallas_call | solution.py:265
  (31 shorter events, 6.8 us)
Async XLA Ops:
  0.0 1.0 copy-start
  2.8 18.0 %collective-permute-start.3 = (f32[8,2,64,128]{3,2,1,0:T(8,128)S(1)}, f32[8,2,64,128]{3,2,1,0:T(8,128)S(1)}, u32[]{:S(2)}, u32[]{:S(2)}) collective-permute-start(f32[8,2,64,128]{3,2,1,0:T(8,128)S(1)} %shard_map.17.own), channel_id=1, source_target_pairs={{2,0},{3,1},{4,2},{5,3},{6,4},{7,5},{8,6},{9,7},{10,8},{11,9},{12,... | collective-permute-start | bytes 1572872 | tf_op jit(solution)/shard_map/ppermute | solution.py:216
  10.2 22.2 %collective-permute-start.2 = (f32[8,2,64,128]{3,2,1,0:T(8,128)S(1)}, f32[8,2,64,128]{3,2,1,0:T(8,128)S(1)}, u32[]{:S(2)}, u32[]{:S(2)}) collective-permute-start(f32[8,2,64,128]{3,2,1,0:T(8,128)S(1)} %shard_map.17.own), channel_id=1, source_target_pairs={{1,0},{2,1},{3,2},{4,3},{5,4},{6,5},{7,6},{8,7},{9,8},{10,9},{11,1... | collective-permute-start | bytes 1572872 | tf_op jit(solution)/shard_map/ppermute | solution.py:216
  12.9 24.1 %collective-permute-start.1 = (f32[8,2,64,128]{3,2,1,0:T(8,128)S(1)}, f32[8,2,64,128]{3,2,1,0:T(8,128)S(1)}, u32[]{:S(2)}, u32[]{:S(2)}) collective-permute-start(f32[8,2,64,128]{3,2,1,0:T(8,128)S(1)} %shard_map.17.own), channel_id=1, source_target_pairs={{0,1},{1,2},{2,3},{3,4},{4,5},{5,6},{6,7},{7,8},{8,9},{9,10},{10,1... | collective-permute-start | bytes 1572872 | tf_op jit(solution)/shard_map/ppermute | solution.py:216
  15.5 27.1 %collective-permute-start = (f32[8,2,64,128]{3,2,1,0:T(8,128)S(1)}, f32[8,2,64,128]{3,2,1,0:T(8,128)S(1)}, u32[]{:S(2)}, u32[]{:S(2)}) collective-permute-start(f32[8,2,64,128]{3,2,1,0:T(8,128)S(1)} %shard_map.17.own), channel_id=1, source_target_pairs={{0,2},{1,3},{2,4},{3,5},{4,6},{5,7},{6,8},{7,9},{8,10},{9,11},{10,... | collective-permute-start | bytes 1572872 | tf_op jit(solution)/shard_map/ppermute | solution.py:216
  76.9 2.0 %collective-permute-start.6 = (f32[4,32,128]{2,1,0:T(8,128)S(1)}, f32[4,32,128]{2,1,0:T(8,128)S(1)}, u32[]{:S(2)}, u32[]{:S(2)}) collective-permute-start(f32[4,32,128]{2,1,0:T(8,128)S(1)} %get-tuple-element.24), channel_id=1, source_target_pairs={{1,32},{2,33},{3,34},{4,35},{5,36},{6,37},{7,38},{8,39},{9,40},{10... | collective-permute-start | bytes 196616 | tf_op jit(solution)/shard_map/ppermute | solution.py:222
  77.6 1.4 collective-permute-start.5
  78.2 0.7 collective-permute-start.4
  79.5 2.0 %collective-permute-start.9 = (f32[4,32,128]{2,1,0:T(8,128)S(1)}, f32[4,32,128]{2,1,0:T(8,128)S(1)}, u32[]{:S(2)}, u32[]{:S(2)}) collective-permute-start(f32[4,32,128]{2,1,0:T(8,128)S(1)} %get-tuple-element.26), channel_id=1, source_target_pairs={{33,64},{34,65},{35,66},{36,67},{37,68},{38,69},{39,70},{40,71},{4... | collective-permute-start | bytes 196616 | tf_op jit(solution)/shard_map/ppermute | solution.py:222
  80.2 1.4 collective-permute-start.8
  80.9 0.7 collective-permute-start.7
  82.1 2.0 %collective-permute-start.12 = (f32[4,32,128]{2,1,0:T(8,128)S(1)}, f32[4,32,128]{2,1,0:T(8,128)S(1)}, u32[]{:S(2)}, u32[]{:S(2)}) collective-permute-start(f32[4,32,128]{2,1,0:T(8,128)S(1)} %get-tuple-element.28), channel_id=1, source_target_pairs={{65,96},{66,97},{67,98},{68,99},{69,100},{70,101},{71,102},{72,103... | collective-permute-start | bytes 196616 | tf_op jit(solution)/shard_map/ppermute | solution.py:222
  82.8 1.4 collective-permute-start.11
  83.5 0.7 collective-permute-start.10
  84.7 2.0 %collective-permute-start.15 = (f32[4,32,128]{2,1,0:T(8,128)S(1)}, f32[4,32,128]{2,1,0:T(8,128)S(1)}, u32[]{:S(2)}, u32[]{:S(2)}) collective-permute-start(f32[4,32,128]{2,1,0:T(8,128)S(1)} %get-tuple-element.30), channel_id=1, source_target_pairs={{97,128},{98,129},{99,130},{100,131},{101,132},{102,133},{103,134}... | collective-permute-start | bytes 196616 | tf_op jit(solution)/shard_map/ppermute | solution.py:222
  85.4 1.4 collective-permute-start.14
  86.1 0.7 collective-permute-start.13
  87.4 2.0 %collective-permute-start.18 = (f32[4,32,128]{2,1,0:T(8,128)S(1)}, f32[4,32,128]{2,1,0:T(8,128)S(1)}, u32[]{:S(2)}, u32[]{:S(2)}) collective-permute-start(f32[4,32,128]{2,1,0:T(8,128)S(1)} %get-tuple-element.32), channel_id=1, source_target_pairs={{129,160},{130,161},{131,162},{132,163},{133,164},{134,165},{135,1... | collective-permute-start | bytes 196616 | tf_op jit(solution)/shard_map/ppermute | solution.py:222
  88.0 1.4 collective-permute-start.17
  88.7 0.7 collective-permute-start.16
  90.0 2.0 %collective-permute-start.21 = (f32[4,32,128]{2,1,0:T(8,128)S(1)}, f32[4,32,128]{2,1,0:T(8,128)S(1)}, u32[]{:S(2)}, u32[]{:S(2)}) collective-permute-start(f32[4,32,128]{2,1,0:T(8,128)S(1)} %get-tuple-element.34), channel_id=1, source_target_pairs={{161,192},{162,193},{163,194},{164,195},{165,196},{166,197},{167,1... | collective-permute-start | bytes 196616 | tf_op jit(solution)/shard_map/ppermute | solution.py:222
  90.6 1.4 collective-permute-start.20
  91.3 0.7 collective-permute-start.19
  92.6 47.1 %collective-permute-start.24 = (f32[4,32,128]{2,1,0:T(8,128)S(1)}, f32[4,32,128]{2,1,0:T(8,128)S(1)}, u32[]{:S(2)}, u32[]{:S(2)}) collective-permute-start(f32[4,32,128]{2,1,0:T(8,128)S(1)} %get-tuple-element.36), channel_id=1, source_target_pairs={{193,224},{194,225},{195,226},{196,227},{197,228},{198,229},{199,2... | collective-permute-start | bytes 196616 | tf_op jit(solution)/shard_map/ppermute | solution.py:222
  93.9 48.7 %collective-permute-start.23 = (f32[4,32,128]{2,1,0:T(8,128)S(1)}, f32[4,32,128]{2,1,0:T(8,128)S(1)}, u32[]{:S(2)}, u32[]{:S(2)}) collective-permute-start(f32[4,32,128]{2,1,0:T(8,128)S(1)} %get-tuple-element.36), channel_id=1, source_target_pairs={{192,224},{193,225},{194,226},{195,227},{196,228},{197,229},{198,2... | collective-permute-start | bytes 196616 | tf_op jit(solution)/shard_map/ppermute | solution.py:222
  95.2 48.8 %collective-permute-start.22 = (f32[4,32,128]{2,1,0:T(8,128)S(1)}, f32[4,32,128]{2,1,0:T(8,128)S(1)}, u32[]{:S(2)}, u32[]{:S(2)}) collective-permute-start(f32[4,32,128]{2,1,0:T(8,128)S(1)} %get-tuple-element.36), channel_id=1, source_target_pairs={{192,225},{193,226},{194,227},{195,228},{196,229},{197,230},{198,2... | collective-permute-start | bytes 196616 | tf_op jit(solution)/shard_map/ppermute | solution.py:222

commit v2 on v0

v2 whole, which is shorter than its diff:
```python
import functools
import math

import jax
import jax.numpy as jnp
from jax import lax
from jax.experimental import pallas as pl
from jax.experimental.pallas import tpu as pltpu
from jax.sharding import PartitionSpec as P

COARSE_STEPS = 2
FINE_STEPS = 8

fine_dt = 0.025
coarse_dt = 0.1
fine_coef = 4.8
coarse_coef = 1.2

KAPPA = math.sqrt(fine_dt)
FINE_A = 1.0 + fine_dt * (1.0 - 6.0 * fine_coef)
FINE_C = fine_dt * fine_coef
COARSE_A = 1.0 + coarse_dt * (1.0 - 6.0 * coarse_coef)
COARSE_B = coarse_dt / fine_dt
COARSE_C = coarse_dt * coarse_coef

CZ, NX, NY = 8, 64, 256
ROUNDS = 2
WIDE = 2 * FINE_STEPS // ROUNDS
CC, CX, CY = CZ // 2, NX // 2, NY // 2
REACH = 2 * COARSE_STEPS
VMEM_LIMIT = 40 * 1024 * 1024


def x_sum(a):
    n = a.shape[0]
    after = jnp.concatenate([a[8:], pltpu.roll(a[:8], 7, 0)], axis=0)
    before = jnp.concatenate([pltpu.roll(a[n - 8 :], 1, 0), a[: n - 8]], axis=0)
    return after + before


def split_dot(a, m):
    hi = a.astype(jnp.bfloat16)
    rest = a - hi.astype(jnp.float32)
    mid = rest.astype(jnp.bfloat16)
    low = (rest - mid.astype(jnp.float32)).astype(jnp.bfloat16)
    dot = functools.partial(jnp.dot, preferred_element_type=jnp.float32)
    return dot(hi, m) + (dot(mid, m) + dot(low, m))


def fine_euler(get, p, c):
    out = []
    for j, by in ((0, 1), (1, CY - 1)):
        a = get(p, j)
        b = get(p, 1 - j)
        total = (get(p - 1, j) + get(p + 1, j)) + (x_sum(a) + (b + pltpu.roll(b, by, 1)))
        out.append(c * total + a * (FINE_A - a * a))
    return out


def coarse_euler(get, p, c):
    a = get(p)
    total = (get(p - 1) + get(p + 1)) + (x_sum(a) + (pltpu.roll(a, 1, 1) + pltpu.roll(a, CY - 1, 1)))
    return c * total + a * (COARSE_A - COARSE_B * (a * a))


def inside(first, p, count, coef):
    g = first + p
    return jnp.where((g >= 0) & (g < count), coef, 0.0).astype(jnp.float32)


def coarse_propagate(get, v, v1, lo, hi, first, count):
    for step in range(COARSE_STEPS):
        lo, hi = lo + 1, hi - 1
        for p in range(lo, hi):
            v1[p] = coarse_euler(get, p, inside(first, p, count, COARSE_C))
        lo, hi = lo + 1, hi - 1
        for p in range(lo, hi):
            new = coarse_euler(lambda q: v1[q], p, inside(first, p, count, COARSE_C))
            v[p] = 0.5 * (get(p) + new)
        get = lambda q: v[q]


def restricted(get, p):
    s = (get(p, 0) + get(p + 1, 0)) + (get(p, 1) + get(p + 1, 1))
    rows = [s[16 * i : 16 * i + 8] + s[16 * i + 8 : 16 * i + 16] for i in range(4)]
    return 0.125 * jnp.concatenate(rows, axis=0)


def prep_kernel(x_ref, out_ref, x, sems):
    copies = [pltpu.make_async_copy(x_ref.at[0, p], x.at[p], sems.at[p]) for p in range(CZ)]
    for copy in copies:
        copy.start()
    y = lax.broadcasted_iota(jnp.int32, (NY, NY), 0)
    k = lax.broadcasted_iota(jnp.int32, (NY, NY), 1)
    m = (y == 2 * (k % CY) + k // CY).astype(jnp.float32).astype(jnp.bfloat16)
    for p in range(CZ):
        copies[p].wait()
        r = split_dot(x[p], m) * KAPPA
        for s in range(8):
            for j in range(2):
                out_ref[p, j, pl.ds(s, 8, stride=8), :] = r[8 * s : 8 * s + 8, j * CY : (j + 1) * CY]


def three(left, mid, right, n):
    def get(p, *rest):
        ref = (left, mid, right)[p // n]
        return ref[(p % n,) + rest]

    return get


def sides(place, n):
    at = jnp.where(place % 2 == 1, 2 * n, 0)
    return at, 2 * n - at


def fine_rounds(own, one, two, put, v, v1, place, blocks):
    for at, ref in zip(sides(place, CZ), (one, two)):
        for p in range(CZ):
            v[at + p] = ref[p]
    get = lambda q, j: own[q - CZ, j] if CZ <= q < 2 * CZ else v[q, j]
    first = place * CZ - WIDE
    n = CZ + 2 * WIDE
    for step in range(WIDE // 2):
        lo = 2 * step + 1
        for p in range(lo, n - lo):
            a, b = fine_euler(get, p, inside(first, p, blocks * CZ, FINE_C))
            v1[p, 0] = a
            v1[p, 1] = b
        for p in range(lo + 1, n - lo - 1):
            a, b = fine_euler(lambda q, j: v1[q, j], p, inside(first, p, blocks * CZ, FINE_C))
            a = 0.5 * (get(p, 0) + a)
            b = 0.5 * (get(p, 1) + b)
            if lo + 1 == WIDE:
                put(p - WIDE, a, b)
            else:
                v[p, 0] = a
                v[p, 1] = b
        get = lambda q, j: v[q, j]


def fine_kernel(blocks, place_ref, own, two, one, out_ref, v, v1):
    def put(p, a, b):
        out_ref[p, 0] = a
        out_ref[p, 1] = b

    fine_rounds(own, one, two, put, v, v1, place_ref[0], blocks)


def last_fine_kernel(blocks, place_ref, own, two, one, co_ref, out_ref, jump_ref, send_ref, v, v1):
    def put(p, a, b):
        out_ref[p, 0] = a
        out_ref[p, 1] = b

    fine_rounds(own, one, two, put, v, v1, place_ref[0], blocks)
    for q in range(CC):
        old = co_ref[q]
        jump = restricted(lambda p, j: out_ref[p, j], 2 * q) - old
        jump_ref[q] = jump
        send_ref[q] = jnp.where(place_ref[1] == 0, old + jump, jump)


def coarse_kernel(blocks, place_ref, own, two, one, co_ref, cv, cv1):
    at, then = sides(place_ref[0], CC)
    for ref, base in ((own, CC), (one, at), (two, then)):
        for q in range(CC):
            cv[base + q] = restricted(lambda p, j: ref[p, j], 2 * q)
    first = (place_ref[0] - 1) * CC
    coarse_propagate(lambda q: cv[q], cv, cv1, 0, 3 * CC, first, blocks * CC)
    for q in range(CC):
        co_ref[q] = cv[CC + q]


def first_sweep_kernel(blocks, place_ref, left, mid, right, jump_ref, old_ref, out_ref, send_ref, cv, cv1):
    @pl.when(place_ref[1] == 1)
    def _():
        first = (place_ref[0] - 1) * CC
        coarse_propagate(three(left, mid, right, CC), cv, cv1, 0, 3 * CC, first, blocks * CC)
        for q in range(CC):
            new = cv[CC + q]
            out_ref[q] = new
            send_ref[q] = new + jump_ref[q]

    @pl.when(place_ref[1] != 1)
    def _():
        out_ref[...] = old_ref[...]
        send_ref[...] = jump_ref[...]


def sweep_kernel(
    blocks, slab, place_ref, a0, a1, a2, a3, a4, j0, j1, j2, jump_ref, old_ref, oldx_ref,
    out_ref, outx_ref, send_ref, cv, cv1,
):
    @pl.when(place_ref[1] == slab)
    def _():
        refs = (a0, a1, a2, a3, a4)
        first = (place_ref[0] - 2) * CC
        get = lambda p: refs[p // CC][p % CC]
        coarse_propagate(get, cv, cv1, 0, 5 * CC, first, blocks * CC)
        for q in range(CC):
            outx_ref[q] = cv[2 * CC + q]
        wide = three(j0, j1, j2, CC)
        for q in range(CC, 4 * CC):
            cv[q] = cv[q] + wide(q - CC)
        coarse_propagate(lambda q: cv[q], cv, cv1, CC, 4 * CC, first, blocks * CC)
        for q in range(CC):
            new = cv[2 * CC + q]
            out_ref[q] = new
            send_ref[q] = new + jump_ref[q]

    @pl.when(place_ref[1] != slab)
    def _():
        out_ref[...] = old_ref[...]
        outx_ref[...] = oldx_ref[...]
        send_ref[...] = jump_ref[...]


def interleave():
    k = lax.broadcasted_iota(jnp.int32, (NY, NY), 0)
    y = lax.broadcasted_iota(jnp.int32, (NY, NY), 1)
    return (y == 2 * (k % CY) + k // CY).astype(jnp.float32).astype(jnp.bfloat16)


def spread(a):
    return jnp.concatenate([a[8 * (i // 2) : 8 * (i // 2) + 8] for i in range(8)], axis=0)


def rest_kernel(fe_ref, co_ref, out_ref):
    m = interleave()
    for p in range(CZ):
        old = spread(co_ref[p // 2])
        r = jnp.concatenate([fe_ref[p, j] - old for j in range(2)], axis=1)
        r = split_dot(r, m) * (1.0 / KAPPA)
        for h in range(2):
            for i in range(8):
                out_ref[h, p, pl.ds(i, 8, stride=8), :] = r[8 * i : 8 * i + 8, h * CY : (h + 1) * CY]


def final_kernel(place_ref, rest_ref, picked_ref, even_ref, out_ref, x, sems):
    slab = place_ref[1]
    use_even = (slab % 2 == 0) & (slab > 0)
    k = lax.broadcasted_iota(jnp.int32, (CY, NY), 0)
    y = lax.broadcasted_iota(jnp.int32, (CY, NY), 1)
    m = (k == y // 2).astype(jnp.float32).astype(jnp.bfloat16)
    copies = []
    for q in range(CC):
        new = jnp.where(use_even, even_ref[q], picked_ref[q])
        r = split_dot(new, m) * (1.0 / KAPPA)
        for p in (2 * q, 2 * q + 1):
            for h in range(2):
                for i in range(8):
                    at = (h, p, pl.ds(i, 8, stride=8), slice(None))
                    c = 8 * (i // 2)
                    x[at] = rest_ref[at] + r[c : c + 8, h * CY : (h + 1) * CY]
                dst = out_ref.at[0, p, :, pl.ds(h * CY, CY)]
                copies.append(pltpu.make_async_copy(x.at[h, p], dst, sems.at[p, h]))
                copies[-1].start()
    for copy in copies:
        copy.wait()


VM = pl.BlockSpec(memory_space=pltpu.VMEM)
SM = pl.BlockSpec(memory_space=pltpu.SMEM)
HB = pl.BlockSpec(memory_space=pltpu.HBM)
PARAMS = pltpu.CompilerParams(vmem_limit_bytes=VMEM_LIMIT)
fine_shape = jax.ShapeDtypeStruct((CZ, 2, NX, CY), jnp.float32)
half_shape = jax.ShapeDtypeStruct((2, CZ, NX, CY), jnp.float32)
coarse_shape = jax.ShapeDtypeStruct((CC, CX, CY), jnp.float32)
WHOLE = [pltpu.VMEM((CZ, NX, NY), jnp.float32), pltpu.SemaphoreType.DMA((CZ,))]
HALVES = [pltpu.VMEM((2, CZ, NX, CY), jnp.float32), pltpu.SemaphoreType.DMA((CZ, 2))]
FINE_WORK = [pltpu.VMEM((CZ + 2 * WIDE, 2, NX, CY), jnp.float32)] * 2


def coarse_work(n):
    return [pltpu.VMEM((n * CC, CX, CY), jnp.float32)] * 2


def call(kernel, out_shape, in_specs, args, scratch=(), out_specs=None):
    if out_specs is None:
        out_specs = (VM,) * len(out_shape) if isinstance(out_shape, tuple) else VM
    return pl.pallas_call(
        kernel,
        out_shape=out_shape,
        in_specs=in_specs,
        out_specs=out_specs,
        scratch_shapes=list(scratch),
        compiler_params=PARAMS,
    )(*args)


def both(array):
    count = lax.axis_size("gz")
    pairs = [[(i, i + 1) for i in range(edge, count - 1, 2)] for edge in (1, 0)]
    one, two = (lax.ppermute(array, "gz", p + [(j, i) for i, j in p]) for p in pairs)
    return two, one


def handed(array, slabs, by=0):
    count = lax.axis_size("gz")
    pairs = [(a * count + i, b * count + i + by) for a, b in slabs for i in range(count) if 0 <= i + by < count]
    return lax.ppermute(array, ("tm", "gz"), pairs)


def per_device(start_states):
    blocks = lax.axis_size("gz")
    slabs = lax.axis_size("tm")
    place = jnp.stack([lax.axis_index("gz"), lax.axis_index("tm")]).astype(jnp.int32)
    start_states = pltpu.with_memory_space_constraint(start_states, pltpu.HBM)
    own = call(prep_kernel, fine_shape, [HB], (start_states,), WHOLE)
    near = (place, own, *both(own))
    own = call(functools.partial(fine_kernel, blocks), fine_shape, [SM] + [VM] * 3, near, FINE_WORK)
    two, one = both(own)
    old = call(functools.partial(coarse_kernel, blocks), coarse_shape, [SM] + [VM] * 3, near, coarse_work(3))
    fine_end, jump, send = call(
        functools.partial(last_fine_kernel, blocks),
        (fine_shape, coarse_shape, coarse_shape),
        [SM] + [VM] * 4,
        (place, own, two, one, old),
        FINE_WORK,
    )
    firsts = range(0, slabs - 1, 2)
    side = [handed(send, [(k, k + 1) for k in firsts], by) for by in (1, 0, -1)]
    picked, send = call(
        functools.partial(first_sweep_kernel, blocks),
        (coarse_shape,) * 2,
        [SM] + [VM] * 5,
        (place, *side, jump, old),
        coarse_work(3),
    )
    rest = call(rest_kernel, half_shape, [VM] * 2, (fine_end, old))
    even = jump
    for k in firsts[1:]:
        got = [handed(send, [(k - 1, k + 1)], by) for by in (2, 1, 0, -1, -2)]
        picked, even, send = call(
            functools.partial(sweep_kernel, blocks, k + 1),
            (coarse_shape,) * 3,
            [SM] + [VM] * 11,
            (place, *got, *side, jump, picked, even),
            coarse_work(5),
        )
    even = handed(even, [(k + 1, k) for k in firsts[1:]])
    return call(
        final_kernel,
        jax.ShapeDtypeStruct((1, CZ, NX, NY), jnp.float32),
        [SM] + [VM] * 3,
        (place, rest, picked, even),
        HALVES,
        HB,
    )


def solution(mesh):
    placed = (P("tm", "gz", None, None),)
    return jax.shard_map(
        per_device, mesh=mesh, in_specs=placed, out_specs=P("tm", "gz", None, None), check_vma=False
    )
```

time: 666 us -> 107 us (0.16)
  the two profiles are of different devices: /device:TPU:158 before, /device:TPU:227 now
where the time goes in v2:
time: 107 us
  waiting for transfers between devices  60.9 us (57%)
  starting transfers between devices  27.3 us (26%)
  Pallas kernels  17.7 us (17%)
    ppermute x19, waiting for transfers between devices, handed(): return lax.ppermute(array, ('tm', 'gz'), pairs)  37.9 us
    ppermute x4, waiting for transfers between devices, both(): lax.ppermute(array, 'gz', p + [(j, i) for i, j in p])  23 us
    ppermute x19, starting transfers between devices, handed(): return lax.ppermute(array, ('tm', 'gz'), pairs)  18.3 us
    pallas_call x10, Pallas kernels, call(): pl.pallas_call(kernel, out_shape=out_shape, in_specs=in_specs, out_specs=...  17.7 us
    ppermute x4, starting transfers between devices, both(): lax.ppermute(array, 'gz', p + [(j, i) for i, j in p])  9.03 us
  transfers between devices with their start and end apart: 23, of which 12 were waited for; matrix products, arithmetic and copies ran while one was open for 0% of the time, Pallas kernels for 2%

profile of v2, /device:TPU:227, one launch (start us, length us, event | category | flops | bytes accessed | tf_op | source)
XLA Modules:
  0.0 106.5 jit_solution(1246831481028185651)
XLA Ops:
  0.0 2.8 %shard_map.17.own = f32[8,2,64,128]{3,2,1,0:T(8,128)S(1)} custom-call(f32[1,8,64,256]{3,2,1,0:T(8,128)} %x_ref.1), custom_call_target="tpu_custom_call" | custom-call | tf_op jit(solution)/shard_map/pallas_call | solution.py:281
  2.8 4.6 %collective-permute-start.1 = (f32[8,2,64,128]{3,2,1,0:T(8,128)S(1)}, f32[8,2,64,128]{3,2,1,0:T(8,128)S(1)}, u32[]{:S(2)}, u32[]{:S(2)}) collective-permute-start(f32[8,2,64,128]{3,2,1,0:T(8,128)S(1)} %shard_map.17.own), channel_id=1, source_target_pairs={{1,2},{3,4},{5,6},{7,8},{9,10},{11,12},{13,14},{15,16},{17,18},{19... | collective-permute-start | bytes 1572872 | tf_op jit(solution)/shard_map/ppermute | solution.py:294
  7.6 12.0 %collective-permute-done.1.one = f32[8,2,64,128]{3,2,1,0:T(8,128)S(1)} collective-permute-done((f32[8,2,64,128]{3,2,1,0:T(8,128)S(1)}, f32[8,2,64,128]{3,2,1,0:T(8,128)S(1)}, u32[]{:S(2)}, u32[]{:S(2)}) %collective-permute-start.1) | collective-permute-done | bytes 524320 | tf_op jit(solution)/shard_map/ppermute | solution.py:294
  20.0 3.7 %shard_map.18.own = f32[8,2,64,128]{3,2,1,0:T(8,128)S(1)} custom-call(s32[2]{0:T(128)S(1)} %pad_add_fusion.place_ref, f32[8,2,64,128]{3,2,1,0:T(8,128)S(1)} %shard_map.17.own, f32[8,2,64,128]{3,2,1,0:T(8,128)S(1)} %collective-permute-done.two, f32[8,2,64,128]{3,2,1,0:T(8,128)S(1)} %collective-permute-done.1.one), custom_call_target="tpu_custom_call" | custom-call | tf_op jit(solution)/shard_map/pallas_call | solution.py:281
  23.7 4.2 %collective-permute-start.3 = (f32[8,2,64,128]{3,2,1,0:T(8,128)S(1)}, f32[8,2,64,128]{3,2,1,0:T(8,128)S(1)}, u32[]{:S(2)}, u32[]{:S(2)}) collective-permute-start(f32[8,2,64,128]{3,2,1,0:T(8,128)S(1)} %shard_map.18.own), channel_id=1, source_target_pairs={{1,2},{3,4},{5,6},{7,8},{9,10},{11,12},{13,14},{15,16},{17,18},{19... | collective-permute-start | bytes 1572872 | tf_op jit(solution)/shard_map/ppermute | solution.py:294
  28.1 0.9 shard_map.19.co_ref.old_ref
  29.0 10.3 %collective-permute-done.3.one = f32[8,2,64,128]{3,2,1,0:T(8,128)S(1)} collective-permute-done((f32[8,2,64,128]{3,2,1,0:T(8,128)S(1)}, f32[8,2,64,128]{3,2,1,0:T(8,128)S(1)}, u32[]{:S(2)}, u32[]{:S(2)}) %collective-permute-start.3) | collective-permute-done | bytes 524320 | tf_op jit(solution)/shard_map/ppermute | solution.py:294
  39.6 3.8 %shard_map.20 = (f32[8,2,64,128]{3,2,1,0:T(8,128)S(1)}, f32[4,32,128]{2,1,0:T(8,128)S(1)}, f32[4,32,128]{2,1,0:T(8,128)S(1)}) custom-call(s32[2]{0:T(128)S(1)} %pad_add_fusion.place_ref, f32[8,2,64,128]{3,2,1,0:T(8,128)S(1)} %shard_map.18.own, f32[8,2,64,128]{3,2,1,0:T(8,128)S(1)} %collective-permute-done.2.two, ...), custom_call_target="tpu_custom_call" | custom-call | tf_op jit(solution)/shard_map/pallas_call | solution.py:281
  43.5 1.3 %collective-permute-start.6 = (f32[4,32,128]{2,1,0:T(8,128)S(1)}, f32[4,32,128]{2,1,0:T(8,128)S(1)}, u32[]{:S(2)}, u32[]{:S(2)}) collective-permute-start(f32[4,32,128]{2,1,0:T(8,128)S(1)} %get-tuple-element.19), channel_id=1, source_target_pairs={{1,32},{2,33},{3,34},{4,35},{5,36},{6,37},{7,38},{8,39},{9,40},{10... | collective-permute-start | bytes 196616 | tf_op jit(solution)/shard_map/ppermute | solution.py:301
  44.8 1.3 %collective-permute-start.5 = (f32[4,32,128]{2,1,0:T(8,128)S(1)}, f32[4,32,128]{2,1,0:T(8,128)S(1)}, u32[]{:S(2)}, u32[]{:S(2)}) collective-permute-start(f32[4,32,128]{2,1,0:T(8,128)S(1)} %get-tuple-element.19), channel_id=1, source_target_pairs={{0,32},{1,33},{2,34},{3,35},{4,36},{5,37},{6,38},{7,39},{8,40},{9,... | collective-permute-start | bytes 196616 | tf_op jit(solution)/shard_map/ppermute | solution.py:301
  46.1 1.3 %collective-permute-start.4 = (f32[4,32,128]{2,1,0:T(8,128)S(1)}, f32[4,32,128]{2,1,0:T(8,128)S(1)}, u32[]{:S(2)}, u32[]{:S(2)}) collective-permute-start(f32[4,32,128]{2,1,0:T(8,128)S(1)} %get-tuple-element.19), channel_id=1, source_target_pairs={{0,33},{1,34},{2,35},{3,36},{4,37},{5,38},{6,39},{7,40},{8,41},{9,... | collective-permute-start | bytes 196616 | tf_op jit(solution)/shard_map/ppermute | solution.py:301
  47.4 2.0 %collective-permute-done.6.right.j2 = f32[4,32,128]{2,1,0:T(8,128)S(1)} collective-permute-done((f32[4,32,128]{2,1,0:T(8,128)S(1)}, f32[4,32,128]{2,1,0:T(8,128)S(1)}, u32[]{:S(2)}, u32[]{:S(2)}) %collective-permute-start.6) | collective-permute-done | bytes 65568 | tf_op jit(solution)/shard_map/ppermute | solution.py:301
  49.3 0.8 collective-permute-done.5.mid.j1
  50.1 3.8 %collective-permute-done.4.left.j0 = f32[4,32,128]{2,1,0:T(8,128)S(1)} collective-permute-done((f32[4,32,128]{2,1,0:T(8,128)S(1)}, f32[4,32,128]{2,1,0:T(8,128)S(1)}, u32[]{:S(2)}, u32[]{:S(2)}) %collective-permute-start.4) | collective-permute-done | bytes 65568 | tf_op jit(solution)/shard_map/ppermute | solution.py:301
  54.5 0.7 collective-permute-start.11
  55.2 0.7 collective-permute-start.10
  56.5 0.7 collective-permute-start.8
  57.2 0.7 collective-permute-start.7
  58.5 0.7 collective-permute-start.16
  61.9 0.7 shard_map.24
  62.7 1.3 %collective-permute-start.21 = (f32[4,32,128]{2,1,0:T(8,128)S(1)}, f32[4,32,128]{2,1,0:T(8,128)S(1)}, u32[]{:S(2)}, u32[]{:S(2)}) collective-permute-start(f32[4,32,128]{2,1,0:T(8,128)S(1)} %get-tuple-element.26), channel_id=1, source_target_pairs={{162,224},{163,225},{164,226},{165,227},{166,228},{167,229},{168,2... | collective-permute-start | bytes 196616 | tf_op jit(solution)/shard_map/ppermute | solution.py:301
  64.0 1.3 %collective-permute-start.20 = (f32[4,32,128]{2,1,0:T(8,128)S(1)}, f32[4,32,128]{2,1,0:T(8,128)S(1)}, u32[]{:S(2)}, u32[]{:S(2)}) collective-permute-start(f32[4,32,128]{2,1,0:T(8,128)S(1)} %get-tuple-element.26), channel_id=1, source_target_pairs={{161,224},{162,225},{163,226},{164,227},{165,228},{166,229},{167,2... | collective-permute-start | bytes 196616 | tf_op jit(solution)/shard_map/ppermute | solution.py:301
  65.3 1.3 %collective-permute-start.19 = (f32[4,32,128]{2,1,0:T(8,128)S(1)}, f32[4,32,128]{2,1,0:T(8,128)S(1)}, u32[]{:S(2)}, u32[]{:S(2)}) collective-permute-start(f32[4,32,128]{2,1,0:T(8,128)S(1)} %get-tuple-element.26), channel_id=1, source_target_pairs={{160,224},{161,225},{162,226},{163,227},{164,228},{165,229},{166,2... | collective-permute-start | bytes 196616 | tf_op jit(solution)/shard_map/ppermute | solution.py:301
  66.6 1.3 %collective-permute-start.18 = (f32[4,32,128]{2,1,0:T(8,128)S(1)}, f32[4,32,128]{2,1,0:T(8,128)S(1)}, u32[]{:S(2)}, u32[]{:S(2)}) collective-permute-start(f32[4,32,128]{2,1,0:T(8,128)S(1)} %get-tuple-element.26), channel_id=1, source_target_pairs={{160,225},{161,226},{162,227},{163,228},{164,229},{165,230},{166,2... | collective-permute-start | bytes 196616 | tf_op jit(solution)/shard_map/ppermute | solution.py:301
  67.9 1.3 %collective-permute-start.17 = (f32[4,32,128]{2,1,0:T(8,128)S(1)}, f32[4,32,128]{2,1,0:T(8,128)S(1)}, u32[]{:S(2)}, u32[]{:S(2)}) collective-permute-start(f32[4,32,128]{2,1,0:T(8,128)S(1)} %get-tuple-element.26), channel_id=1, source_target_pairs={{160,226},{161,227},{162,228},{163,229},{164,230},{165,231},{166,2... | collective-permute-start | bytes 196616 | tf_op jit(solution)/shard_map/ppermute | solution.py:301
  69.2 23.4 %collective-permute-done.21.a4 = f32[4,32,128]{2,1,0:T(8,128)S(1)} collective-permute-done((f32[4,32,128]{2,1,0:T(8,128)S(1)}, f32[4,32,128]{2,1,0:T(8,128)S(1)}, u32[]{:S(2)}, u32[]{:S(2)}) %collective-permute-start.21) | collective-permute-done | bytes 65568 | tf_op jit(solution)/shard_map/ppermute | solution.py:301
  92.8 5.9 %collective-permute-done.18.a1 = f32[4,32,128]{2,1,0:T(8,128)S(1)} collective-permute-done((f32[4,32,128]{2,1,0:T(8,128)S(1)}, f32[4,32,128]{2,1,0:T(8,128)S(1)}, u32[]{:S(2)}, u32[]{:S(2)}) %collective-permute-start.18) | collective-permute-done | bytes 65568 | tf_op jit(solution)/shard_map/ppermute | solution.py:301
  98.7 1.7 %collective-permute-done.17.a0 = f32[4,32,128]{2,1,0:T(8,128)S(1)} collective-permute-done((f32[4,32,128]{2,1,0:T(8,128)S(1)}, f32[4,32,128]{2,1,0:T(8,128)S(1)}, u32[]{:S(2)}, u32[]{:S(2)}) %collective-permute-start.17) | collective-permute-done | bytes 65568 | tf_op jit(solution)/shard_map/ppermute | solution.py:301
  100.4 2.1 %shard_map.25 = (f32[4,32,128]{2,1,0:T(8,128)S(1)}, f32[4,32,128]{2,1,0:T(8,128)S(1)}, f32[4,32,128]{2,1,0:T(8,128)}) custom-call(s32[2]{0:T(128)S(1)} %pad_add_fusion.place_ref, f32[4,32,128]{2,1,0:T(8,128)S(1)} %collective-permute-done.17.a0, f32[4,32,128]{2,1,0:T(8,128)S(1)} %collective-permute-done.18.a1, f32[4,32,128]{2,1,0:T(8,128)S(1)} %collective-permute-done.19.a2, ...), custom_call_target="tpu_custom_call" | custom-call | tf_op jit(solution)/shard_map/pallas_call | solution.py:281
  102.5 1.3 %collective-permute-start.22 = (f32[4,32,128]{2,1,0:T(8,128)S(1)}, f32[4,32,128]{2,1,0:T(8,128)S(1)}, u32[]{:S(2)}, u32[]{:S(2)}) collective-permute-start(f32[4,32,128]{2,1,0:T(8,128)S(1)} %get-tuple-element.30), channel_id=1, source_target_pairs={{96,64},{97,65},{98,66},{99,67},{100,68},{101,69},{102,70},{103,71... | collective-permute-start | bytes 196616 | tf_op jit(solution)/shard_map/ppermute | solution.py:301
  103.8 0.7 shard_map.21.rest_ref
  104.7 1.7 %shard_map.26 = f32[1,8,64,256]{3,2,1,0:T(8,128)} custom-call(s32[2]{0:T(128)S(1)} %pad_add_fusion.place_ref, f32[2,8,64,128]{3,2,1,0:T(8,128)S(1)} %shard_map.21.rest_ref, f32[4,32,128]{2,1,0:T(8,128)S(1)} %get-tuple-element.29.picked_ref, f32[4,32,128]{2,1,0:T(8,128)S(1)} %collective-permute-done.22.even_ref), custom_call_target="tpu_custom_call" | custom-call | tf_op jit(solution)/shard_map/pallas_call | solution.py:281
  (25 shorter events, 5.9 us)
Async XLA Ops:
  2.8 16.8 %collective-permute-start.1 = (f32[8,2,64,128]{3,2,1,0:T(8,128)S(1)}, f32[8,2,64,128]{3,2,1,0:T(8,128)S(1)}, u32[]{:S(2)}, u32[]{:S(2)}) collective-permute-start(f32[8,2,64,128]{3,2,1,0:T(8,128)S(1)} %shard_map.17.own), channel_id=1, source_target_pairs={{1,2},{3,4},{5,6},{7,8},{9,10},{11,12},{13,14},{15,16},{17,18},{19... | collective-permute-start | bytes 1572872 | tf_op jit(solution)/shard_map/ppermute | solution.py:294
  7.4 12.6 %collective-permute-start = (f32[8,2,64,128]{3,2,1,0:T(8,128)S(1)}, f32[8,2,64,128]{3,2,1,0:T(8,128)S(1)}, u32[]{:S(2)}, u32[]{:S(2)}) collective-permute-start(f32[8,2,64,128]{3,2,1,0:T(8,128)S(1)} %shard_map.17.own), channel_id=1, source_target_pairs={{0,1},{2,3},{4,5},{6,7},{8,9},{10,11},{12,13},{14,15},{16,17},{18,... | collective-permute-start | bytes 1572872 | tf_op jit(solution)/shard_map/ppermute | solution.py:294
  23.7 15.6 %collective-permute-start.3 = (f32[8,2,64,128]{3,2,1,0:T(8,128)S(1)}, f32[8,2,64,128]{3,2,1,0:T(8,128)S(1)}, u32[]{:S(2)}, u32[]{:S(2)}) collective-permute-start(f32[8,2,64,128]{3,2,1,0:T(8,128)S(1)} %shard_map.18.own), channel_id=1, source_target_pairs={{1,2},{3,4},{5,6},{7,8},{9,10},{11,12},{13,14},{15,16},{17,18},{19... | collective-permute-start | bytes 1572872 | tf_op jit(solution)/shard_map/ppermute | solution.py:294
  28.0 11.7 %collective-permute-start.2 = (f32[8,2,64,128]{3,2,1,0:T(8,128)S(1)}, f32[8,2,64,128]{3,2,1,0:T(8,128)S(1)}, u32[]{:S(2)}, u32[]{:S(2)}) collective-permute-start(f32[8,2,64,128]{3,2,1,0:T(8,128)S(1)} %shard_map.18.own), channel_id=1, source_target_pairs={{0,1},{2,3},{4,5},{6,7},{8,9},{10,11},{12,13},{14,15},{16,17},{18,... | collective-permute-start | bytes 1572872 | tf_op jit(solution)/shard_map/ppermute | solution.py:294
  43.5 5.9 %collective-permute-start.6 = (f32[4,32,128]{2,1,0:T(8,128)S(1)}, f32[4,32,128]{2,1,0:T(8,128)S(1)}, u32[]{:S(2)}, u32[]{:S(2)}) collective-permute-start(f32[4,32,128]{2,1,0:T(8,128)S(1)} %get-tuple-element.19), channel_id=1, source_target_pairs={{1,32},{2,33},{3,34},{4,35},{5,36},{6,37},{7,38},{8,39},{9,40},{10... | collective-permute-start | bytes 196616 | tf_op jit(solution)/shard_map/ppermute | solution.py:301
  44.8 5.3 %collective-permute-start.5 = (f32[4,32,128]{2,1,0:T(8,128)S(1)}, f32[4,32,128]{2,1,0:T(8,128)S(1)}, u32[]{:S(2)}, u32[]{:S(2)}) collective-permute-start(f32[4,32,128]{2,1,0:T(8,128)S(1)} %get-tuple-element.19), channel_id=1, source_target_pairs={{0,32},{1,33},{2,34},{3,35},{4,36},{5,37},{6,38},{7,39},{8,40},{9,... | collective-permute-start | bytes 196616 | tf_op jit(solution)/shard_map/ppermute | solution.py:301
  46.1 7.9 %collective-permute-start.4 = (f32[4,32,128]{2,1,0:T(8,128)S(1)}, f32[4,32,128]{2,1,0:T(8,128)S(1)}, u32[]{:S(2)}, u32[]{:S(2)}) collective-permute-start(f32[4,32,128]{2,1,0:T(8,128)S(1)} %get-tuple-element.19), channel_id=1, source_target_pairs={{0,33},{1,34},{2,35},{3,36},{4,37},{5,38},{6,39},{7,40},{8,41},{9,... | collective-permute-start | bytes 196616 | tf_op jit(solution)/shard_map/ppermute | solution.py:301
  54.5 3.4 %collective-permute-start.11 = (f32[4,32,128]{2,1,0:T(8,128)S(1)}, f32[4,32,128]{2,1,0:T(8,128)S(1)}, u32[]{:S(2)}, u32[]{:S(2)}) collective-permute-start(f32[4,32,128]{2,1,0:T(8,128)S(1)} %get-tuple-element.21), channel_id=1, source_target_pairs={{34,96},{35,97},{36,98},{37,99},{38,100},{39,101},{40,102},{41,103... | collective-permute-start | bytes 196616 | tf_op jit(solution)/shard_map/ppermute | solution.py:301
  55.2 2.7 %collective-permute-start.10 = (f32[4,32,128]{2,1,0:T(8,128)S(1)}, f32[4,32,128]{2,1,0:T(8,128)S(1)}, u32[]{:S(2)}, u32[]{:S(2)}) collective-permute-start(f32[4,32,128]{2,1,0:T(8,128)S(1)} %get-tuple-element.21), channel_id=1, source_target_pairs={{33,96},{34,97},{35,98},{36,99},{37,100},{38,101},{39,102},{40,103... | collective-permute-start | bytes 196616 | tf_op jit(solution)/shard_map/ppermute | solution.py:301
  55.9 2.0 %collective-permute-start.9 = (f32[4,32,128]{2,1,0:T(8,128)S(1)}, f32[4,32,128]{2,1,0:T(8,128)S(1)}, u32[]{:S(2)}, u32[]{:S(2)}) collective-permute-start(f32[4,32,128]{2,1,0:T(8,128)S(1)} %get-tuple-element.21), channel_id=1, source_target_pairs={{32,96},{33,97},{34,98},{35,99},{36,100},{37,101},{38,102},{39,103... | collective-permute-start | bytes 196616 | tf_op jit(solution)/shard_map/ppermute | solution.py:301
  56.5 1.4 %collective-permute-start.8 = (f32[4,32,128]{2,1,0:T(8,128)S(1)}, f32[4,32,128]{2,1,0:T(8,128)S(1)}, u32[]{:S(2)}, u32[]{:S(2)}) collective-permute-start(f32[4,32,128]{2,1,0:T(8,128)S(1)} %get-tuple-element.21), channel_id=1, source_target_pairs={{32,97},{33,98},{34,99},{35,100},{36,101},{37,102},{38,103},{39,10... | collective-permute-start | bytes 196616 | tf_op jit(solution)/shard_map/ppermute | solution.py:301
  57.2 0.7 collective-permute-start.7
  58.5 3.4 %collective-permute-start.16 = (f32[4,32,128]{2,1,0:T(8,128)S(1)}, f32[4,32,128]{2,1,0:T(8,128)S(1)}, u32[]{:S(2)}, u32[]{:S(2)}) collective-permute-start(f32[4,32,128]{2,1,0:T(8,128)S(1)} %get-tuple-element.23), channel_id=1, source_target_pairs={{98,160},{99,161},{100,162},{101,163},{102,164},{103,165},{104,166... | collective-permute-start | bytes 196616 | tf_op jit(solution)/shard_map/ppermute | solution.py:301
  59.2 2.7 %collective-permute-start.15 = (f32[4,32,128]{2,1,0:T(8,128)S(1)}, f32[4,32,128]{2,1,0:T(8,128)S(1)}, u32[]{:S(2)}, u32[]{:S(2)}) collective-permute-start(f32[4,32,128]{2,1,0:T(8,128)S(1)} %get-tuple-element.23), channel_id=1, source_target_pairs={{97,160},{98,161},{99,162},{100,163},{101,164},{102,165},{103,166}... | collective-permute-start | bytes 196616 | tf_op jit(solution)/shard_map/ppermute | solution.py:301
  59.9 2.0 %collective-permute-start.14 = (f32[4,32,128]{2,1,0:T(8,128)S(1)}, f32[4,32,128]{2,1,0:T(8,128)S(1)}, u32[]{:S(2)}, u32[]{:S(2)}) collective-permute-start(f32[4,32,128]{2,1,0:T(8,128)S(1)} %get-tuple-element.23), channel_id=1, source_target_pairs={{96,160},{97,161},{98,162},{99,163},{100,164},{101,165},{102,166},... | collective-permute-start | bytes 196616 | tf_op jit(solution)/shard_map/ppermute | solution.py:301
  60.5 1.4 %collective-permute-start.13 = (f32[4,32,128]{2,1,0:T(8,128)S(1)}, f32[4,32,128]{2,1,0:T(8,128)S(1)}, u32[]{:S(2)}, u32[]{:S(2)}) collective-permute-start(f32[4,32,128]{2,1,0:T(8,128)S(1)} %get-tuple-element.23), channel_id=1, source_target_pairs={{96,161},{97,162},{98,163},{99,164},{100,165},{101,166},{102,167},... | collective-permute-start | bytes 196616 | tf_op jit(solution)/shard_map/ppermute | solution.py:301
  61.2 0.7 collective-permute-start.12
  62.7 29.9 %collective-permute-start.21 = (f32[4,32,128]{2,1,0:T(8,128)S(1)}, f32[4,32,128]{2,1,0:T(8,128)S(1)}, u32[]{:S(2)}, u32[]{:S(2)}) collective-permute-start(f32[4,32,128]{2,1,0:T(8,128)S(1)} %get-tuple-element.26), channel_id=1, source_target_pairs={{162,224},{163,225},{164,226},{165,227},{166,228},{167,229},{168,2... | collective-permute-start | bytes 196616 | tf_op jit(solution)/shard_map/ppermute | solution.py:301
  64.0 28.6 %collective-permute-start.20 = (f32[4,32,128]{2,1,0:T(8,128)S(1)}, f32[4,32,128]{2,1,0:T(8,128)S(1)}, u32[]{:S(2)}, u32[]{:S(2)}) collective-permute-start(f32[4,32,128]{2,1,0:T(8,128)S(1)} %get-tuple-element.26), channel_id=1, source_target_pairs={{161,224},{162,225},{163,226},{164,227},{165,228},{166,229},{167,2... | collective-permute-start | bytes 196616 | tf_op jit(solution)/shard_map/ppermute | solution.py:301
  65.3 27.6 %collective-permute-start.19 = (f32[4,32,128]{2,1,0:T(8,128)S(1)}, f32[4,32,128]{2,1,0:T(8,128)S(1)}, u32[]{:S(2)}, u32[]{:S(2)}) collective-permute-start(f32[4,32,128]{2,1,0:T(8,128)S(1)} %get-tuple-element.26), channel_id=1, source_target_pairs={{160,224},{161,225},{162,226},{163,227},{164,228},{165,229},{166,2... | collective-permute-start | bytes 196616 | tf_op jit(solution)/shard_map/ppermute | solution.py:301
  66.6 32.1 %collective-permute-start.18 = (f32[4,32,128]{2,1,0:T(8,128)S(1)}, f32[4,32,128]{2,1,0:T(8,128)S(1)}, u32[]{:S(2)}, u32[]{:S(2)}) collective-permute-start(f32[4,32,128]{2,1,0:T(8,128)S(1)} %get-tuple-element.26), channel_id=1, source_target_pairs={{160,225},{161,226},{162,227},{163,228},{164,229},{165,230},{166,2... | collective-permute-start | bytes 196616 | tf_op jit(solution)/shard_map/ppermute | solution.py:301
  67.9 32.5 %collective-permute-start.17 = (f32[4,32,128]{2,1,0:T(8,128)S(1)}, f32[4,32,128]{2,1,0:T(8,128)S(1)}, u32[]{:S(2)}, u32[]{:S(2)}) collective-permute-start(f32[4,32,128]{2,1,0:T(8,128)S(1)} %get-tuple-element.26), channel_id=1, source_target_pairs={{160,226},{161,227},{162,228},{163,229},{164,230},{165,231},{166,2... | collective-permute-start | bytes 196616 | tf_op jit(solution)/shard_map/ppermute | solution.py:301
  102.5 2.2 %collective-permute-start.22 = (f32[4,32,128]{2,1,0:T(8,128)S(1)}, f32[4,32,128]{2,1,0:T(8,128)S(1)}, u32[]{:S(2)}, u32[]{:S(2)}) collective-permute-start(f32[4,32,128]{2,1,0:T(8,128)S(1)} %get-tuple-element.30), channel_id=1, source_target_pairs={{96,64},{97,65},{98,66},{99,67},{100,68},{101,69},{102,70},{103,71... | collective-permute-start | bytes 196616 | tf_op jit(solution)/shard_map/ppermute | solution.py:301

commit v3 on v2

--- a/solution.py
+++ b/solution.py
@@ -86,7 +86,7 @@
     return 0.125 * jnp.concatenate(rows, axis=0)
 
 
-def prep_kernel(x_ref, out_ref, x, sems):
+def prep_kernel(x_ref, even_ref, odd_ref, x, sems):
     copies = [pltpu.make_async_copy(x_ref.at[0, p], x.at[p], sems.at[p]) for p in range(CZ)]
     for copy in copies:
         copy.start()
@@ -96,9 +96,18 @@
     for p in range(CZ):
         copies[p].wait()
         r = split_dot(x[p], m) * KAPPA
-        for s in range(8):
-            for j in range(2):
-                out_ref[p, j, pl.ds(s, 8, stride=8), :] = r[8 * s : 8 * s + 8, j * CY : (j + 1) * CY]
+        for out_ref in (even_ref, odd_ref):
+            for s in range(8):
+                for j in range(2):
+                    out_ref[p, j, pl.ds(s, 8, stride=8), :] = r[8 * s : 8 * s + 8, j * CY : (j + 1) * CY]
+
+
+def word_kernel(own_ref, out_ref):
+    out_ref[...] = own_ref[0, 0, pl.ds(0, 8)]
+
+
+def gate_kernel(own_ref, word_ref, out_ref):
+    del own_ref, word_ref, out_ref
 
 
 def three(left, mid, right, n):
@@ -139,39 +148,77 @@
         get = lambda q, j: v[q, j]
 
 
-def fine_kernel(blocks, place_ref, own, two, one, out_ref, v, v1):
+def fine_kernel(blocks, odd, place_ref, own, one, two, out_ref, v, v1):
     def put(p, a, b):
         out_ref[p, 0] = a
         out_ref[p, 1] = b
 
-    fine_rounds(own, one, two, put, v, v1, place_ref[0], blocks)
-
-
-def last_fine_kernel(blocks, place_ref, own, two, one, co_ref, out_ref, jump_ref, send_ref, v, v1):
+    @pl.when(place_ref[1] % 2 == odd)
+    def _():
+        fine_rounds(own, one, two, put, v, v1, place_ref[0], blocks)
+
+
+def last_fine_kernel(blocks, part, place_ref, own, one, two, co_ref, *refs):
+    slab = place_ref[1]
+    mine = (slab % 2 == 0, slab == 1, (slab % 2 == 1) & (slab > 1))[part]
+    if part:
+        out_ref, jump_ref, v, v1 = refs[-4:]
+    else:
+        out_ref, jump_ref, send_ref, v, v1 = refs
+
     def put(p, a, b):
         out_ref[p, 0] = a
         out_ref[p, 1] = b
 
-    fine_rounds(own, one, two, put, v, v1, place_ref[0], blocks)
-    for q in range(CC):
-        old = co_ref[q]
-        jump = restricted(lambda p, j: out_ref[p, j], 2 * q) - old
-        jump_ref[q] = jump
-        send_ref[q] = jnp.where(place_ref[1] == 0, old + jump, jump)
-
-
-def coarse_kernel(blocks, place_ref, own, two, one, co_ref, cv, cv1):
+    @pl.when(mine)
+    def _():
+        fine_rounds(own, one, two, put, v, v1, place_ref[0], blocks)
+        for q in range(CC):
+            old = co_ref[q]
+            jump = restricted(lambda p, j: out_ref[p, j], 2 * q) - old
+            jump_ref[q] = jump
+            if part == 0:
+                send_ref[q] = jnp.where(slab == 0, old + jump, jump)
+
+
+def coarse_kernel(blocks, place_ref, own0, one0, two0, own1, one1, two1, co_ref, cv, cv1):
     at, then = sides(place_ref[0], CC)
-    for ref, base in ((own, CC), (one, at), (two, then)):
+
+    def fill(ref, base):
         for q in range(CC):
             cv[base + q] = restricted(lambda p, j: ref[p, j], 2 * q)
+
+    for odd, own, one, two in ((0, own0, one0, two0), (1, own1, one1, two1)):
+
+        @pl.when(place_ref[1] % 2 == odd)
+        def _():
+            fill(own, CC)
+            fill(one, at)
+            fill(two, then)
+
     first = (place_ref[0] - 1) * CC
     coarse_propagate(lambda q: cv[q], cv, cv1, 0, 3 * CC, first, blocks * CC)
     for q in range(CC):
         co_ref[q] = cv[CC + q]
 
 
-def first_sweep_kernel(blocks, place_ref, left, mid, right, jump_ref, old_ref, out_ref, send_ref, cv, cv1):
+def first_sweep_kernel(
+    blocks, place_ref, left, mid, right, jump_ref, old_ref, out_ref, send_ref, wide_ref, cv, cv1
+):
+    at, then = sides(place_ref[0], CC)
+
+    @pl.when(place_ref[1] == 2)
+    def _():
+        for ref, base in ((jump_ref, CC), (left, at), (right, then)):
+            for q in range(CC):
+                wide_ref[base + q] = ref[q]
+
+    @pl.when(place_ref[1] > 3)
+    def _():
+        for n, ref in enumerate((left, mid, right)):
+            for q in range(CC):
+                wide_ref[n * CC + q] = ref[q]
+
     @pl.when(place_ref[1] == 1)
     def _():
         first = (place_ref[0] - 1) * CC
@@ -188,9 +235,10 @@
 
 
 def sweep_kernel(
-    blocks, slab, place_ref, a0, a1, a2, a3, a4, j0, j1, j2, jump_ref, old_ref, oldx_ref,
-    out_ref, outx_ref, send_ref, cv, cv1,
+    blocks, slab, place_ref, a0, a1, a2, a3, a4, wide_ref, jump_ref, old_ref, oldx_ref, *refs
 ):
+    out_ref, outx_ref, send_ref, cv, cv1 = refs[-5:]
+
     @pl.when(place_ref[1] == slab)
     def _():
         refs = (a0, a1, a2, a3, a4)
@@ -199,9 +247,8 @@
         coarse_propagate(get, cv, cv1, 0, 5 * CC, first, blocks * CC)
         for q in range(CC):
             outx_ref[q] = cv[2 * CC + q]
-        wide = three(j0, j1, j2, CC)
         for q in range(CC, 4 * CC):
-            cv[q] = cv[q] + wide(q - CC)
+            cv[q] = cv[q] + wide_ref[q - CC]
         coarse_propagate(lambda q: cv[q], cv, cv1, CC, 4 * CC, first, blocks * CC)
         for q in range(CC):
             new = cv[2 * CC + q]
@@ -275,7 +322,7 @@
     return [pltpu.VMEM((n * CC, CX, CY), jnp.float32)] * 2
 
 
-def call(kernel, out_shape, in_specs, args, scratch=(), out_specs=None):
+def call(kernel, out_shape, in_specs, args, scratch=(), out_specs=None, **kw):
     if out_specs is None:
         out_specs = (VM,) * len(out_shape) if isinstance(out_shape, tuple) else VM
     return pl.pallas_call(
@@ -285,19 +332,25 @@
         out_specs=out_specs,
         scratch_shapes=list(scratch),
         compiler_params=PARAMS,
+        **kw,
     )(*args)
 
 
-def both(array):
+def both(array, slabs):
     count = lax.axis_size("gz")
-    pairs = [[(i, i + 1) for i in range(edge, count - 1, 2)] for edge in (1, 0)]
-    one, two = (lax.ppermute(array, "gz", p + [(j, i) for i, j in p]) for p in pairs)
-    return two, one
-
-
-def handed(array, slabs, by=0):
+    out = []
+    for edge in (1, 0):
+        pairs = [(k * count + i, k * count + i + 1) for k in slabs for i in range(edge, count - 1, 2)]
+        out.append(lax.ppermute(array, ("tm", "gz"), pairs + [(j, i) for i, j in pairs]))
+    return out[0], out[1]
+
+
+def handed(array, slabs, by=0, swap=()):
     count = lax.axis_size("gz")
     pairs = [(a * count + i, b * count + i + by) for a, b in slabs for i in range(count) if 0 <= i + by < count]
+    for k in swap:
+        for i in range(int(by == 1), count - 1, 2):
+            pairs += [(k * count + i, k * count + i + 1), (k * count + i + 1, k * count + i)]
     return lax.ppermute(array, ("tm", "gz"), pairs)
 
 
@@ -305,37 +358,74 @@
     blocks = lax.axis_size("gz")
     slabs = lax.axis_size("tm")
     place = jnp.stack([lax.axis_index("gz"), lax.axis_index("tm")]).astype(jnp.int32)
+    evens, odds = range(0, slabs, 2), range(1, slabs, 2)
     start_states = pltpu.with_memory_space_constraint(start_states, pltpu.HBM)
-    own = call(prep_kernel, fine_shape, [HB], (start_states,), WHOLE)
-    near = (place, own, *both(own))
-    own = call(functools.partial(fine_kernel, blocks), fine_shape, [SM] + [VM] * 3, near, FINE_WORK)
-    two, one = both(own)
-    old = call(functools.partial(coarse_kernel, blocks), coarse_shape, [SM] + [VM] * 3, near, coarse_work(3))
+    own, own1 = call(prep_kernel, (fine_shape,) * 2, [HB], (start_states,), WHOLE)
+    near = both(own, evens)
+    word_shape = jax.ShapeDtypeStruct((8, CY), jnp.float32)
+    word = handed(call(word_kernel, word_shape, [VM], (own,)), [(k, k + 1) for k in evens])
+    own1 = call(gate_kernel, fine_shape, [VM] * 2, (own1, word), input_output_aliases={0: 0})
+    near1 = both(own1, odds)
+    fine = [SM] + [VM] * 3
+    mid = call(functools.partial(fine_kernel, blocks, 0), fine_shape, fine, (place, own, *near), FINE_WORK)
+    next0 = both(mid, evens)
+    mid1 = call(functools.partial(fine_kernel, blocks, 1), fine_shape, fine, (place, own1, *near1), FINE_WORK)
+    next1 = both(mid1, odds)
+    old = call(
+        functools.partial(coarse_kernel, blocks),
+        coarse_shape,
+        [SM] + [VM] * 6,
+        (place, own, *near, own1, *near1),
+        coarse_work(3),
+    )
     fine_end, jump, send = call(
-        functools.partial(last_fine_kernel, blocks),
+        functools.partial(last_fine_kernel, blocks, 0),
         (fine_shape, coarse_shape, coarse_shape),
         [SM] + [VM] * 4,
-        (place, own, two, one, old),
+        (place, mid, *next0, old),
         FINE_WORK,
     )
+    fine_end, jump = call(
+        functools.partial(last_fine_kernel, blocks, 1),
+        (fine_shape, coarse_shape),
+        [SM] + [VM] * 6,
+        (place, mid1, *next1, old, fine_end, jump),
+        FINE_WORK,
+        input_output_aliases={5: 0, 6: 1},
+    )
     firsts = range(0, slabs - 1, 2)
-    side = [handed(send, [(k, k + 1) for k in firsts], by) for by in (1, 0, -1)]
-    picked, send = call(
+    pairs = [(k, k + 1) for k in firsts if k != 2]
+    side = [handed(send, pairs, by, (2,) if by else ()) for by in (1, 0, -1)]
+    wide_shape = jax.ShapeDtypeStruct((3 * CC, CX, CY), jnp.float32)
+    picked, send, wide = call(
         functools.partial(first_sweep_kernel, blocks),
-        (coarse_shape,) * 2,
+        (coarse_shape, coarse_shape, wide_shape),
         [SM] + [VM] * 5,
         (place, *side, jump, old),
         coarse_work(3),
     )
+    fine_end, jump = call(
+        functools.partial(last_fine_kernel, blocks, 2),
+        (fine_shape, coarse_shape),
+        [SM] + [VM] * 7,
+        (place, mid1, *next1, old, fine_end, jump, send),
+        FINE_WORK,
+        input_output_aliases={5: 0, 6: 1},
+    )
     rest = call(rest_kernel, half_shape, [VM] * 2, (fine_end, old))
     even = jump
     for k in firsts[1:]:
+        early = (rest,) if k == firsts[-1] else ()
         got = [handed(send, [(k - 1, k + 1)], by) for by in (2, 1, 0, -1, -2)]
+        near = wide
+        if k == 2:
+            near, jump, *got = lax.optimization_barrier((wide, jump, *got))
+            near = handed(near, [(2, 3)])
         picked, even, send = call(
             functools.partial(sweep_kernel, blocks, k + 1),
             (coarse_shape,) * 3,
-            [SM] + [VM] * 11,
-            (place, *got, *side, jump, picked, even),
+            [SM] + [VM] * 9 + [HB] * len(early),
+            (place, *got, near, jump, picked, even, *early),
             coarse_work(5),
         )
     even = handed(even, [(k + 1, k) for k in firsts[1:]])

time: 107 us -> 97 us (0.907)
  the two profiles are of different devices: /device:TPU:227 before, /device:TPU:225 now
where the time goes in v3:
time: 97 us; the launch traced here: 95.2 us
  waiting for transfers between devices  39 us (40%)
  starting transfers between devices  35.8 us (37%)
  Pallas kernels  19.8 us (20%)
    ppermute x21, waiting for transfers between devices, handed(): return lax.ppermute(array, ('tm', 'gz'), pairs)  30.1 us
    ppermute x21, starting transfers between devices, handed(): return lax.ppermute(array, ('tm', 'gz'), pairs)  20.2 us
    pallas_call x15, Pallas kernels, call(): pl.pallas_call(kernel, out_shape=out_shape, in_specs=in_specs, out_specs=...  19.8 us
    ppermute x8, starting transfers between devices, both(): lax.ppermute(array, ('tm', 'gz'), pairs + [(j, i) for i, j in pairs])  15.5 us
    ppermute x8, waiting for transfers between devices, both(): lax.ppermute(array, ('tm', 'gz'), pairs + [(j, i) for i, j in pairs])  8.85 us
  transfers between devices with their start and end apart: 29, of which 10 were waited for; matrix products, arithmetic and copies ran while one was open for 0% of the time, Pallas kernels for 12%

profile of v3, /device:TPU:225, one launch (start us, length us, event | category | flops | bytes accessed | tf_op | source)
XLA Modules:
  0.0 95.2 jit_solution(4433848708814980554)
XLA Ops:
  0.0 2.9 %shard_map.17 = (f32[8,2,64,128]{3,2,1,0:T(8,128)S(1)}, f32[8,2,64,128]{3,2,1,0:T(8,128)S(1)}) custom-call(f32[1,8,64,256]{3,2,1,0:T(8,128)} %x_ref.1), custom_call_target="tpu_custom_call" | custom-call | tf_op jit(solution)/shard_map/pallas_call | solution.py:328
  4.3 1.3 %collective-permute-start = (f32[8,128]{1,0:T(8,128)S(1)}, f32[8,128]{1,0:T(8,128)S(1)}, u32[]{:S(2)}, u32[]{:S(2)}) collective-permute-start(f32[8,128]{1,0:T(8,128)S(1)} %shard_map.18), channel_id=1, source_target_pairs={{0,32},{1,33},{2,34},{3,35},{4,36},{5,37},{6,38},{7,39},{8,40},{9,... | collective-permute-start | bytes 12296 | tf_op jit(solution)/shard_map/ppermute | solution.py:354
  5.6 9.4 %collective-permute-done.word_ref = f32[8,128]{1,0:T(8,128)S(1)} collective-permute-done((f32[8,128]{1,0:T(8,128)S(1)}, f32[8,128]{1,0:T(8,128)S(1)}, u32[]{:S(2)}, u32[]{:S(2)}) %collective-permute-start) | collective-permute-done | bytes 4128 | tf_op jit(solution)/shard_map/ppermute | solution.py:354
  15.0 2.8 %collective-permute-start.1 = (f32[8,2,64,128]{3,2,1,0:T(8,128)S(1)}, f32[8,2,64,128]{3,2,1,0:T(8,128)S(1)}, u32[]{:S(2)}, u32[]{:S(2)}) collective-permute-start(f32[8,2,64,128]{3,2,1,0:T(8,128)S(1)} %shard_map.19.own.own1), channel_id=1, source_target_pairs={{33,34},{35,36},{37,38},{39,40},{41,42},{43,44},{45,46},{47,48},{4... | collective-permute-start | bytes 1572872 | tf_op jit(solution)/shard_map/ppermute | solution.py:344
  17.8 2.8 %collective-permute-start.2 = (f32[8,2,64,128]{3,2,1,0:T(8,128)S(1)}, f32[8,2,64,128]{3,2,1,0:T(8,128)S(1)}, u32[]{:S(2)}, u32[]{:S(2)}) collective-permute-start(f32[8,2,64,128]{3,2,1,0:T(8,128)S(1)} %shard_map.19.own.own1), channel_id=1, source_target_pairs={{32,33},{34,35},{36,37},{38,39},{40,41},{42,43},{44,45},{46,47},{4... | collective-permute-start | bytes 1572872 | tf_op jit(solution)/shard_map/ppermute | solution.py:344
  22.6 6.5 %collective-permute-done.1.one.one1 = f32[8,2,64,128]{3,2,1,0:T(8,128)S(1)} collective-permute-done((f32[8,2,64,128]{3,2,1,0:T(8,128)S(1)}, f32[8,2,64,128]{3,2,1,0:T(8,128)S(1)}, u32[]{:S(2)}, u32[]{:S(2)}) %collective-permute-start.1) | collective-permute-done | bytes 524320 | tf_op jit(solution)/shard_map/ppermute | solution.py:344
  29.1 3.7 %shard_map.20.own = f32[8,2,64,128]{3,2,1,0:T(8,128)S(1)} custom-call(s32[2]{0:T(128)S(1)} %pad_add_fusion.place_ref, f32[8,2,64,128]{3,2,1,0:T(8,128)S(1)} %shard_map.19.own.own1, f32[8,2,64,128]{3,2,1,0:T(8,128)S(1)} %collective-permute-done.1.one.one1, f32[8,2,64,128]{3,2,1,0:T(8,128)S(1)} %collective-permute-done.2.two.two1), custom_call_target="tpu_custom_call" | custom-call | tf_op jit(solution)/shard_map/pallas_call | solution.py:328
  32.9 5.3 %collective-permute-start.3 = (f32[8,2,64,128]{3,2,1,0:T(8,128)S(1)}, f32[8,2,64,128]{3,2,1,0:T(8,128)S(1)}, u32[]{:S(2)}, u32[]{:S(2)}) collective-permute-start(f32[8,2,64,128]{3,2,1,0:T(8,128)S(1)} %shard_map.20.own), channel_id=1, source_target_pairs={{33,34},{35,36},{37,38},{39,40},{41,42},{43,44},{45,46},{47,48},{4... | collective-permute-start | bytes 1572872 | tf_op jit(solution)/shard_map/ppermute | solution.py:344
  38.2 1.9 %collective-permute-start.4 = (f32[8,2,64,128]{3,2,1,0:T(8,128)S(1)}, f32[8,2,64,128]{3,2,1,0:T(8,128)S(1)}, u32[]{:S(2)}, u32[]{:S(2)}) collective-permute-start(f32[8,2,64,128]{3,2,1,0:T(8,128)S(1)} %shard_map.20.own), channel_id=1, source_target_pairs={{32,33},{34,35},{36,37},{38,39},{40,41},{42,43},{44,45},{46,47},{4... | collective-permute-start | bytes 1572872 | tf_op jit(solution)/shard_map/ppermute | solution.py:344
  40.1 1.0 %shard_map.21.co_ref.old_ref = f32[4,32,128]{2,1,0:T(8,128)S(1)} custom-call(s32[2]{0:T(128)S(1)} %pad_add_fusion.place_ref, f32[8,2,64,128]{3,2,1,0:T(8,128)S(1)} %get-tuple-element.33.own_ref.own0.own, f32[8,2,64,128]{3,2,1,0:T(8,128)S(1)} %collective-permute-done.5.one0.one, f32[8,2,64,128]{3,2,1,0:T(8,128)S(1)} %collective-permute-done.6.two0.two, ...), custom_call_target="tpu_custom_call" | custom-call | tf_op jit(solution)/shard_map/pallas_call | solution.py:328
  41.1 0.7 shard_map.23
  41.9 1.3 %collective-permute-start.10 = (f32[4,32,128]{2,1,0:T(8,128)S(1)}, f32[4,32,128]{2,1,0:T(8,128)S(1)}, u32[]{:S(2)}, u32[]{:S(2)}) collective-permute-start(f32[4,32,128]{2,1,0:T(8,128)S(1)} %get-tuple-element.38), channel_id=1, source_target_pairs={{0,32},{1,33},{2,34},{3,35},{4,36},{5,37},{6,38},{7,39},{8,40},{9,... | collective-permute-start | bytes 196616 | tf_op jit(solution)/shard_map/ppermute | solution.py:354
  43.2 1.3 %collective-permute-start.11 = (f32[4,32,128]{2,1,0:T(8,128)S(1)}, f32[4,32,128]{2,1,0:T(8,128)S(1)}, u32[]{:S(2)}, u32[]{:S(2)}) collective-permute-start(f32[4,32,128]{2,1,0:T(8,128)S(1)} %get-tuple-element.38), channel_id=1, source_target_pairs={{1,32},{2,33},{3,34},{4,35},{5,36},{6,37},{7,38},{8,39},{9,40},{10... | collective-permute-start | bytes 196616 | tf_op jit(solution)/shard_map/ppermute | solution.py:354
  44.5 1.3 %collective-permute-start.9 = (f32[4,32,128]{2,1,0:T(8,128)S(1)}, f32[4,32,128]{2,1,0:T(8,128)S(1)}, u32[]{:S(2)}, u32[]{:S(2)}) collective-permute-start(f32[4,32,128]{2,1,0:T(8,128)S(1)} %get-tuple-element.38), channel_id=1, source_target_pairs={{0,33},{1,34},{2,35},{3,36},{4,37},{5,38},{6,39},{7,40},{8,41},{9,... | collective-permute-start | bytes 196616 | tf_op jit(solution)/shard_map/ppermute | solution.py:354
  45.8 1.2 %collective-permute-done.3.one = f32[8,2,64,128]{3,2,1,0:T(8,128)S(1)} collective-permute-done((f32[8,2,64,128]{3,2,1,0:T(8,128)S(1)}, f32[8,2,64,128]{3,2,1,0:T(8,128)S(1)}, u32[]{:S(2)}, u32[]{:S(2)}) %collective-permute-start.3) | collective-permute-done | bytes 524320 | tf_op jit(solution)/shard_map/ppermute | solution.py:344
  47.0 1.1 %collective-permute-done.4.two = f32[8,2,64,128]{3,2,1,0:T(8,128)S(1)} collective-permute-done((f32[8,2,64,128]{3,2,1,0:T(8,128)S(1)}, f32[8,2,64,128]{3,2,1,0:T(8,128)S(1)}, u32[]{:S(2)}, u32[]{:S(2)}) %collective-permute-start.4) | collective-permute-done | bytes 524320 | tf_op jit(solution)/shard_map/ppermute | solution.py:344
  48.7 0.7 collective-permute-done.11.right
  49.4 5.2 %collective-permute-done.9.left = f32[4,32,128]{2,1,0:T(8,128)S(1)} collective-permute-done((f32[4,32,128]{2,1,0:T(8,128)S(1)}, f32[4,32,128]{2,1,0:T(8,128)S(1)}, u32[]{:S(2)}, u32[]{:S(2)}) %collective-permute-start.9) | collective-permute-done | bytes 65568 | tf_op jit(solution)/shard_map/ppermute | solution.py:354
  58.6 3.8 %shard_map.26 = (f32[8,2,64,128]{3,2,1,0:T(8,128)S(1)}, f32[4,32,128]{2,1,0:T(8,128)S(1)}) custom-call(s32[2]{0:T(128)S(1)} %pad_add_fusion.place_ref, f32[8,2,64,128]{3,2,1,0:T(8,128)S(1)} %shard_map.20.own, f32[8,2,64,128]{3,2,1,0:T(8,128)S(1)} %collective-permute-done.3.one, ...), custom_call_target="tpu_custom_call", output_to_operand_aliasing={{0}: (5, {}), {1}: (6, {})} | custom-call | tf_op jit(solution)/shard_map/pallas_call | solution.py:328
  63.2 0.8 shard_map.28
  68.0 1.3 %collective-permute-start.23 = (f32[4,32,128]{2,1,0:T(8,128)S(1)}, f32[4,32,128]{2,1,0:T(8,128)S(1)}, u32[]{:S(2)}, u32[]{:S(2)}) collective-permute-start(f32[4,32,128]{2,1,0:T(8,128)S(1)} %get-tuple-element.54), channel_id=1, source_target_pairs={{160,226},{161,227},{162,228},{163,229},{164,230},{165,231},{166,2... | collective-permute-start | bytes 196616 | tf_op jit(solution)/shard_map/ppermute | solution.py:354
  69.3 1.3 %collective-permute-start.24 = (f32[4,32,128]{2,1,0:T(8,128)S(1)}, f32[4,32,128]{2,1,0:T(8,128)S(1)}, u32[]{:S(2)}, u32[]{:S(2)}) collective-permute-start(f32[4,32,128]{2,1,0:T(8,128)S(1)} %get-tuple-element.54), channel_id=1, source_target_pairs={{160,225},{161,226},{162,227},{163,228},{164,229},{165,230},{166,2... | collective-permute-start | bytes 196616 | tf_op jit(solution)/shard_map/ppermute | solution.py:354
  70.6 1.3 %collective-permute-start.25 = (f32[4,32,128]{2,1,0:T(8,128)S(1)}, f32[4,32,128]{2,1,0:T(8,128)S(1)}, u32[]{:S(2)}, u32[]{:S(2)}) collective-permute-start(f32[4,32,128]{2,1,0:T(8,128)S(1)} %get-tuple-element.54), channel_id=1, source_target_pairs={{160,224},{161,225},{162,226},{163,227},{164,228},{165,229},{166,2... | collective-permute-start | bytes 196616 | tf_op jit(solution)/shard_map/ppermute | solution.py:354
  71.9 1.3 %collective-permute-start.26 = (f32[4,32,128]{2,1,0:T(8,128)S(1)}, f32[4,32,128]{2,1,0:T(8,128)S(1)}, u32[]{:S(2)}, u32[]{:S(2)}) collective-permute-start(f32[4,32,128]{2,1,0:T(8,128)S(1)} %get-tuple-element.54), channel_id=1, source_target_pairs={{161,224},{162,225},{163,226},{164,227},{165,228},{166,229},{167,2... | collective-permute-start | bytes 196616 | tf_op jit(solution)/shard_map/ppermute | solution.py:354
  73.2 1.3 %collective-permute-start.27 = (f32[4,32,128]{2,1,0:T(8,128)S(1)}, f32[4,32,128]{2,1,0:T(8,128)S(1)}, u32[]{:S(2)}, u32[]{:S(2)}) collective-permute-start(f32[4,32,128]{2,1,0:T(8,128)S(1)} %get-tuple-element.54), channel_id=1, source_target_pairs={{162,224},{163,225},{164,226},{165,227},{166,228},{167,229},{168,2... | collective-permute-start | bytes 196616 | tf_op jit(solution)/shard_map/ppermute | solution.py:354
  74.5 0.7 shard_map.27.refs_0_.rest_ref
  75.2 11.4 %collective-permute-done.23.a0 = f32[4,32,128]{2,1,0:T(8,128)S(1)} collective-permute-done((f32[4,32,128]{2,1,0:T(8,128)S(1)}, f32[4,32,128]{2,1,0:T(8,128)S(1)}, u32[]{:S(2)}, u32[]{:S(2)}) %collective-permute-start.23) | collective-permute-done | bytes 65568 | tf_op jit(solution)/shard_map/ppermute | solution.py:354
  86.6 2.3 %collective-permute-done.24.a1 = f32[4,32,128]{2,1,0:T(8,128)S(1)} collective-permute-done((f32[4,32,128]{2,1,0:T(8,128)S(1)}, f32[4,32,128]{2,1,0:T(8,128)S(1)}, u32[]{:S(2)}, u32[]{:S(2)}) %collective-permute-start.24) | collective-permute-done | bytes 65568 | tf_op jit(solution)/shard_map/ppermute | solution.py:354
  89.0 2.1 %shard_map.30 = (f32[4,32,128]{2,1,0:T(8,128)S(1)}, f32[4,32,128]{2,1,0:T(8,128)S(1)}, f32[4,32,128]{2,1,0:T(8,128)}) custom-call(s32[2]{0:T(128)S(1)} %pad_add_fusion.place_ref, f32[4,32,128]{2,1,0:T(8,128)S(1)} %collective-permute-done.23.a0, f32[4,32,128]{2,1,0:T(8,128)S(1)} %collective-permute-done.24.a1, f32[4,32,128]{2,1,0:T(8,128)S(1)} %collective-permute-done.25.a2, ...), custom_call_target="tpu_custom_call" | custom-call | tf_op jit(solution)/shard_map/pallas_call | solution.py:328
  91.2 1.3 %collective-permute-start.28 = (f32[4,32,128]{2,1,0:T(8,128)S(1)}, f32[4,32,128]{2,1,0:T(8,128)S(1)}, u32[]{:S(2)}, u32[]{:S(2)}) collective-permute-start(f32[4,32,128]{2,1,0:T(8,128)S(1)} %get-tuple-element.58), channel_id=1, source_target_pairs={{96,64},{97,65},{98,66},{99,67},{100,68},{101,69},{102,70},{103,71... | collective-permute-start | bytes 196616 | tf_op jit(solution)/shard_map/ppermute | solution.py:354
  92.5 0.9 collective-permute-done.28.even_ref
  93.3 1.7 %shard_map.31 = f32[1,8,64,256]{3,2,1,0:T(8,128)} custom-call(s32[2]{0:T(128)S(1)} %pad_add_fusion.place_ref, f32[2,8,64,128]{3,2,1,0:T(8,128)S(1)} %shard_map.27.refs_0_.rest_ref, f32[4,32,128]{2,1,0:T(8,128)S(1)} %get-tuple-element.57.picked_ref, f32[4,32,128]{2,1,0:T(8,128)S(1)} %collective-permute-done.28.even_ref), custom_call_target="tpu_custom_call" | custom-call | tf_op jit(solution)/shard_map/pallas_call | solution.py:328
  (42 shorter events, 12.6 us)
Async XLA Ops:
  2.9 17.8 %collective-permute-start.5 = (f32[8,2,64,128]{3,2,1,0:T(8,128)S(1)}, f32[8,2,64,128]{3,2,1,0:T(8,128)S(1)}, u32[]{:S(2)}, u32[]{:S(2)}) collective-permute-start(f32[8,2,64,128]{3,2,1,0:T(8,128)S(1)} %get-tuple-element.33.own_ref.own0.own), channel_id=1, source_target_pairs={{1,2},{3,4},{5,6},{7,8},{9,10},{11,12},{13,14},{15,16},{17,18},{19... | collective-permute-start | bytes 1572872 | tf_op jit(solution)/shard_map/ppermute | solution.py:344
  3.6 17.1 %collective-permute-start.6 = (f32[8,2,64,128]{3,2,1,0:T(8,128)S(1)}, f32[8,2,64,128]{3,2,1,0:T(8,128)S(1)}, u32[]{:S(2)}, u32[]{:S(2)}) collective-permute-start(f32[8,2,64,128]{3,2,1,0:T(8,128)S(1)} %get-tuple-element.33.own_ref.own0.own), channel_id=1, source_target_pairs={{0,1},{2,3},{4,5},{6,7},{8,9},{10,11},{12,13},{14,15},{16,17},{18,... | collective-permute-start | bytes 1572872 | tf_op jit(solution)/shard_map/ppermute | solution.py:344
  4.3 10.7 %collective-permute-start = (f32[8,128]{1,0:T(8,128)S(1)}, f32[8,128]{1,0:T(8,128)S(1)}, u32[]{:S(2)}, u32[]{:S(2)}) collective-permute-start(f32[8,128]{1,0:T(8,128)S(1)} %shard_map.18), channel_id=1, source_target_pairs={{0,32},{1,33},{2,34},{3,35},{4,36},{5,37},{6,38},{7,39},{8,40},{9,... | collective-permute-start | bytes 12296 | tf_op jit(solution)/shard_map/ppermute | solution.py:354
  15.0 14.1 %collective-permute-start.1 = (f32[8,2,64,128]{3,2,1,0:T(8,128)S(1)}, f32[8,2,64,128]{3,2,1,0:T(8,128)S(1)}, u32[]{:S(2)}, u32[]{:S(2)}) collective-permute-start(f32[8,2,64,128]{3,2,1,0:T(8,128)S(1)} %shard_map.19.own.own1), channel_id=1, source_target_pairs={{33,34},{35,36},{37,38},{39,40},{41,42},{43,44},{45,46},{47,48},{4... | collective-permute-start | bytes 1572872 | tf_op jit(solution)/shard_map/ppermute | solution.py:344
  17.8 11.3 %collective-permute-start.2 = (f32[8,2,64,128]{3,2,1,0:T(8,128)S(1)}, f32[8,2,64,128]{3,2,1,0:T(8,128)S(1)}, u32[]{:S(2)}, u32[]{:S(2)}) collective-permute-start(f32[8,2,64,128]{3,2,1,0:T(8,128)S(1)} %shard_map.19.own.own1), channel_id=1, source_target_pairs={{32,33},{34,35},{36,37},{38,39},{40,41},{42,43},{44,45},{46,47},{4... | collective-permute-start | bytes 1572872 | tf_op jit(solution)/shard_map/ppermute | solution.py:344
  21.2 19.9 %collective-permute-start.7 = (f32[8,2,64,128]{3,2,1,0:T(8,128)S(1)}, f32[8,2,64,128]{3,2,1,0:T(8,128)S(1)}, u32[]{:S(2)}, u32[]{:S(2)}) collective-permute-start(f32[8,2,64,128]{3,2,1,0:T(8,128)S(1)} %shard_map.22.own), channel_id=1, source_target_pairs={{1,2},{3,4},{5,6},{7,8},{9,10},{11,12},{13,14},{15,16},{17,18},{19... | collective-permute-start | bytes 1572872 | tf_op jit(solution)/shard_map/ppermute | solution.py:344
  21.9 19.2 %collective-permute-start.8 = (f32[8,2,64,128]{3,2,1,0:T(8,128)S(1)}, f32[8,2,64,128]{3,2,1,0:T(8,128)S(1)}, u32[]{:S(2)}, u32[]{:S(2)}) collective-permute-start(f32[8,2,64,128]{3,2,1,0:T(8,128)S(1)} %shard_map.22.own), channel_id=1, source_target_pairs={{0,1},{2,3},{4,5},{6,7},{8,9},{10,11},{12,13},{14,15},{16,17},{18,... | collective-permute-start | bytes 1572872 | tf_op jit(solution)/shard_map/ppermute | solution.py:344
  32.9 14.1 %collective-permute-start.3 = (f32[8,2,64,128]{3,2,1,0:T(8,128)S(1)}, f32[8,2,64,128]{3,2,1,0:T(8,128)S(1)}, u32[]{:S(2)}, u32[]{:S(2)}) collective-permute-start(f32[8,2,64,128]{3,2,1,0:T(8,128)S(1)} %shard_map.20.own), channel_id=1, source_target_pairs={{33,34},{35,36},{37,38},{39,40},{41,42},{43,44},{45,46},{47,48},{4... | collective-permute-start | bytes 1572872 | tf_op jit(solution)/shard_map/ppermute | solution.py:344
  38.2 9.9 %collective-permute-start.4 = (f32[8,2,64,128]{3,2,1,0:T(8,128)S(1)}, f32[8,2,64,128]{3,2,1,0:T(8,128)S(1)}, u32[]{:S(2)}, u32[]{:S(2)}) collective-permute-start(f32[8,2,64,128]{3,2,1,0:T(8,128)S(1)} %shard_map.20.own), channel_id=1, source_target_pairs={{32,33},{34,35},{36,37},{38,39},{40,41},{42,43},{44,45},{46,47},{4... | collective-permute-start | bytes 1572872 | tf_op jit(solution)/shard_map/ppermute | solution.py:344
  41.9 6.8 %collective-permute-start.10 = (f32[4,32,128]{2,1,0:T(8,128)S(1)}, f32[4,32,128]{2,1,0:T(8,128)S(1)}, u32[]{:S(2)}, u32[]{:S(2)}) collective-permute-start(f32[4,32,128]{2,1,0:T(8,128)S(1)} %get-tuple-element.38), channel_id=1, source_target_pairs={{0,32},{1,33},{2,34},{3,35},{4,36},{5,37},{6,38},{7,39},{8,40},{9,... | collective-permute-start | bytes 196616 | tf_op jit(solution)/shard_map/ppermute | solution.py:354
  43.2 6.2 %collective-permute-start.11 = (f32[4,32,128]{2,1,0:T(8,128)S(1)}, f32[4,32,128]{2,1,0:T(8,128)S(1)}, u32[]{:S(2)}, u32[]{:S(2)}) collective-permute-start(f32[4,32,128]{2,1,0:T(8,128)S(1)} %get-tuple-element.38), channel_id=1, source_target_pairs={{1,32},{2,33},{3,34},{4,35},{5,36},{6,37},{7,38},{8,39},{9,40},{10... | collective-permute-start | bytes 196616 | tf_op jit(solution)/shard_map/ppermute | solution.py:354
  44.5 10.2 %collective-permute-start.9 = (f32[4,32,128]{2,1,0:T(8,128)S(1)}, f32[4,32,128]{2,1,0:T(8,128)S(1)}, u32[]{:S(2)}, u32[]{:S(2)}) collective-permute-start(f32[4,32,128]{2,1,0:T(8,128)S(1)} %get-tuple-element.38), channel_id=1, source_target_pairs={{0,33},{1,34},{2,35},{3,36},{4,37},{5,38},{6,39},{7,40},{8,41},{9,... | collective-permute-start | bytes 196616 | tf_op jit(solution)/shard_map/ppermute | solution.py:354
  55.2 7.2 %collective-permute-start.12 = (f32[4,32,128]{2,1,0:T(8,128)S(1)}, f32[4,32,128]{2,1,0:T(8,128)S(1)}, u32[]{:S(2)}, u32[]{:S(2)}) collective-permute-start(f32[4,32,128]{2,1,0:T(8,128)S(1)} %get-tuple-element.39.refs_2_), channel_id=1, source_target_pairs={{32,98},{33,99},{34,100},{35,101},{36,102},{37,103},{38,104},{39,1... | collective-permute-start | bytes 196616 | tf_op jit(solution)/shard_map/ppermute | solution.py:354
  55.9 6.6 %collective-permute-start.13 = (f32[4,32,128]{2,1,0:T(8,128)S(1)}, f32[4,32,128]{2,1,0:T(8,128)S(1)}, u32[]{:S(2)}, u32[]{:S(2)}) collective-permute-start(f32[4,32,128]{2,1,0:T(8,128)S(1)} %get-tuple-element.39.refs_2_), channel_id=1, source_target_pairs={{32,97},{33,98},{34,99},{35,100},{36,101},{37,102},{38,103},{39,10... | collective-permute-start | bytes 196616 | tf_op jit(solution)/shard_map/ppermute | solution.py:354
  56.6 5.9 %collective-permute-start.14 = (f32[4,32,128]{2,1,0:T(8,128)S(1)}, f32[4,32,128]{2,1,0:T(8,128)S(1)}, u32[]{:S(2)}, u32[]{:S(2)}) collective-permute-start(f32[4,32,128]{2,1,0:T(8,128)S(1)} %get-tuple-element.39.refs_2_), channel_id=1, source_target_pairs={{32,96},{33,97},{34,98},{35,99},{36,100},{37,101},{38,102},{39,103... | collective-permute-start | bytes 196616 | tf_op jit(solution)/shard_map/ppermute | solution.py:354
  57.3 5.2 %collective-permute-start.15 = (f32[4,32,128]{2,1,0:T(8,128)S(1)}, f32[4,32,128]{2,1,0:T(8,128)S(1)}, u32[]{:S(2)}, u32[]{:S(2)}) collective-permute-start(f32[4,32,128]{2,1,0:T(8,128)S(1)} %get-tuple-element.39.refs_2_), channel_id=1, source_target_pairs={{33,96},{34,97},{35,98},{36,99},{37,100},{38,101},{39,102},{40,103... | collective-permute-start | bytes 196616 | tf_op jit(solution)/shard_map/ppermute | solution.py:354
  57.9 4.6 %collective-permute-start.16 = (f32[4,32,128]{2,1,0:T(8,128)S(1)}, f32[4,32,128]{2,1,0:T(8,128)S(1)}, u32[]{:S(2)}, u32[]{:S(2)}) collective-permute-start(f32[4,32,128]{2,1,0:T(8,128)S(1)} %get-tuple-element.39.refs_2_), channel_id=1, source_target_pairs={{34,96},{35,97},{36,98},{37,99},{38,100},{39,101},{40,102},{41,103... | collective-permute-start | bytes 196616 | tf_op jit(solution)/shard_map/ppermute | solution.py:354
  62.5 0.7 collective-permute-start.17
  64.0 3.4 %collective-permute-start.18 = (f32[4,32,128]{2,1,0:T(8,128)S(1)}, f32[4,32,128]{2,1,0:T(8,128)S(1)}, u32[]{:S(2)}, u32[]{:S(2)}) collective-permute-start(f32[4,32,128]{2,1,0:T(8,128)S(1)} %get-tuple-element.51), channel_id=1, source_target_pairs={{96,162},{97,163},{98,164},{99,165},{100,166},{101,167},{102,168},... | collective-permute-start | bytes 196616 | tf_op jit(solution)/shard_map/ppermute | solution.py:354
  64.7 2.7 %collective-permute-start.19 = (f32[4,32,128]{2,1,0:T(8,128)S(1)}, f32[4,32,128]{2,1,0:T(8,128)S(1)}, u32[]{:S(2)}, u32[]{:S(2)}) collective-permute-start(f32[4,32,128]{2,1,0:T(8,128)S(1)} %get-tuple-element.51), channel_id=1, source_target_pairs={{96,161},{97,162},{98,163},{99,164},{100,165},{101,166},{102,167},... | collective-permute-start | bytes 196616 | tf_op jit(solution)/shard_map/ppermute | solution.py:354
  65.3 2.0 %collective-permute-start.20 = (f32[4,32,128]{2,1,0:T(8,128)S(1)}, f32[4,32,128]{2,1,0:T(8,128)S(1)}, u32[]{:S(2)}, u32[]{:S(2)}) collective-permute-start(f32[4,32,128]{2,1,0:T(8,128)S(1)} %get-tuple-element.51), channel_id=1, source_target_pairs={{96,160},{97,161},{98,162},{99,163},{100,164},{101,165},{102,166},... | collective-permute-start | bytes 196616 | tf_op jit(solution)/shard_map/ppermute | solution.py:354
  66.0 1.4 %collective-permute-start.21 = (f32[4,32,128]{2,1,0:T(8,128)S(1)}, f32[4,32,128]{2,1,0:T(8,128)S(1)}, u32[]{:S(2)}, u32[]{:S(2)}) collective-permute-start(f32[4,32,128]{2,1,0:T(8,128)S(1)} %get-tuple-element.51), channel_id=1, source_target_pairs={{97,160},{98,161},{99,162},{100,163},{101,164},{102,165},{103,166}... | collective-permute-start | bytes 196616 | tf_op jit(solution)/shard_map/ppermute | solution.py:354
  66.7 0.7 collective-permute-start.22
  68.0 18.7 %collective-permute-start.23 = (f32[4,32,128]{2,1,0:T(8,128)S(1)}, f32[4,32,128]{2,1,0:T(8,128)S(1)}, u32[]{:S(2)}, u32[]{:S(2)}) collective-permute-start(f32[4,32,128]{2,1,0:T(8,128)S(1)} %get-tuple-element.54), channel_id=1, source_target_pairs={{160,226},{161,227},{162,228},{163,229},{164,230},{165,231},{166,2... | collective-permute-start | bytes 196616 | tf_op jit(solution)/shard_map/ppermute | solution.py:354
  69.3 19.7 %collective-permute-start.24 = (f32[4,32,128]{2,1,0:T(8,128)S(1)}, f32[4,32,128]{2,1,0:T(8,128)S(1)}, u32[]{:S(2)}, u32[]{:S(2)}) collective-permute-start(f32[4,32,128]{2,1,0:T(8,128)S(1)} %get-tuple-element.54), channel_id=1, source_target_pairs={{160,225},{161,226},{162,227},{163,228},{164,229},{165,230},{166,2... | collective-permute-start | bytes 196616 | tf_op jit(solution)/shard_map/ppermute | solution.py:354
  70.6 18.4 %collective-permute-start.25 = (f32[4,32,128]{2,1,0:T(8,128)S(1)}, f32[4,32,128]{2,1,0:T(8,128)S(1)}, u32[]{:S(2)}, u32[]{:S(2)}) collective-permute-start(f32[4,32,128]{2,1,0:T(8,128)S(1)} %get-tuple-element.54), channel_id=1, source_target_pairs={{160,224},{161,225},{162,226},{163,227},{164,228},{165,229},{166,2... | collective-permute-start | bytes 196616 | tf_op jit(solution)/shard_map/ppermute | solution.py:354
  71.9 17.1 %collective-permute-start.26 = (f32[4,32,128]{2,1,0:T(8,128)S(1)}, f32[4,32,128]{2,1,0:T(8,128)S(1)}, u32[]{:S(2)}, u32[]{:S(2)}) collective-permute-start(f32[4,32,128]{2,1,0:T(8,128)S(1)} %get-tuple-element.54), channel_id=1, source_target_pairs={{161,224},{162,225},{163,226},{164,227},{165,228},{166,229},{167,2... | collective-permute-start | bytes 196616 | tf_op jit(solution)/shard_map/ppermute | solution.py:354
  73.2 15.9 %collective-permute-start.27 = (f32[4,32,128]{2,1,0:T(8,128)S(1)}, f32[4,32,128]{2,1,0:T(8,128)S(1)}, u32[]{:S(2)}, u32[]{:S(2)}) collective-permute-start(f32[4,32,128]{2,1,0:T(8,128)S(1)} %get-tuple-element.54), channel_id=1, source_target_pairs={{162,224},{163,225},{164,226},{165,227},{166,228},{167,229},{168,2... | collective-permute-start | bytes 196616 | tf_op jit(solution)/shard_map/ppermute | solution.py:354
  91.2 2.2 %collective-permute-start.28 = (f32[4,32,128]{2,1,0:T(8,128)S(1)}, f32[4,32,128]{2,1,0:T(8,128)S(1)}, u32[]{:S(2)}, u32[]{:S(2)}) collective-permute-start(f32[4,32,128]{2,1,0:T(8,128)S(1)} %get-tuple-element.58), channel_id=1, source_target_pairs={{96,64},{97,65},{98,66},{99,67},{100,68},{101,69},{102,70},{103,71... | collective-permute-start | bytes 196616 | tf_op jit(solution)/shard_map/ppermute | solution.py:354

commit v4 on v3

--- a/solution.py
+++ b/solution.py
@@ -86,7 +86,7 @@
     return 0.125 * jnp.concatenate(rows, axis=0)
 
 
-def prep_kernel(x_ref, even_ref, odd_ref, x, sems):
+def prep_kernel(x_ref, out_ref, x, sems):
     copies = [pltpu.make_async_copy(x_ref.at[0, p], x.at[p], sems.at[p]) for p in range(CZ)]
     for copy in copies:
         copy.start()
@@ -96,18 +96,13 @@
     for p in range(CZ):
         copies[p].wait()
         r = split_dot(x[p], m) * KAPPA
-        for out_ref in (even_ref, odd_ref):
-            for s in range(8):
-                for j in range(2):
-                    out_ref[p, j, pl.ds(s, 8, stride=8), :] = r[8 * s : 8 * s + 8, j * CY : (j + 1) * CY]
+        for s in range(8):
+            for j in range(2):
+                out_ref[p, j, pl.ds(s, 8, stride=8), :] = r[8 * s : 8 * s + 8, j * CY : (j + 1) * CY]
 
 
 def word_kernel(own_ref, out_ref):
     out_ref[...] = own_ref[0, 0, pl.ds(0, 8)]
-
-
-def gate_kernel(own_ref, word_ref, out_ref):
-    del own_ref, word_ref, out_ref
 
 
 def three(left, mid, right, n):
@@ -148,7 +143,9 @@
         get = lambda q, j: v[q, j]
 
 
-def fine_kernel(blocks, odd, place_ref, own, one, two, out_ref, v, v1):
+def fine_kernel(blocks, odd, place_ref, own, one, two, *refs):
+    out_ref, v, v1 = refs[-3:]
+
     def put(p, a, b):
         out_ref[p, 0] = a
         out_ref[p, 1] = b
@@ -160,7 +157,7 @@
 
 def last_fine_kernel(blocks, part, place_ref, own, one, two, co_ref, *refs):
     slab = place_ref[1]
-    mine = (slab % 2 == 0, slab == 1, (slab % 2 == 1) & (slab > 1))[part]
+    mine = (slab % 2 == 0, slab == 1, slab == 3, (slab % 2 == 1) & (slab > 3))[part]
     if part:
         out_ref, jump_ref, v, v1 = refs[-4:]
     else:
@@ -181,18 +178,18 @@
                 send_ref[q] = jnp.where(slab == 0, old + jump, jump)
 
 
-def coarse_kernel(blocks, place_ref, own0, one0, two0, own1, one1, two1, co_ref, cv, cv1):
+def coarse_kernel(blocks, place_ref, own, one0, two0, one1, two1, co_ref, cv, cv1):
     at, then = sides(place_ref[0], CC)
 
     def fill(ref, base):
         for q in range(CC):
             cv[base + q] = restricted(lambda p, j: ref[p, j], 2 * q)
 
-    for odd, own, one, two in ((0, own0, one0, two0), (1, own1, one1, two1)):
+    fill(own, CC)
+    for odd, one, two in ((0, one0, two0), (1, one1, two1)):
 
         @pl.when(place_ref[1] % 2 == odd)
         def _():
-            fill(own, CC)
             fill(one, at)
             fill(two, then)
 
@@ -203,7 +200,7 @@
 
 
 def first_sweep_kernel(
-    blocks, place_ref, left, mid, right, jump_ref, old_ref, out_ref, send_ref, wide_ref, cv, cv1
+    blocks, place_ref, mid, left, right, jump_ref, old_ref, out_ref, send_ref, wide_ref, cv, cv1
 ):
     at, then = sides(place_ref[0], CC)
 
@@ -235,7 +232,7 @@
 
 
 def sweep_kernel(
-    blocks, slab, place_ref, a0, a1, a2, a3, a4, wide_ref, jump_ref, old_ref, oldx_ref, *refs
+    blocks, slab, place_ref, a0, a4, a1, a3, a2, wide_ref, jump_ref, old_ref, oldx_ref, *refs
 ):
     out_ref, outx_ref, send_ref, cv, cv1 = refs[-5:]
 
@@ -259,6 +256,42 @@
     def _():
         out_ref[...] = old_ref[...]
         outx_ref[...] = oldx_ref[...]
+        send_ref[...] = jump_ref[...]
+
+
+def even_sweep_kernel(blocks, slab, place_ref, a0, a4, a1, a3, a2, oldx_ref, *refs):
+    outx_ref, next_ref, cv, cv1 = refs[-4:]
+
+    @pl.when(place_ref[1] == slab)
+    def _():
+        refs = (a0, a1, a2, a3, a4)
+        first = (place_ref[0] - 2) * CC
+        coarse_propagate(lambda p: refs[p // CC][p % CC], cv, cv1, 0, 5 * CC, first, blocks * CC)
+        for q in range(CC):
+            outx_ref[q] = cv[2 * CC + q]
+        for q in range(3 * CC):
+            next_ref[q] = cv[CC + q]
+
+    @pl.when(place_ref[1] != slab)
+    def _():
+        outx_ref[...] = oldx_ref[...]
+
+
+def odd_sweep_kernel(blocks, slab, place_ref, next_ref, wide_ref, jump_ref, old_ref, out_ref, send_ref, cv, cv1):
+    @pl.when(place_ref[1] == slab)
+    def _():
+        for q in range(3 * CC):
+            cv[q] = next_ref[q] + wide_ref[q]
+        first = (place_ref[0] - 1) * CC
+        coarse_propagate(lambda q: cv[q], cv, cv1, 0, 3 * CC, first, blocks * CC)
+        for q in range(CC):
+            new = cv[CC + q]
+            out_ref[q] = new
+            send_ref[q] = new + jump_ref[q]
+
+    @pl.when(place_ref[1] != slab)
+    def _():
+        out_ref[...] = old_ref[...]
         send_ref[...] = jump_ref[...]
 
 
@@ -360,22 +393,24 @@
     place = jnp.stack([lax.axis_index("gz"), lax.axis_index("tm")]).astype(jnp.int32)
     evens, odds = range(0, slabs, 2), range(1, slabs, 2)
     start_states = pltpu.with_memory_space_constraint(start_states, pltpu.HBM)
-    own, own1 = call(prep_kernel, (fine_shape,) * 2, [HB], (start_states,), WHOLE)
+    own = call(prep_kernel, fine_shape, [HB], (start_states,), WHOLE)
     near = both(own, evens)
     word_shape = jax.ShapeDtypeStruct((8, CY), jnp.float32)
     word = handed(call(word_kernel, word_shape, [VM], (own,)), [(k, k + 1) for k in evens])
-    own1 = call(gate_kernel, fine_shape, [VM] * 2, (own1, word), input_output_aliases={0: 0})
+    own1, word = lax.optimization_barrier((own, word))
     near1 = both(own1, odds)
     fine = [SM] + [VM] * 3
     mid = call(functools.partial(fine_kernel, blocks, 0), fine_shape, fine, (place, own, *near), FINE_WORK)
     next0 = both(mid, evens)
-    mid1 = call(functools.partial(fine_kernel, blocks, 1), fine_shape, fine, (place, own1, *near1), FINE_WORK)
+    mid1 = call(
+        functools.partial(fine_kernel, blocks, 1), fine_shape, fine + [HB], (place, own1, *near1, word), FINE_WORK
+    )
     next1 = both(mid1, odds)
     old = call(
         functools.partial(coarse_kernel, blocks),
         coarse_shape,
-        [SM] + [VM] * 6,
-        (place, own, *near, own1, *near1),
+        [SM] + [VM] * 5,
+        (place, own, *near, *near1),
         coarse_work(3),
     )
     fine_end, jump, send = call(
@@ -395,7 +430,7 @@
     )
     firsts = range(0, slabs - 1, 2)
     pairs = [(k, k + 1) for k in firsts if k != 2]
-    side = [handed(send, pairs, by, (2,) if by else ()) for by in (1, 0, -1)]
+    side = [handed(send, pairs, by, (2,) if by else ()) for by in (0, 1, -1)]
     wide_shape = jax.ShapeDtypeStruct((3 * CC, CX, CY), jnp.float32)
     picked, send, wide = call(
         functools.partial(first_sweep_kernel, blocks),
@@ -404,30 +439,52 @@
         (place, *side, jump, old),
         coarse_work(3),
     )
-    fine_end, jump = call(
-        functools.partial(last_fine_kernel, blocks, 2),
-        (fine_shape, coarse_shape),
-        [SM] + [VM] * 7,
-        (place, mid1, *next1, old, fine_end, jump, send),
-        FINE_WORK,
-        input_output_aliases={5: 0, 6: 1},
-    )
-    rest = call(rest_kernel, half_shape, [VM] * 2, (fine_end, old))
-    even = jump
+
+    def end_fine(part, *after):
+        return call(
+            functools.partial(last_fine_kernel, blocks, part),
+            (fine_shape, coarse_shape),
+            [SM] + [VM] * 6 + [HB] * len(after),
+            (place, mid1, *next1, old, fine_end, jump, *after),
+            FINE_WORK,
+            input_output_aliases={5: 0, 6: 1},
+        )
+
+    fine_end, jump = end_fine(2, send)
+    even = old
     for k in firsts[1:]:
+        if k == 4:
+            fine_end, jump = end_fine(3, send)
+            rest = call(rest_kernel, half_shape, [VM] * 2, (fine_end, old))
         early = (rest,) if k == firsts[-1] else ()
-        got = [handed(send, [(k - 1, k + 1)], by) for by in (2, 1, 0, -1, -2)]
+        got = [handed(send, [(k - 1, k + 1)], by) for by in (2, -2, 1, -1, 0)]
         near = wide
         if k == 2:
             near, jump, *got = lax.optimization_barrier((wide, jump, *got))
             near = handed(near, [(2, 3)])
-        picked, even, send = call(
-            functools.partial(sweep_kernel, blocks, k + 1),
-            (coarse_shape,) * 3,
-            [SM] + [VM] * 9 + [HB] * len(early),
-            (place, *got, near, jump, picked, even, *early),
-            coarse_work(5),
-        )
+        if k == 2:
+            even, state = call(
+                functools.partial(even_sweep_kernel, blocks, k + 1),
+                (coarse_shape, wide_shape),
+                [SM] + [VM] * 6 + [HB] * len(early),
+                (place, *got, even, *early),
+                coarse_work(5),
+            )
+            picked, send = call(
+                functools.partial(odd_sweep_kernel, blocks, k + 1),
+                (coarse_shape,) * 2,
+                [SM] + [VM] * 4,
+                (place, state, near, jump, picked),
+                coarse_work(3),
+            )
+        else:
+            picked, even, send = call(
+                functools.partial(sweep_kernel, blocks, k + 1),
+                (coarse_shape,) * 3,
+                [SM] + [VM] * 9 + [HB] * len(early),
+                (place, *got, near, jump, picked, even, *early),
+                coarse_work(5),
+            )
     even = handed(even, [(k + 1, k) for k in firsts[1:]])
     return call(
         final_kernel,

time: 97 us -> 92.7 us (0.956); the launches traced: 95.2 us -> 92.1 us
  waiting for transfers between devices: 39 us -> 34.9 us
  Pallas kernels: 19.8 us -> 20.8 us
    ppermute x21, waiting for transfers between devices: 30.1 us -> 26 us  [handed(): return lax.ppermute(array, ('tm', 'gz'), pairs)]
    pallas_call x15 -> x16, Pallas kernels: 19.8 us -> 20.8 us  [call(): pl.pallas_call(kernel, out_shape=out_shape, in_specs=in_specs, out_specs=...]
  transfers between devices with their start and end apart: 29 -> 29, of which waited for: 10 -> 8; matrix products, arithmetic and copies ran while one was open for 0% -> 0% of each run, Pallas kernels for 12% -> 13%
where the time goes in v4:
time: 92.7 us; the launch traced here: 92.1 us
  starting transfers between devices  35.8 us (39%)
  waiting for transfers between devices  34.9 us (38%)
  Pallas kernels  20.8 us (22%)
    ppermute x21, waiting for transfers between devices, handed(): return lax.ppermute(array, ('tm', 'gz'), pairs)  26 us
    pallas_call x16, Pallas kernels, call(): pl.pallas_call(kernel, out_shape=out_shape, in_specs=in_specs, out_specs=...  20.8 us
    ppermute x21, starting transfers between devices, handed(): return lax.ppermute(array, ('tm', 'gz'), pairs)  20.2 us
    ppermute x8, starting transfers between devices, both(): lax.ppermute(array, ('tm', 'gz'), pairs + [(j, i) for i, j in pairs])  15.5 us
    ppermute x8, waiting for transfers between devices, both(): lax.ppermute(array, ('tm', 'gz'), pairs + [(j, i) for i, j in pairs])  8.86 us
  transfers between devices with their start and end apart: 29, of which 8 were waited for; matrix products, arithmetic and copies ran while one was open for 0% of the time, Pallas kernels for 13%

profile of v4, /device:TPU:225, one launch (start us, length us, event | category | flops | bytes accessed | tf_op | source)
XLA Modules:
  0.0 92.1 jit_solution(11624834312537493668)
XLA Ops:
  0.0 2.8 %shard_map.17.own_ref.own = f32[8,2,64,128]{3,2,1,0:T(8,128)S(1)} custom-call(f32[1,8,64,256]{3,2,1,0:T(8,128)} %x_ref.1), custom_call_target="tpu_custom_call" | custom-call | tf_op jit(solution)/shard_map/pallas_call | solution.py:361
  4.2 1.3 %collective-permute-start = (f32[8,128]{1,0:T(8,128)S(1)}, f32[8,128]{1,0:T(8,128)S(1)}, u32[]{:S(2)}, u32[]{:S(2)}) collective-permute-start(f32[8,128]{1,0:T(8,128)S(1)} %shard_map.18), channel_id=1, source_target_pairs={{0,32},{1,33},{2,34},{3,35},{4,36},{5,37},{6,38},{7,39},{8,40},{9,... | collective-permute-start | bytes 12296 | tf_op jit(solution)/shard_map/ppermute | solution.py:387
  5.5 9.4 %collective-permute-done.refs_0_ = f32[8,128]{1,0:T(8,128)S(1)} collective-permute-done((f32[8,128]{1,0:T(8,128)S(1)}, f32[8,128]{1,0:T(8,128)S(1)}, u32[]{:S(2)}, u32[]{:S(2)}) %collective-permute-start) | collective-permute-done | bytes 4128 | tf_op jit(solution)/shard_map/ppermute | solution.py:387
  14.9 2.8 %collective-permute-start.1 = (f32[8,2,64,128]{3,2,1,0:T(8,128)S(1)}, f32[8,2,64,128]{3,2,1,0:T(8,128)S(1)}, u32[]{:S(2)}, u32[]{:S(2)}) collective-permute-start(f32[8,2,64,128]{3,2,1,0:T(8,128)S(1)} %shard_map.17.own_ref.own), channel_id=1, source_target_pairs={{33,34},{35,36},{37,38},{39,40},{41,42},{43,44},{45,46},{47,48},{4... | collective-permute-start | bytes 1572872 | tf_op jit(solution)/shard_map/ppermute | solution.py:377
  17.7 2.8 %collective-permute-start.2 = (f32[8,2,64,128]{3,2,1,0:T(8,128)S(1)}, f32[8,2,64,128]{3,2,1,0:T(8,128)S(1)}, u32[]{:S(2)}, u32[]{:S(2)}) collective-permute-start(f32[8,2,64,128]{3,2,1,0:T(8,128)S(1)} %shard_map.17.own_ref.own), channel_id=1, source_target_pairs={{32,33},{34,35},{36,37},{38,39},{40,41},{42,43},{44,45},{46,47},{4... | collective-permute-start | bytes 1572872 | tf_op jit(solution)/shard_map/ppermute | solution.py:377
  21.1 0.7 collective-permute-start.7
  22.6 6.5 %collective-permute-done.1.one.one1 = f32[8,2,64,128]{3,2,1,0:T(8,128)S(1)} collective-permute-done((f32[8,2,64,128]{3,2,1,0:T(8,128)S(1)}, f32[8,2,64,128]{3,2,1,0:T(8,128)S(1)}, u32[]{:S(2)}, u32[]{:S(2)}) %collective-permute-start.1) | collective-permute-done | bytes 524320 | tf_op jit(solution)/shard_map/ppermute | solution.py:377
  29.1 3.7 %shard_map.19.own = f32[8,2,64,128]{3,2,1,0:T(8,128)S(1)} custom-call(s32[2]{0:T(128)S(1)} %pad_add_fusion.place_ref, f32[8,2,64,128]{3,2,1,0:T(8,128)S(1)} %shard_map.17.own_ref.own, f32[8,2,64,128]{3,2,1,0:T(8,128)S(1)} %collective-permute-done.1.one.one1, f32[8,2,64,128]{3,2,1,0:T(8,128)S(1)} %collective-permute-done.2.two.two1, ...), custom_call_target="tpu_custom_call" | custom-call | tf_op jit(solution)/shard_map/pallas_call | solution.py:361
  32.8 5.3 %collective-permute-start.3 = (f32[8,2,64,128]{3,2,1,0:T(8,128)S(1)}, f32[8,2,64,128]{3,2,1,0:T(8,128)S(1)}, u32[]{:S(2)}, u32[]{:S(2)}) collective-permute-start(f32[8,2,64,128]{3,2,1,0:T(8,128)S(1)} %shard_map.19.own), channel_id=1, source_target_pairs={{33,34},{35,36},{37,38},{39,40},{41,42},{43,44},{45,46},{47,48},{4... | collective-permute-start | bytes 1572872 | tf_op jit(solution)/shard_map/ppermute | solution.py:377
  38.1 1.9 %collective-permute-start.4 = (f32[8,2,64,128]{3,2,1,0:T(8,128)S(1)}, f32[8,2,64,128]{3,2,1,0:T(8,128)S(1)}, u32[]{:S(2)}, u32[]{:S(2)}) collective-permute-start(f32[8,2,64,128]{3,2,1,0:T(8,128)S(1)} %shard_map.19.own), channel_id=1, source_target_pairs={{32,33},{34,35},{36,37},{38,39},{40,41},{42,43},{44,45},{46,47},{4... | collective-permute-start | bytes 1572872 | tf_op jit(solution)/shard_map/ppermute | solution.py:377
  40.0 1.0 %shard_map.20.co_ref.old_ref.oldx_ref = f32[4,32,128]{2,1,0:T(8,128)S(1)} custom-call(s32[2]{0:T(128)S(1)} %pad_add_fusion.place_ref, f32[8,2,64,128]{3,2,1,0:T(8,128)S(1)} %shard_map.17.own_ref.own, f32[8,2,64,128]{3,2,1,0:T(8,128)S(1)} %collective-permute-done.5.one0.one, f32[8,2,64,128]{3,2,1,0:T(8,128)S(1)} %collective-permute-done.6.two0.two, ...), custom_call_target="tpu_custom_call" | custom-call | tf_op jit(solution)/shard_map/pallas_call | solution.py:361
  41.1 0.7 shard_map.22
  41.8 1.3 %collective-permute-start.10 = (f32[4,32,128]{2,1,0:T(8,128)S(1)}, f32[4,32,128]{2,1,0:T(8,128)S(1)}, u32[]{:S(2)}, u32[]{:S(2)}) collective-permute-start(f32[4,32,128]{2,1,0:T(8,128)S(1)} %get-tuple-element.41), channel_id=1, source_target_pairs={{0,33},{1,34},{2,35},{3,36},{4,37},{5,38},{6,39},{7,40},{8,41},{9,... | collective-permute-start | bytes 196616 | tf_op jit(solution)/shard_map/ppermute | solution.py:387
  43.1 1.3 %collective-permute-start.11 = (f32[4,32,128]{2,1,0:T(8,128)S(1)}, f32[4,32,128]{2,1,0:T(8,128)S(1)}, u32[]{:S(2)}, u32[]{:S(2)}) collective-permute-start(f32[4,32,128]{2,1,0:T(8,128)S(1)} %get-tuple-element.41), channel_id=1, source_target_pairs={{1,32},{2,33},{3,34},{4,35},{5,36},{6,37},{7,38},{8,39},{9,40},{10... | collective-permute-start | bytes 196616 | tf_op jit(solution)/shard_map/ppermute | solution.py:387
  44.4 1.3 %collective-permute-start.9 = (f32[4,32,128]{2,1,0:T(8,128)S(1)}, f32[4,32,128]{2,1,0:T(8,128)S(1)}, u32[]{:S(2)}, u32[]{:S(2)}) collective-permute-start(f32[4,32,128]{2,1,0:T(8,128)S(1)} %get-tuple-element.41), channel_id=1, source_target_pairs={{0,32},{1,33},{2,34},{3,35},{4,36},{5,37},{6,38},{7,39},{8,40},{9,... | collective-permute-start | bytes 196616 | tf_op jit(solution)/shard_map/ppermute | solution.py:387
  45.7 1.3 %collective-permute-done.3.one = f32[8,2,64,128]{3,2,1,0:T(8,128)S(1)} collective-permute-done((f32[8,2,64,128]{3,2,1,0:T(8,128)S(1)}, f32[8,2,64,128]{3,2,1,0:T(8,128)S(1)}, u32[]{:S(2)}, u32[]{:S(2)}) %collective-permute-start.3) | collective-permute-done | bytes 524320 | tf_op jit(solution)/shard_map/ppermute | solution.py:377
  47.0 1.1 %collective-permute-done.4.two = f32[8,2,64,128]{3,2,1,0:T(8,128)S(1)} collective-permute-done((f32[8,2,64,128]{3,2,1,0:T(8,128)S(1)}, f32[8,2,64,128]{3,2,1,0:T(8,128)S(1)}, u32[]{:S(2)}, u32[]{:S(2)}) %collective-permute-start.4) | collective-permute-done | bytes 524320 | tf_op jit(solution)/shard_map/ppermute | solution.py:377
  48.6 3.4 %collective-permute-done.10.left = f32[4,32,128]{2,1,0:T(8,128)S(1)} collective-permute-done((f32[4,32,128]{2,1,0:T(8,128)S(1)}, f32[4,32,128]{2,1,0:T(8,128)S(1)}, u32[]{:S(2)}, u32[]{:S(2)}) %collective-permute-start.10) | collective-permute-done | bytes 65568 | tf_op jit(solution)/shard_map/ppermute | solution.py:387
  57.8 0.8 shard_map.27
  62.0 3.8 %shard_map.28 = (f32[8,2,64,128]{3,2,1,0:T(8,128)S(1)}, f32[4,32,128]{2,1,0:T(8,128)S(1)}) custom-call(s32[2]{0:T(128)S(1)} %pad_add_fusion.place_ref, f32[8,2,64,128]{3,2,1,0:T(8,128)S(1)} %shard_map.19.own, f32[8,2,64,128]{3,2,1,0:T(8,128)S(1)} %collective-permute-done.3.one, ...), custom_call_target="tpu_custom_call", output_to_operand_aliasing={{0}: (5, {}), {1}: (6, {})} | custom-call | tf_op jit(solution)/shard_map/pallas_call | solution.py:361
  66.4 1.3 %collective-permute-start.23 = (f32[4,32,128]{2,1,0:T(8,128)S(1)}, f32[4,32,128]{2,1,0:T(8,128)S(1)}, u32[]{:S(2)}, u32[]{:S(2)}) collective-permute-start(f32[4,32,128]{2,1,0:T(8,128)S(1)} %get-tuple-element.60), channel_id=1, source_target_pairs={{160,226},{161,227},{162,228},{163,229},{164,230},{165,231},{166,2... | collective-permute-start | bytes 196616 | tf_op jit(solution)/shard_map/ppermute | solution.py:387
  67.7 1.3 %collective-permute-start.24 = (f32[4,32,128]{2,1,0:T(8,128)S(1)}, f32[4,32,128]{2,1,0:T(8,128)S(1)}, u32[]{:S(2)}, u32[]{:S(2)}) collective-permute-start(f32[4,32,128]{2,1,0:T(8,128)S(1)} %get-tuple-element.60), channel_id=1, source_target_pairs={{162,224},{163,225},{164,226},{165,227},{166,228},{167,229},{168,2... | collective-permute-start | bytes 196616 | tf_op jit(solution)/shard_map/ppermute | solution.py:387
  69.0 1.3 %collective-permute-start.25 = (f32[4,32,128]{2,1,0:T(8,128)S(1)}, f32[4,32,128]{2,1,0:T(8,128)S(1)}, u32[]{:S(2)}, u32[]{:S(2)}) collective-permute-start(f32[4,32,128]{2,1,0:T(8,128)S(1)} %get-tuple-element.60), channel_id=1, source_target_pairs={{160,225},{161,226},{162,227},{163,228},{164,229},{165,230},{166,2... | collective-permute-start | bytes 196616 | tf_op jit(solution)/shard_map/ppermute | solution.py:387
  70.3 1.3 %collective-permute-start.26 = (f32[4,32,128]{2,1,0:T(8,128)S(1)}, f32[4,32,128]{2,1,0:T(8,128)S(1)}, u32[]{:S(2)}, u32[]{:S(2)}) collective-permute-start(f32[4,32,128]{2,1,0:T(8,128)S(1)} %get-tuple-element.60), channel_id=1, source_target_pairs={{161,224},{162,225},{163,226},{164,227},{165,228},{166,229},{167,2... | collective-permute-start | bytes 196616 | tf_op jit(solution)/shard_map/ppermute | solution.py:387
  71.6 1.3 %collective-permute-start.27 = (f32[4,32,128]{2,1,0:T(8,128)S(1)}, f32[4,32,128]{2,1,0:T(8,128)S(1)}, u32[]{:S(2)}, u32[]{:S(2)}) collective-permute-start(f32[4,32,128]{2,1,0:T(8,128)S(1)} %get-tuple-element.60), channel_id=1, source_target_pairs={{160,224},{161,225},{162,226},{163,227},{164,228},{165,229},{166,2... | collective-permute-start | bytes 196616 | tf_op jit(solution)/shard_map/ppermute | solution.py:387
  72.9 0.7 shard_map.29.refs_0_.rest_ref
  73.7 10.3 %collective-permute-done.23.a0 = f32[4,32,128]{2,1,0:T(8,128)S(1)} collective-permute-done((f32[4,32,128]{2,1,0:T(8,128)S(1)}, f32[4,32,128]{2,1,0:T(8,128)S(1)}, u32[]{:S(2)}, u32[]{:S(2)}) %collective-permute-start.23) | collective-permute-done | bytes 65568 | tf_op jit(solution)/shard_map/ppermute | solution.py:387
  84.0 2.0 %collective-permute-done.25.a1 = f32[4,32,128]{2,1,0:T(8,128)S(1)} collective-permute-done((f32[4,32,128]{2,1,0:T(8,128)S(1)}, f32[4,32,128]{2,1,0:T(8,128)S(1)}, u32[]{:S(2)}, u32[]{:S(2)}) %collective-permute-start.25) | collective-permute-done | bytes 65568 | tf_op jit(solution)/shard_map/ppermute | solution.py:387
  86.0 2.1 %shard_map.31 = (f32[4,32,128]{2,1,0:T(8,128)S(1)}, f32[4,32,128]{2,1,0:T(8,128)S(1)}, f32[4,32,128]{2,1,0:T(8,128)}) custom-call(s32[2]{0:T(128)S(1)} %pad_add_fusion.place_ref, f32[4,32,128]{2,1,0:T(8,128)S(1)} %collective-permute-done.23.a0, f32[4,32,128]{2,1,0:T(8,128)S(1)} %collective-permute-done.24.a4, f32[4,32,128]{2,1,0:T(8,128)S(1)} %collective-permute-done.25.a1, ...), custom_call_target="tpu_custom_call" | custom-call | tf_op jit(solution)/shard_map/pallas_call | solution.py:361
  88.1 1.3 %collective-permute-start.28 = (f32[4,32,128]{2,1,0:T(8,128)S(1)}, f32[4,32,128]{2,1,0:T(8,128)S(1)}, u32[]{:S(2)}, u32[]{:S(2)}) collective-permute-start(f32[4,32,128]{2,1,0:T(8,128)S(1)} %get-tuple-element.64), channel_id=1, source_target_pairs={{96,64},{97,65},{98,66},{99,67},{100,68},{101,69},{102,70},{103,71... | collective-permute-start | bytes 196616 | tf_op jit(solution)/shard_map/ppermute | solution.py:387
  89.4 0.9 collective-permute-done.28.even_ref
  90.3 1.7 %shard_map.32 = f32[1,8,64,256]{3,2,1,0:T(8,128)} custom-call(s32[2]{0:T(128)S(1)} %pad_add_fusion.place_ref, f32[2,8,64,128]{3,2,1,0:T(8,128)S(1)} %shard_map.29.refs_0_.rest_ref, f32[4,32,128]{2,1,0:T(8,128)S(1)} %get-tuple-element.63.picked_ref, f32[4,32,128]{2,1,0:T(8,128)S(1)} %collective-permute-done.28.even_ref), custom_call_target="tpu_custom_call" | custom-call | tf_op jit(solution)/shard_map/pallas_call | solution.py:361
  (43 shorter events, 12.9 us)
Async XLA Ops:
  2.8 17.8 %collective-permute-start.5 = (f32[8,2,64,128]{3,2,1,0:T(8,128)S(1)}, f32[8,2,64,128]{3,2,1,0:T(8,128)S(1)}, u32[]{:S(2)}, u32[]{:S(2)}) collective-permute-start(f32[8,2,64,128]{3,2,1,0:T(8,128)S(1)} %shard_map.17.own_ref.own), channel_id=1, source_target_pairs={{1,2},{3,4},{5,6},{7,8},{9,10},{11,12},{13,14},{15,16},{17,18},{19... | collective-permute-start | bytes 1572872 | tf_op jit(solution)/shard_map/ppermute | solution.py:377
  3.5 17.1 %collective-permute-start.6 = (f32[8,2,64,128]{3,2,1,0:T(8,128)S(1)}, f32[8,2,64,128]{3,2,1,0:T(8,128)S(1)}, u32[]{:S(2)}, u32[]{:S(2)}) collective-permute-start(f32[8,2,64,128]{3,2,1,0:T(8,128)S(1)} %shard_map.17.own_ref.own), channel_id=1, source_target_pairs={{0,1},{2,3},{4,5},{6,7},{8,9},{10,11},{12,13},{14,15},{16,17},{18,... | collective-permute-start | bytes 1572872 | tf_op jit(solution)/shard_map/ppermute | solution.py:377
  4.2 10.7 %collective-permute-start = (f32[8,128]{1,0:T(8,128)S(1)}, f32[8,128]{1,0:T(8,128)S(1)}, u32[]{:S(2)}, u32[]{:S(2)}) collective-permute-start(f32[8,128]{1,0:T(8,128)S(1)} %shard_map.18), channel_id=1, source_target_pairs={{0,32},{1,33},{2,34},{3,35},{4,36},{5,37},{6,38},{7,39},{8,40},{9,... | collective-permute-start | bytes 12296 | tf_op jit(solution)/shard_map/ppermute | solution.py:387
  14.9 14.1 %collective-permute-start.1 = (f32[8,2,64,128]{3,2,1,0:T(8,128)S(1)}, f32[8,2,64,128]{3,2,1,0:T(8,128)S(1)}, u32[]{:S(2)}, u32[]{:S(2)}) collective-permute-start(f32[8,2,64,128]{3,2,1,0:T(8,128)S(1)} %shard_map.17.own_ref.own), channel_id=1, source_target_pairs={{33,34},{35,36},{37,38},{39,40},{41,42},{43,44},{45,46},{47,48},{4... | collective-permute-start | bytes 1572872 | tf_op jit(solution)/shard_map/ppermute | solution.py:377
  17.7 11.3 %collective-permute-start.2 = (f32[8,2,64,128]{3,2,1,0:T(8,128)S(1)}, f32[8,2,64,128]{3,2,1,0:T(8,128)S(1)}, u32[]{:S(2)}, u32[]{:S(2)}) collective-permute-start(f32[8,2,64,128]{3,2,1,0:T(8,128)S(1)} %shard_map.17.own_ref.own), channel_id=1, source_target_pairs={{32,33},{34,35},{36,37},{38,39},{40,41},{42,43},{44,45},{46,47},{4... | collective-permute-start | bytes 1572872 | tf_op jit(solution)/shard_map/ppermute | solution.py:377
  21.1 19.9 %collective-permute-start.7 = (f32[8,2,64,128]{3,2,1,0:T(8,128)S(1)}, f32[8,2,64,128]{3,2,1,0:T(8,128)S(1)}, u32[]{:S(2)}, u32[]{:S(2)}) collective-permute-start(f32[8,2,64,128]{3,2,1,0:T(8,128)S(1)} %shard_map.21.own), channel_id=1, source_target_pairs={{1,2},{3,4},{5,6},{7,8},{9,10},{11,12},{13,14},{15,16},{17,18},{19... | collective-permute-start | bytes 1572872 | tf_op jit(solution)/shard_map/ppermute | solution.py:377
  21.8 19.2 %collective-permute-start.8 = (f32[8,2,64,128]{3,2,1,0:T(8,128)S(1)}, f32[8,2,64,128]{3,2,1,0:T(8,128)S(1)}, u32[]{:S(2)}, u32[]{:S(2)}) collective-permute-start(f32[8,2,64,128]{3,2,1,0:T(8,128)S(1)} %shard_map.21.own), channel_id=1, source_target_pairs={{0,1},{2,3},{4,5},{6,7},{8,9},{10,11},{12,13},{14,15},{16,17},{18,... | collective-permute-start | bytes 1572872 | tf_op jit(solution)/shard_map/ppermute | solution.py:377
  32.8 14.1 %collective-permute-start.3 = (f32[8,2,64,128]{3,2,1,0:T(8,128)S(1)}, f32[8,2,64,128]{3,2,1,0:T(8,128)S(1)}, u32[]{:S(2)}, u32[]{:S(2)}) collective-permute-start(f32[8,2,64,128]{3,2,1,0:T(8,128)S(1)} %shard_map.19.own), channel_id=1, source_target_pairs={{33,34},{35,36},{37,38},{39,40},{41,42},{43,44},{45,46},{47,48},{4... | collective-permute-start | bytes 1572872 | tf_op jit(solution)/shard_map/ppermute | solution.py:377
  38.1 9.9 %collective-permute-start.4 = (f32[8,2,64,128]{3,2,1,0:T(8,128)S(1)}, f32[8,2,64,128]{3,2,1,0:T(8,128)S(1)}, u32[]{:S(2)}, u32[]{:S(2)}) collective-permute-start(f32[8,2,64,128]{3,2,1,0:T(8,128)S(1)} %shard_map.19.own), channel_id=1, source_target_pairs={{32,33},{34,35},{36,37},{38,39},{40,41},{42,43},{44,45},{46,47},{4... | collective-permute-start | bytes 1572872 | tf_op jit(solution)/shard_map/ppermute | solution.py:377
  41.8 10.2 %collective-permute-start.10 = (f32[4,32,128]{2,1,0:T(8,128)S(1)}, f32[4,32,128]{2,1,0:T(8,128)S(1)}, u32[]{:S(2)}, u32[]{:S(2)}) collective-permute-start(f32[4,32,128]{2,1,0:T(8,128)S(1)} %get-tuple-element.41), channel_id=1, source_target_pairs={{0,33},{1,34},{2,35},{3,36},{4,37},{5,38},{6,39},{7,40},{8,41},{9,... | collective-permute-start | bytes 196616 | tf_op jit(solution)/shard_map/ppermute | solution.py:387
  43.1 8.9 %collective-permute-start.11 = (f32[4,32,128]{2,1,0:T(8,128)S(1)}, f32[4,32,128]{2,1,0:T(8,128)S(1)}, u32[]{:S(2)}, u32[]{:S(2)}) collective-permute-start(f32[4,32,128]{2,1,0:T(8,128)S(1)} %get-tuple-element.41), channel_id=1, source_target_pairs={{1,32},{2,33},{3,34},{4,35},{5,36},{6,37},{7,38},{8,39},{9,40},{10... | collective-permute-start | bytes 196616 | tf_op jit(solution)/shard_map/ppermute | solution.py:387
  44.4 7.6 %collective-permute-start.9 = (f32[4,32,128]{2,1,0:T(8,128)S(1)}, f32[4,32,128]{2,1,0:T(8,128)S(1)}, u32[]{:S(2)}, u32[]{:S(2)}) collective-permute-start(f32[4,32,128]{2,1,0:T(8,128)S(1)} %get-tuple-element.41), channel_id=1, source_target_pairs={{0,32},{1,33},{2,34},{3,35},{4,36},{5,37},{6,38},{7,39},{8,40},{9,... | collective-permute-start | bytes 196616 | tf_op jit(solution)/shard_map/ppermute | solution.py:387
  52.6 3.9 %collective-permute-start.12 = (f32[4,32,128]{2,1,0:T(8,128)S(1)}, f32[4,32,128]{2,1,0:T(8,128)S(1)}, u32[]{:S(2)}, u32[]{:S(2)}) collective-permute-start(f32[4,32,128]{2,1,0:T(8,128)S(1)} %get-tuple-element.42.refs_2_), channel_id=1, source_target_pairs={{32,98},{33,99},{34,100},{35,101},{36,102},{37,103},{38,104},{39,1... | collective-permute-start | bytes 196616 | tf_op jit(solution)/shard_map/ppermute | solution.py:387
  53.2 3.3 %collective-permute-start.13 = (f32[4,32,128]{2,1,0:T(8,128)S(1)}, f32[4,32,128]{2,1,0:T(8,128)S(1)}, u32[]{:S(2)}, u32[]{:S(2)}) collective-permute-start(f32[4,32,128]{2,1,0:T(8,128)S(1)} %get-tuple-element.42.refs_2_), channel_id=1, source_target_pairs={{34,96},{35,97},{36,98},{37,99},{38,100},{39,101},{40,102},{41,103... | collective-permute-start | bytes 196616 | tf_op jit(solution)/shard_map/ppermute | solution.py:387
  53.9 2.6 %collective-permute-start.14 = (f32[4,32,128]{2,1,0:T(8,128)S(1)}, f32[4,32,128]{2,1,0:T(8,128)S(1)}, u32[]{:S(2)}, u32[]{:S(2)}) collective-permute-start(f32[4,32,128]{2,1,0:T(8,128)S(1)} %get-tuple-element.42.refs_2_), channel_id=1, source_target_pairs={{32,97},{33,98},{34,99},{35,100},{36,101},{37,102},{38,103},{39,10... | collective-permute-start | bytes 196616 | tf_op jit(solution)/shard_map/ppermute | solution.py:387
  54.6 1.9 %collective-permute-start.15 = (f32[4,32,128]{2,1,0:T(8,128)S(1)}, f32[4,32,128]{2,1,0:T(8,128)S(1)}, u32[]{:S(2)}, u32[]{:S(2)}) collective-permute-start(f32[4,32,128]{2,1,0:T(8,128)S(1)} %get-tuple-element.42.refs_2_), channel_id=1, source_target_pairs={{33,96},{34,97},{35,98},{36,99},{37,100},{38,101},{39,102},{40,103... | collective-permute-start | bytes 196616 | tf_op jit(solution)/shard_map/ppermute | solution.py:387
  55.3 1.3 %collective-permute-start.16 = (f32[4,32,128]{2,1,0:T(8,128)S(1)}, f32[4,32,128]{2,1,0:T(8,128)S(1)}, u32[]{:S(2)}, u32[]{:S(2)}) collective-permute-start(f32[4,32,128]{2,1,0:T(8,128)S(1)} %get-tuple-element.42.refs_2_), channel_id=1, source_target_pairs={{32,96},{33,97},{34,98},{35,99},{36,100},{37,101},{38,102},{39,103... | collective-permute-start | bytes 196616 | tf_op jit(solution)/shard_map/ppermute | solution.py:387
  56.5 1.3 %collective-permute-start.17 = (f32[12,32,128]{2,1,0:T(8,128)S(1)}, f32[12,32,128]{2,1,0:T(8,128)S(1)}, u32[]{:S(2)}, u32[]{:S(2)}) collective-permute-start(f32[12,32,128]{2,1,0:T(8,128)S(1)} %get-tuple-element.53.wide_ref), channel_id=1, source_target_pairs={{64,96},{65,97},{66,98},{67,99},{68,100},{69,101},{70,102},{71,103... | collective-permute-start | bytes 589832 | tf_op jit(solution)/shard_map/ppermute | solution.py:387
  58.6 7.2 %collective-permute-start.18 = (f32[4,32,128]{2,1,0:T(8,128)S(1)}, f32[4,32,128]{2,1,0:T(8,128)S(1)}, u32[]{:S(2)}, u32[]{:S(2)}) collective-permute-start(f32[4,32,128]{2,1,0:T(8,128)S(1)} %get-tuple-element.55.refs_2_), channel_id=1, source_target_pairs={{96,162},{97,163},{98,164},{99,165},{100,166},{101,167},{102,168},... | collective-permute-start | bytes 196616 | tf_op jit(solution)/shard_map/ppermute | solution.py:387
  59.3 6.6 %collective-permute-start.19 = (f32[4,32,128]{2,1,0:T(8,128)S(1)}, f32[4,32,128]{2,1,0:T(8,128)S(1)}, u32[]{:S(2)}, u32[]{:S(2)}) collective-permute-start(f32[4,32,128]{2,1,0:T(8,128)S(1)} %get-tuple-element.55.refs_2_), channel_id=1, source_target_pairs={{98,160},{99,161},{100,162},{101,163},{102,164},{103,165},{104,166... | collective-permute-start | bytes 196616 | tf_op jit(solution)/shard_map/ppermute | solution.py:387
  59.9 5.9 %collective-permute-start.20 = (f32[4,32,128]{2,1,0:T(8,128)S(1)}, f32[4,32,128]{2,1,0:T(8,128)S(1)}, u32[]{:S(2)}, u32[]{:S(2)}) collective-permute-start(f32[4,32,128]{2,1,0:T(8,128)S(1)} %get-tuple-element.55.refs_2_), channel_id=1, source_target_pairs={{96,161},{97,162},{98,163},{99,164},{100,165},{101,166},{102,167},... | collective-permute-start | bytes 196616 | tf_op jit(solution)/shard_map/ppermute | solution.py:387
  60.6 5.2 %collective-permute-start.21 = (f32[4,32,128]{2,1,0:T(8,128)S(1)}, f32[4,32,128]{2,1,0:T(8,128)S(1)}, u32[]{:S(2)}, u32[]{:S(2)}) collective-permute-start(f32[4,32,128]{2,1,0:T(8,128)S(1)} %get-tuple-element.55.refs_2_), channel_id=1, source_target_pairs={{97,160},{98,161},{99,162},{100,163},{101,164},{102,165},{103,166}... | collective-permute-start | bytes 196616 | tf_op jit(solution)/shard_map/ppermute | solution.py:387
  61.3 4.6 %collective-permute-start.22 = (f32[4,32,128]{2,1,0:T(8,128)S(1)}, f32[4,32,128]{2,1,0:T(8,128)S(1)}, u32[]{:S(2)}, u32[]{:S(2)}) collective-permute-start(f32[4,32,128]{2,1,0:T(8,128)S(1)} %get-tuple-element.55.refs_2_), channel_id=1, source_target_pairs={{96,160},{97,161},{98,162},{99,163},{100,164},{101,165},{102,166},... | collective-permute-start | bytes 196616 | tf_op jit(solution)/shard_map/ppermute | solution.py:387
  66.4 17.6 %collective-permute-start.23 = (f32[4,32,128]{2,1,0:T(8,128)S(1)}, f32[4,32,128]{2,1,0:T(8,128)S(1)}, u32[]{:S(2)}, u32[]{:S(2)}) collective-permute-start(f32[4,32,128]{2,1,0:T(8,128)S(1)} %get-tuple-element.60), channel_id=1, source_target_pairs={{160,226},{161,227},{162,228},{163,229},{164,230},{165,231},{166,2... | collective-permute-start | bytes 196616 | tf_op jit(solution)/shard_map/ppermute | solution.py:387
  67.7 16.3 %collective-permute-start.24 = (f32[4,32,128]{2,1,0:T(8,128)S(1)}, f32[4,32,128]{2,1,0:T(8,128)S(1)}, u32[]{:S(2)}, u32[]{:S(2)}) collective-permute-start(f32[4,32,128]{2,1,0:T(8,128)S(1)} %get-tuple-element.60), channel_id=1, source_target_pairs={{162,224},{163,225},{164,226},{165,227},{166,228},{167,229},{168,2... | collective-permute-start | bytes 196616 | tf_op jit(solution)/shard_map/ppermute | solution.py:387
  69.0 16.9 %collective-permute-start.25 = (f32[4,32,128]{2,1,0:T(8,128)S(1)}, f32[4,32,128]{2,1,0:T(8,128)S(1)}, u32[]{:S(2)}, u32[]{:S(2)}) collective-permute-start(f32[4,32,128]{2,1,0:T(8,128)S(1)} %get-tuple-element.60), channel_id=1, source_target_pairs={{160,225},{161,226},{162,227},{163,228},{164,229},{165,230},{166,2... | collective-permute-start | bytes 196616 | tf_op jit(solution)/shard_map/ppermute | solution.py:387
  70.3 15.6 %collective-permute-start.26 = (f32[4,32,128]{2,1,0:T(8,128)S(1)}, f32[4,32,128]{2,1,0:T(8,128)S(1)}, u32[]{:S(2)}, u32[]{:S(2)}) collective-permute-start(f32[4,32,128]{2,1,0:T(8,128)S(1)} %get-tuple-element.60), channel_id=1, source_target_pairs={{161,224},{162,225},{163,226},{164,227},{165,228},{166,229},{167,2... | collective-permute-start | bytes 196616 | tf_op jit(solution)/shard_map/ppermute | solution.py:387
  71.6 14.3 %collective-permute-start.27 = (f32[4,32,128]{2,1,0:T(8,128)S(1)}, f32[4,32,128]{2,1,0:T(8,128)S(1)}, u32[]{:S(2)}, u32[]{:S(2)}) collective-permute-start(f32[4,32,128]{2,1,0:T(8,128)S(1)} %get-tuple-element.60), channel_id=1, source_target_pairs={{160,224},{161,225},{162,226},{163,227},{164,228},{165,229},{166,2... | collective-permute-start | bytes 196616 | tf_op jit(solution)/shard_map/ppermute | solution.py:387
  88.1 2.2 %collective-permute-start.28 = (f32[4,32,128]{2,1,0:T(8,128)S(1)}, f32[4,32,128]{2,1,0:T(8,128)S(1)}, u32[]{:S(2)}, u32[]{:S(2)}) collective-permute-start(f32[4,32,128]{2,1,0:T(8,128)S(1)} %get-tuple-element.64), channel_id=1, source_target_pairs={{96,64},{97,65},{98,66},{99,67},{100,68},{101,69},{102,70},{103,71... | collective-permute-start | bytes 196616 | tf_op jit(solution)/shard_map/ppermute | solution.py:387

commit v5 on v4

--- a/solution.py
+++ b/solution.py
@@ -478,13 +478,15 @@
                 coarse_work(3),
             )
         else:
-            picked, even, send = call(
+            more = k != firsts[-1]
+            picked, even, *rests = call(
                 functools.partial(sweep_kernel, blocks, k + 1),
-                (coarse_shape,) * 3,
+                (coarse_shape,) * (2 + more),
                 [SM] + [VM] * 9 + [HB] * len(early),
                 (place, *got, near, jump, picked, even, *early),
-                coarse_work(5),
+                coarse_work(1)[: 1 - more] + coarse_work(5),
             )
+            send = rests[0] if more else None
     even = handed(even, [(k + 1, k) for k in firsts[1:]])
     return call(
         final_kernel,

time: 92.7 us -> 92.1 us (level)
  no operation moved by 1% of the time
where the time goes in v5:
time: 92.1 us; the launch traced here: 91.5 us
  starting transfers between devices  35.8 us (39%)
  waiting for transfers between devices  34.9 us (38%)
  Pallas kernels  20.2 us (22%)
    ppermute x21, waiting for transfers between devices, handed(): return lax.ppermute(array, ('tm', 'gz'), pairs)  26 us
    ppermute x21, starting transfers between devices, handed(): return lax.ppermute(array, ('tm', 'gz'), pairs)  20.2 us
    pallas_call x16, Pallas kernels, call(): pl.pallas_call(kernel, out_shape=out_shape, in_specs=in_specs, out_specs=...  20.2 us
    ppermute x8, starting transfers between devices, both(): lax.ppermute(array, ('tm', 'gz'), pairs + [(j, i) for i, j in pairs])  15.5 us
    ppermute x8, waiting for transfers between devices, both(): lax.ppermute(array, ('tm', 'gz'), pairs + [(j, i) for i, j in pairs])  8.86 us
  transfers between devices with their start and end apart: 29, of which 8 were waited for; matrix products, arithmetic and copies ran while one was open for 0% of the time, Pallas kernels for 13%

profile of v5, /device:TPU:225, one launch (start us, length us, event | category | flops | bytes accessed | tf_op | source)
XLA Modules:
  0.0 91.5 jit_solution(11932720365991602934)
XLA Ops:
  0.0 2.8 %shard_map.17.own_ref.own = f32[8,2,64,128]{3,2,1,0:T(8,128)S(1)} custom-call(f32[1,8,64,256]{3,2,1,0:T(8,128)} %x_ref.1), custom_call_target="tpu_custom_call" | custom-call | tf_op jit(solution)/shard_map/pallas_call | solution.py:361
  3.5 0.7 collective-permute-start.6
  4.2 1.3 %collective-permute-start = (f32[8,128]{1,0:T(8,128)S(1)}, f32[8,128]{1,0:T(8,128)S(1)}, u32[]{:S(2)}, u32[]{:S(2)}) collective-permute-start(f32[8,128]{1,0:T(8,128)S(1)} %shard_map.18), channel_id=1, source_target_pairs={{0,32},{1,33},{2,34},{3,35},{4,36},{5,37},{6,38},{7,39},{8,40},{9,... | collective-permute-start | bytes 12296 | tf_op jit(solution)/shard_map/ppermute | solution.py:387
  5.5 9.4 %collective-permute-done.refs_0_ = f32[8,128]{1,0:T(8,128)S(1)} collective-permute-done((f32[8,128]{1,0:T(8,128)S(1)}, f32[8,128]{1,0:T(8,128)S(1)}, u32[]{:S(2)}, u32[]{:S(2)}) %collective-permute-start) | collective-permute-done | bytes 4128 | tf_op jit(solution)/shard_map/ppermute | solution.py:387
  14.9 2.8 %collective-permute-start.1 = (f32[8,2,64,128]{3,2,1,0:T(8,128)S(1)}, f32[8,2,64,128]{3,2,1,0:T(8,128)S(1)}, u32[]{:S(2)}, u32[]{:S(2)}) collective-permute-start(f32[8,2,64,128]{3,2,1,0:T(8,128)S(1)} %shard_map.17.own_ref.own), channel_id=1, source_target_pairs={{33,34},{35,36},{37,38},{39,40},{41,42},{43,44},{45,46},{47,48},{4... | collective-permute-start | bytes 1572872 | tf_op jit(solution)/shard_map/ppermute | solution.py:377
  17.7 2.8 %collective-permute-start.2 = (f32[8,2,64,128]{3,2,1,0:T(8,128)S(1)}, f32[8,2,64,128]{3,2,1,0:T(8,128)S(1)}, u32[]{:S(2)}, u32[]{:S(2)}) collective-permute-start(f32[8,2,64,128]{3,2,1,0:T(8,128)S(1)} %shard_map.17.own_ref.own), channel_id=1, source_target_pairs={{32,33},{34,35},{36,37},{38,39},{40,41},{42,43},{44,45},{46,47},{4... | collective-permute-start | bytes 1572872 | tf_op jit(solution)/shard_map/ppermute | solution.py:377
  22.6 6.5 %collective-permute-done.1.one.one1 = f32[8,2,64,128]{3,2,1,0:T(8,128)S(1)} collective-permute-done((f32[8,2,64,128]{3,2,1,0:T(8,128)S(1)}, f32[8,2,64,128]{3,2,1,0:T(8,128)S(1)}, u32[]{:S(2)}, u32[]{:S(2)}) %collective-permute-start.1) | collective-permute-done | bytes 524320 | tf_op jit(solution)/shard_map/ppermute | solution.py:377
  29.1 3.7 %shard_map.19.own = f32[8,2,64,128]{3,2,1,0:T(8,128)S(1)} custom-call(s32[2]{0:T(128)S(1)} %pad_add_fusion.place_ref, f32[8,2,64,128]{3,2,1,0:T(8,128)S(1)} %shard_map.17.own_ref.own, f32[8,2,64,128]{3,2,1,0:T(8,128)S(1)} %collective-permute-done.1.one.one1, f32[8,2,64,128]{3,2,1,0:T(8,128)S(1)} %collective-permute-done.2.two.two1, ...), custom_call_target="tpu_custom_call" | custom-call | tf_op jit(solution)/shard_map/pallas_call | solution.py:361
  32.8 5.3 %collective-permute-start.3 = (f32[8,2,64,128]{3,2,1,0:T(8,128)S(1)}, f32[8,2,64,128]{3,2,1,0:T(8,128)S(1)}, u32[]{:S(2)}, u32[]{:S(2)}) collective-permute-start(f32[8,2,64,128]{3,2,1,0:T(8,128)S(1)} %shard_map.19.own), channel_id=1, source_target_pairs={{33,34},{35,36},{37,38},{39,40},{41,42},{43,44},{45,46},{47,48},{4... | collective-permute-start | bytes 1572872 | tf_op jit(solution)/shard_map/ppermute | solution.py:377
  38.1 1.9 %collective-permute-start.4 = (f32[8,2,64,128]{3,2,1,0:T(8,128)S(1)}, f32[8,2,64,128]{3,2,1,0:T(8,128)S(1)}, u32[]{:S(2)}, u32[]{:S(2)}) collective-permute-start(f32[8,2,64,128]{3,2,1,0:T(8,128)S(1)} %shard_map.19.own), channel_id=1, source_target_pairs={{32,33},{34,35},{36,37},{38,39},{40,41},{42,43},{44,45},{46,47},{4... | collective-permute-start | bytes 1572872 | tf_op jit(solution)/shard_map/ppermute | solution.py:377
  40.0 1.0 %shard_map.20.co_ref.old_ref.oldx_ref = f32[4,32,128]{2,1,0:T(8,128)S(1)} custom-call(s32[2]{0:T(128)S(1)} %pad_add_fusion.place_ref, f32[8,2,64,128]{3,2,1,0:T(8,128)S(1)} %shard_map.17.own_ref.own, f32[8,2,64,128]{3,2,1,0:T(8,128)S(1)} %collective-permute-done.5.one0.one, f32[8,2,64,128]{3,2,1,0:T(8,128)S(1)} %collective-permute-done.6.two0.two, ...), custom_call_target="tpu_custom_call" | custom-call | tf_op jit(solution)/shard_map/pallas_call | solution.py:361
  41.1 0.7 shard_map.22
  41.8 1.3 %collective-permute-start.10 = (f32[4,32,128]{2,1,0:T(8,128)S(1)}, f32[4,32,128]{2,1,0:T(8,128)S(1)}, u32[]{:S(2)}, u32[]{:S(2)}) collective-permute-start(f32[4,32,128]{2,1,0:T(8,128)S(1)} %get-tuple-element.41), channel_id=1, source_target_pairs={{0,33},{1,34},{2,35},{3,36},{4,37},{5,38},{6,39},{7,40},{8,41},{9,... | collective-permute-start | bytes 196616 | tf_op jit(solution)/shard_map/ppermute | solution.py:387
  43.1 1.3 %collective-permute-start.11 = (f32[4,32,128]{2,1,0:T(8,128)S(1)}, f32[4,32,128]{2,1,0:T(8,128)S(1)}, u32[]{:S(2)}, u32[]{:S(2)}) collective-permute-start(f32[4,32,128]{2,1,0:T(8,128)S(1)} %get-tuple-element.41), channel_id=1, source_target_pairs={{1,32},{2,33},{3,34},{4,35},{5,36},{6,37},{7,38},{8,39},{9,40},{10... | collective-permute-start | bytes 196616 | tf_op jit(solution)/shard_map/ppermute | solution.py:387
  44.4 1.3 %collective-permute-start.9 = (f32[4,32,128]{2,1,0:T(8,128)S(1)}, f32[4,32,128]{2,1,0:T(8,128)S(1)}, u32[]{:S(2)}, u32[]{:S(2)}) collective-permute-start(f32[4,32,128]{2,1,0:T(8,128)S(1)} %get-tuple-element.41), channel_id=1, source_target_pairs={{0,32},{1,33},{2,34},{3,35},{4,36},{5,37},{6,38},{7,39},{8,40},{9,... | collective-permute-start | bytes 196616 | tf_op jit(solution)/shard_map/ppermute | solution.py:387
  45.7 1.3 %collective-permute-done.3.one = f32[8,2,64,128]{3,2,1,0:T(8,128)S(1)} collective-permute-done((f32[8,2,64,128]{3,2,1,0:T(8,128)S(1)}, f32[8,2,64,128]{3,2,1,0:T(8,128)S(1)}, u32[]{:S(2)}, u32[]{:S(2)}) %collective-permute-start.3) | collective-permute-done | bytes 524320 | tf_op jit(solution)/shard_map/ppermute | solution.py:377
  47.0 1.1 %collective-permute-done.4.two = f32[8,2,64,128]{3,2,1,0:T(8,128)S(1)} collective-permute-done((f32[8,2,64,128]{3,2,1,0:T(8,128)S(1)}, f32[8,2,64,128]{3,2,1,0:T(8,128)S(1)}, u32[]{:S(2)}, u32[]{:S(2)}) %collective-permute-start.4) | collective-permute-done | bytes 524320 | tf_op jit(solution)/shard_map/ppermute | solution.py:377
  48.6 3.4 %collective-permute-done.10.left = f32[4,32,128]{2,1,0:T(8,128)S(1)} collective-permute-done((f32[4,32,128]{2,1,0:T(8,128)S(1)}, f32[4,32,128]{2,1,0:T(8,128)S(1)}, u32[]{:S(2)}, u32[]{:S(2)}) %collective-permute-start.10) | collective-permute-done | bytes 65568 | tf_op jit(solution)/shard_map/ppermute | solution.py:387
  57.8 0.8 shard_map.27
  62.0 3.8 %shard_map.28 = (f32[8,2,64,128]{3,2,1,0:T(8,128)S(1)}, f32[4,32,128]{2,1,0:T(8,128)S(1)}) custom-call(s32[2]{0:T(128)S(1)} %pad_add_fusion.place_ref, f32[8,2,64,128]{3,2,1,0:T(8,128)S(1)} %shard_map.19.own, f32[8,2,64,128]{3,2,1,0:T(8,128)S(1)} %collective-permute-done.3.one, ...), custom_call_target="tpu_custom_call", output_to_operand_aliasing={{0}: (5, {}), {1}: (6, {})} | custom-call | tf_op jit(solution)/shard_map/pallas_call | solution.py:361
  66.4 1.3 %collective-permute-start.23 = (f32[4,32,128]{2,1,0:T(8,128)S(1)}, f32[4,32,128]{2,1,0:T(8,128)S(1)}, u32[]{:S(2)}, u32[]{:S(2)}) collective-permute-start(f32[4,32,128]{2,1,0:T(8,128)S(1)} %get-tuple-element.60), channel_id=1, source_target_pairs={{160,226},{161,227},{162,228},{163,229},{164,230},{165,231},{166,2... | collective-permute-start | bytes 196616 | tf_op jit(solution)/shard_map/ppermute | solution.py:387
  67.7 1.3 %collective-permute-start.24 = (f32[4,32,128]{2,1,0:T(8,128)S(1)}, f32[4,32,128]{2,1,0:T(8,128)S(1)}, u32[]{:S(2)}, u32[]{:S(2)}) collective-permute-start(f32[4,32,128]{2,1,0:T(8,128)S(1)} %get-tuple-element.60), channel_id=1, source_target_pairs={{162,224},{163,225},{164,226},{165,227},{166,228},{167,229},{168,2... | collective-permute-start | bytes 196616 | tf_op jit(solution)/shard_map/ppermute | solution.py:387
  69.0 1.3 %collective-permute-start.25 = (f32[4,32,128]{2,1,0:T(8,128)S(1)}, f32[4,32,128]{2,1,0:T(8,128)S(1)}, u32[]{:S(2)}, u32[]{:S(2)}) collective-permute-start(f32[4,32,128]{2,1,0:T(8,128)S(1)} %get-tuple-element.60), channel_id=1, source_target_pairs={{160,225},{161,226},{162,227},{163,228},{164,229},{165,230},{166,2... | collective-permute-start | bytes 196616 | tf_op jit(solution)/shard_map/ppermute | solution.py:387
  70.3 1.3 %collective-permute-start.26 = (f32[4,32,128]{2,1,0:T(8,128)S(1)}, f32[4,32,128]{2,1,0:T(8,128)S(1)}, u32[]{:S(2)}, u32[]{:S(2)}) collective-permute-start(f32[4,32,128]{2,1,0:T(8,128)S(1)} %get-tuple-element.60), channel_id=1, source_target_pairs={{161,224},{162,225},{163,226},{164,227},{165,228},{166,229},{167,2... | collective-permute-start | bytes 196616 | tf_op jit(solution)/shard_map/ppermute | solution.py:387
  71.6 1.3 %collective-permute-start.27 = (f32[4,32,128]{2,1,0:T(8,128)S(1)}, f32[4,32,128]{2,1,0:T(8,128)S(1)}, u32[]{:S(2)}, u32[]{:S(2)}) collective-permute-start(f32[4,32,128]{2,1,0:T(8,128)S(1)} %get-tuple-element.60), channel_id=1, source_target_pairs={{160,224},{161,225},{162,226},{163,227},{164,228},{165,229},{166,2... | collective-permute-start | bytes 196616 | tf_op jit(solution)/shard_map/ppermute | solution.py:387
  72.9 0.7 shard_map.29.refs_0_.rest_ref
  73.7 10.3 %collective-permute-done.23.a0 = f32[4,32,128]{2,1,0:T(8,128)S(1)} collective-permute-done((f32[4,32,128]{2,1,0:T(8,128)S(1)}, f32[4,32,128]{2,1,0:T(8,128)S(1)}, u32[]{:S(2)}, u32[]{:S(2)}) %collective-permute-start.23) | collective-permute-done | bytes 65568 | tf_op jit(solution)/shard_map/ppermute | solution.py:387
  84.0 2.0 %collective-permute-done.25.a1 = f32[4,32,128]{2,1,0:T(8,128)S(1)} collective-permute-done((f32[4,32,128]{2,1,0:T(8,128)S(1)}, f32[4,32,128]{2,1,0:T(8,128)S(1)}, u32[]{:S(2)}, u32[]{:S(2)}) %collective-permute-start.25) | collective-permute-done | bytes 65568 | tf_op jit(solution)/shard_map/ppermute | solution.py:387
  86.0 1.5 %shard_map.31 = (f32[4,32,128]{2,1,0:T(8,128)S(1)}, f32[4,32,128]{2,1,0:T(8,128)S(1)}) custom-call(s32[2]{0:T(128)S(1)} %pad_add_fusion.place_ref, f32[4,32,128]{2,1,0:T(8,128)S(1)} %collective-permute-done.23.a0, f32[4,32,128]{2,1,0:T(8,128)S(1)} %collective-permute-done.24.a4, f32[4,32,128]{2,1,0:T(8,128)S(1)} %collective-permute-done.25.a1, ...), custom_call_target="tpu_custom_call" | custom-call | tf_op jit(solution)/shard_map/pallas_call | solution.py:361
  87.5 1.3 %collective-permute-start.28 = (f32[4,32,128]{2,1,0:T(8,128)S(1)}, f32[4,32,128]{2,1,0:T(8,128)S(1)}, u32[]{:S(2)}, u32[]{:S(2)}) collective-permute-start(f32[4,32,128]{2,1,0:T(8,128)S(1)} %get-tuple-element.64), channel_id=1, source_target_pairs={{96,64},{97,65},{98,66},{99,67},{100,68},{101,69},{102,70},{103,71... | collective-permute-start | bytes 196616 | tf_op jit(solution)/shard_map/ppermute | solution.py:387
  88.8 0.9 collective-permute-done.28.even_ref
  89.7 1.7 %shard_map.32 = f32[1,8,64,256]{3,2,1,0:T(8,128)} custom-call(s32[2]{0:T(128)S(1)} %pad_add_fusion.place_ref, f32[2,8,64,128]{3,2,1,0:T(8,128)S(1)} %shard_map.29.refs_0_.rest_ref, f32[4,32,128]{2,1,0:T(8,128)S(1)} %get-tuple-element.63.picked_ref, f32[4,32,128]{2,1,0:T(8,128)S(1)} %collective-permute-done.28.even_ref), custom_call_target="tpu_custom_call" | custom-call | tf_op jit(solution)/shard_map/pallas_call | solution.py:361
  (43 shorter events, 12.9 us)
Async XLA Ops:
  2.8 17.8 %collective-permute-start.5 = (f32[8,2,64,128]{3,2,1,0:T(8,128)S(1)}, f32[8,2,64,128]{3,2,1,0:T(8,128)S(1)}, u32[]{:S(2)}, u32[]{:S(2)}) collective-permute-start(f32[8,2,64,128]{3,2,1,0:T(8,128)S(1)} %shard_map.17.own_ref.own), channel_id=1, source_target_pairs={{1,2},{3,4},{5,6},{7,8},{9,10},{11,12},{13,14},{15,16},{17,18},{19... | collective-permute-start | bytes 1572872 | tf_op jit(solution)/shard_map/ppermute | solution.py:377
  3.5 17.1 %collective-permute-start.6 = (f32[8,2,64,128]{3,2,1,0:T(8,128)S(1)}, f32[8,2,64,128]{3,2,1,0:T(8,128)S(1)}, u32[]{:S(2)}, u32[]{:S(2)}) collective-permute-start(f32[8,2,64,128]{3,2,1,0:T(8,128)S(1)} %shard_map.17.own_ref.own), channel_id=1, source_target_pairs={{0,1},{2,3},{4,5},{6,7},{8,9},{10,11},{12,13},{14,15},{16,17},{18,... | collective-permute-start | bytes 1572872 | tf_op jit(solution)/shard_map/ppermute | solution.py:377
  4.2 10.7 %collective-permute-start = (f32[8,128]{1,0:T(8,128)S(1)}, f32[8,128]{1,0:T(8,128)S(1)}, u32[]{:S(2)}, u32[]{:S(2)}) collective-permute-start(f32[8,128]{1,0:T(8,128)S(1)} %shard_map.18), channel_id=1, source_target_pairs={{0,32},{1,33},{2,34},{3,35},{4,36},{5,37},{6,38},{7,39},{8,40},{9,... | collective-permute-start | bytes 12296 | tf_op jit(solution)/shard_map/ppermute | solution.py:387
  14.9 14.1 %collective-permute-start.1 = (f32[8,2,64,128]{3,2,1,0:T(8,128)S(1)}, f32[8,2,64,128]{3,2,1,0:T(8,128)S(1)}, u32[]{:S(2)}, u32[]{:S(2)}) collective-permute-start(f32[8,2,64,128]{3,2,1,0:T(8,128)S(1)} %shard_map.17.own_ref.own), channel_id=1, source_target_pairs={{33,34},{35,36},{37,38},{39,40},{41,42},{43,44},{45,46},{47,48},{4... | collective-permute-start | bytes 1572872 | tf_op jit(solution)/shard_map/ppermute | solution.py:377
  17.7 11.3 %collective-permute-start.2 = (f32[8,2,64,128]{3,2,1,0:T(8,128)S(1)}, f32[8,2,64,128]{3,2,1,0:T(8,128)S(1)}, u32[]{:S(2)}, u32[]{:S(2)}) collective-permute-start(f32[8,2,64,128]{3,2,1,0:T(8,128)S(1)} %shard_map.17.own_ref.own), channel_id=1, source_target_pairs={{32,33},{34,35},{36,37},{38,39},{40,41},{42,43},{44,45},{46,47},{4... | collective-permute-start | bytes 1572872 | tf_op jit(solution)/shard_map/ppermute | solution.py:377
  21.1 19.9 %collective-permute-start.7 = (f32[8,2,64,128]{3,2,1,0:T(8,128)S(1)}, f32[8,2,64,128]{3,2,1,0:T(8,128)S(1)}, u32[]{:S(2)}, u32[]{:S(2)}) collective-permute-start(f32[8,2,64,128]{3,2,1,0:T(8,128)S(1)} %shard_map.21.own), channel_id=1, source_target_pairs={{1,2},{3,4},{5,6},{7,8},{9,10},{11,12},{13,14},{15,16},{17,18},{19... | collective-permute-start | bytes 1572872 | tf_op jit(solution)/shard_map/ppermute | solution.py:377
  21.8 19.2 %collective-permute-start.8 = (f32[8,2,64,128]{3,2,1,0:T(8,128)S(1)}, f32[8,2,64,128]{3,2,1,0:T(8,128)S(1)}, u32[]{:S(2)}, u32[]{:S(2)}) collective-permute-start(f32[8,2,64,128]{3,2,1,0:T(8,128)S(1)} %shard_map.21.own), channel_id=1, source_target_pairs={{0,1},{2,3},{4,5},{6,7},{8,9},{10,11},{12,13},{14,15},{16,17},{18,... | collective-permute-start | bytes 1572872 | tf_op jit(solution)/shard_map/ppermute | solution.py:377
  32.8 14.1 %collective-permute-start.3 = (f32[8,2,64,128]{3,2,1,0:T(8,128)S(1)}, f32[8,2,64,128]{3,2,1,0:T(8,128)S(1)}, u32[]{:S(2)}, u32[]{:S(2)}) collective-permute-start(f32[8,2,64,128]{3,2,1,0:T(8,128)S(1)} %shard_map.19.own), channel_id=1, source_target_pairs={{33,34},{35,36},{37,38},{39,40},{41,42},{43,44},{45,46},{47,48},{4... | collective-permute-start | bytes 1572872 | tf_op jit(solution)/shard_map/ppermute | solution.py:377
  38.1 9.9 %collective-permute-start.4 = (f32[8,2,64,128]{3,2,1,0:T(8,128)S(1)}, f32[8,2,64,128]{3,2,1,0:T(8,128)S(1)}, u32[]{:S(2)}, u32[]{:S(2)}) collective-permute-start(f32[8,2,64,128]{3,2,1,0:T(8,128)S(1)} %shard_map.19.own), channel_id=1, source_target_pairs={{32,33},{34,35},{36,37},{38,39},{40,41},{42,43},{44,45},{46,47},{4... | collective-permute-start | bytes 1572872 | tf_op jit(solution)/shard_map/ppermute | solution.py:377
  41.8 10.2 %collective-permute-start.10 = (f32[4,32,128]{2,1,0:T(8,128)S(1)}, f32[4,32,128]{2,1,0:T(8,128)S(1)}, u32[]{:S(2)}, u32[]{:S(2)}) collective-permute-start(f32[4,32,128]{2,1,0:T(8,128)S(1)} %get-tuple-element.41), channel_id=1, source_target_pairs={{0,33},{1,34},{2,35},{3,36},{4,37},{5,38},{6,39},{7,40},{8,41},{9,... | collective-permute-start | bytes 196616 | tf_op jit(solution)/shard_map/ppermute | solution.py:387
  43.1 8.9 %collective-permute-start.11 = (f32[4,32,128]{2,1,0:T(8,128)S(1)}, f32[4,32,128]{2,1,0:T(8,128)S(1)}, u32[]{:S(2)}, u32[]{:S(2)}) collective-permute-start(f32[4,32,128]{2,1,0:T(8,128)S(1)} %get-tuple-element.41), channel_id=1, source_target_pairs={{1,32},{2,33},{3,34},{4,35},{5,36},{6,37},{7,38},{8,39},{9,40},{10... | collective-permute-start | bytes 196616 | tf_op jit(solution)/shard_map/ppermute | solution.py:387
  44.4 7.6 %collective-permute-start.9 = (f32[4,32,128]{2,1,0:T(8,128)S(1)}, f32[4,32,128]{2,1,0:T(8,128)S(1)}, u32[]{:S(2)}, u32[]{:S(2)}) collective-permute-start(f32[4,32,128]{2,1,0:T(8,128)S(1)} %get-tuple-element.41), channel_id=1, source_target_pairs={{0,32},{1,33},{2,34},{3,35},{4,36},{5,37},{6,38},{7,39},{8,40},{9,... | collective-permute-start | bytes 196616 | tf_op jit(solution)/shard_map/ppermute | solution.py:387
  52.6 3.9 %collective-permute-start.12 = (f32[4,32,128]{2,1,0:T(8,128)S(1)}, f32[4,32,128]{2,1,0:T(8,128)S(1)}, u32[]{:S(2)}, u32[]{:S(2)}) collective-permute-start(f32[4,32,128]{2,1,0:T(8,128)S(1)} %get-tuple-element.42.refs_2_), channel_id=1, source_target_pairs={{32,98},{33,99},{34,100},{35,101},{36,102},{37,103},{38,104},{39,1... | collective-permute-start | bytes 196616 | tf_op jit(solution)/shard_map/ppermute | solution.py:387
  53.2 3.3 %collective-permute-start.13 = (f32[4,32,128]{2,1,0:T(8,128)S(1)}, f32[4,32,128]{2,1,0:T(8,128)S(1)}, u32[]{:S(2)}, u32[]{:S(2)}) collective-permute-start(f32[4,32,128]{2,1,0:T(8,128)S(1)} %get-tuple-element.42.refs_2_), channel_id=1, source_target_pairs={{34,96},{35,97},{36,98},{37,99},{38,100},{39,101},{40,102},{41,103... | collective-permute-start | bytes 196616 | tf_op jit(solution)/shard_map/ppermute | solution.py:387
  53.9 2.6 %collective-permute-start.14 = (f32[4,32,128]{2,1,0:T(8,128)S(1)}, f32[4,32,128]{2,1,0:T(8,128)S(1)}, u32[]{:S(2)}, u32[]{:S(2)}) collective-permute-start(f32[4,32,128]{2,1,0:T(8,128)S(1)} %get-tuple-element.42.refs_2_), channel_id=1, source_target_pairs={{32,97},{33,98},{34,99},{35,100},{36,101},{37,102},{38,103},{39,10... | collective-permute-start | bytes 196616 | tf_op jit(solution)/shard_map/ppermute | solution.py:387
  54.6 1.9 %collective-permute-start.15 = (f32[4,32,128]{2,1,0:T(8,128)S(1)}, f32[4,32,128]{2,1,0:T(8,128)S(1)}, u32[]{:S(2)}, u32[]{:S(2)}) collective-permute-start(f32[4,32,128]{2,1,0:T(8,128)S(1)} %get-tuple-element.42.refs_2_), channel_id=1, source_target_pairs={{33,96},{34,97},{35,98},{36,99},{37,100},{38,101},{39,102},{40,103... | collective-permute-start | bytes 196616 | tf_op jit(solution)/shard_map/ppermute | solution.py:387
  55.3 1.3 %collective-permute-start.16 = (f32[4,32,128]{2,1,0:T(8,128)S(1)}, f32[4,32,128]{2,1,0:T(8,128)S(1)}, u32[]{:S(2)}, u32[]{:S(2)}) collective-permute-start(f32[4,32,128]{2,1,0:T(8,128)S(1)} %get-tuple-element.42.refs_2_), channel_id=1, source_target_pairs={{32,96},{33,97},{34,98},{35,99},{36,100},{37,101},{38,102},{39,103... | collective-permute-start | bytes 196616 | tf_op jit(solution)/shard_map/ppermute | solution.py:387
  56.5 1.3 %collective-permute-start.17 = (f32[12,32,128]{2,1,0:T(8,128)S(1)}, f32[12,32,128]{2,1,0:T(8,128)S(1)}, u32[]{:S(2)}, u32[]{:S(2)}) collective-permute-start(f32[12,32,128]{2,1,0:T(8,128)S(1)} %get-tuple-element.53.wide_ref), channel_id=1, source_target_pairs={{64,96},{65,97},{66,98},{67,99},{68,100},{69,101},{70,102},{71,103... | collective-permute-start | bytes 589832 | tf_op jit(solution)/shard_map/ppermute | solution.py:387
  58.6 7.2 %collective-permute-start.18 = (f32[4,32,128]{2,1,0:T(8,128)S(1)}, f32[4,32,128]{2,1,0:T(8,128)S(1)}, u32[]{:S(2)}, u32[]{:S(2)}) collective-permute-start(f32[4,32,128]{2,1,0:T(8,128)S(1)} %get-tuple-element.55.refs_2_), channel_id=1, source_target_pairs={{96,162},{97,163},{98,164},{99,165},{100,166},{101,167},{102,168},... | collective-permute-start | bytes 196616 | tf_op jit(solution)/shard_map/ppermute | solution.py:387
  59.3 6.6 %collective-permute-start.19 = (f32[4,32,128]{2,1,0:T(8,128)S(1)}, f32[4,32,128]{2,1,0:T(8,128)S(1)}, u32[]{:S(2)}, u32[]{:S(2)}) collective-permute-start(f32[4,32,128]{2,1,0:T(8,128)S(1)} %get-tuple-element.55.refs_2_), channel_id=1, source_target_pairs={{98,160},{99,161},{100,162},{101,163},{102,164},{103,165},{104,166... | collective-permute-start | bytes 196616 | tf_op jit(solution)/shard_map/ppermute | solution.py:387
  59.9 5.9 %collective-permute-start.20 = (f32[4,32,128]{2,1,0:T(8,128)S(1)}, f32[4,32,128]{2,1,0:T(8,128)S(1)}, u32[]{:S(2)}, u32[]{:S(2)}) collective-permute-start(f32[4,32,128]{2,1,0:T(8,128)S(1)} %get-tuple-element.55.refs_2_), channel_id=1, source_target_pairs={{96,161},{97,162},{98,163},{99,164},{100,165},{101,166},{102,167},... | collective-permute-start | bytes 196616 | tf_op jit(solution)/shard_map/ppermute | solution.py:387
  60.6 5.2 %collective-permute-start.21 = (f32[4,32,128]{2,1,0:T(8,128)S(1)}, f32[4,32,128]{2,1,0:T(8,128)S(1)}, u32[]{:S(2)}, u32[]{:S(2)}) collective-permute-start(f32[4,32,128]{2,1,0:T(8,128)S(1)} %get-tuple-element.55.refs_2_), channel_id=1, source_target_pairs={{97,160},{98,161},{99,162},{100,163},{101,164},{102,165},{103,166}... | collective-permute-start | bytes 196616 | tf_op jit(solution)/shard_map/ppermute | solution.py:387
  61.3 4.6 %collective-permute-start.22 = (f32[4,32,128]{2,1,0:T(8,128)S(1)}, f32[4,32,128]{2,1,0:T(8,128)S(1)}, u32[]{:S(2)}, u32[]{:S(2)}) collective-permute-start(f32[4,32,128]{2,1,0:T(8,128)S(1)} %get-tuple-element.55.refs_2_), channel_id=1, source_target_pairs={{96,160},{97,161},{98,162},{99,163},{100,164},{101,165},{102,166},... | collective-permute-start | bytes 196616 | tf_op jit(solution)/shard_map/ppermute | solution.py:387
  66.4 17.6 %collective-permute-start.23 = (f32[4,32,128]{2,1,0:T(8,128)S(1)}, f32[4,32,128]{2,1,0:T(8,128)S(1)}, u32[]{:S(2)}, u32[]{:S(2)}) collective-permute-start(f32[4,32,128]{2,1,0:T(8,128)S(1)} %get-tuple-element.60), channel_id=1, source_target_pairs={{160,226},{161,227},{162,228},{163,229},{164,230},{165,231},{166,2... | collective-permute-start | bytes 196616 | tf_op jit(solution)/shard_map/ppermute | solution.py:387
  67.7 16.3 %collective-permute-start.24 = (f32[4,32,128]{2,1,0:T(8,128)S(1)}, f32[4,32,128]{2,1,0:T(8,128)S(1)}, u32[]{:S(2)}, u32[]{:S(2)}) collective-permute-start(f32[4,32,128]{2,1,0:T(8,128)S(1)} %get-tuple-element.60), channel_id=1, source_target_pairs={{162,224},{163,225},{164,226},{165,227},{166,228},{167,229},{168,2... | collective-permute-start | bytes 196616 | tf_op jit(solution)/shard_map/ppermute | solution.py:387
  69.0 16.9 %collective-permute-start.25 = (f32[4,32,128]{2,1,0:T(8,128)S(1)}, f32[4,32,128]{2,1,0:T(8,128)S(1)}, u32[]{:S(2)}, u32[]{:S(2)}) collective-permute-start(f32[4,32,128]{2,1,0:T(8,128)S(1)} %get-tuple-element.60), channel_id=1, source_target_pairs={{160,225},{161,226},{162,227},{163,228},{164,229},{165,230},{166,2... | collective-permute-start | bytes 196616 | tf_op jit(solution)/shard_map/ppermute | solution.py:387
  70.3 15.6 %collective-permute-start.26 = (f32[4,32,128]{2,1,0:T(8,128)S(1)}, f32[4,32,128]{2,1,0:T(8,128)S(1)}, u32[]{:S(2)}, u32[]{:S(2)}) collective-permute-start(f32[4,32,128]{2,1,0:T(8,128)S(1)} %get-tuple-element.60), channel_id=1, source_target_pairs={{161,224},{162,225},{163,226},{164,227},{165,228},{166,229},{167,2... | collective-permute-start | bytes 196616 | tf_op jit(solution)/shard_map/ppermute | solution.py:387
  71.6 14.3 %collective-permute-start.27 = (f32[4,32,128]{2,1,0:T(8,128)S(1)}, f32[4,32,128]{2,1,0:T(8,128)S(1)}, u32[]{:S(2)}, u32[]{:S(2)}) collective-permute-start(f32[4,32,128]{2,1,0:T(8,128)S(1)} %get-tuple-element.60), channel_id=1, source_target_pairs={{160,224},{161,225},{162,226},{163,227},{164,228},{165,229},{166,2... | collective-permute-start | bytes 196616 | tf_op jit(solution)/shard_map/ppermute | solution.py:387
  87.5 2.2 %collective-permute-start.28 = (f32[4,32,128]{2,1,0:T(8,128)S(1)}, f32[4,32,128]{2,1,0:T(8,128)S(1)}, u32[]{:S(2)}, u32[]{:S(2)}) collective-permute-start(f32[4,32,128]{2,1,0:T(8,128)S(1)} %get-tuple-element.64), channel_id=1, source_target_pairs={{96,64},{97,65},{98,66},{99,67},{100,68},{101,69},{102,70},{103,71... | collective-permute-start | bytes 196616 | tf_op jit(solution)/shard_map/ppermute | solution.py:387
